TPU v7x, 32 devices: a whole 2x2x4 slice. The times are simulated.
32 devices in a mesh: client: 16 (over z, y, x), chan: 2 (over core).
Axes of the slice: x: 2, y: 2, z: 4, core: 2. Of those that a mesh axis runs over, the one named last changes fastest.
Arguments:
- features: bfloat16 [16, 3136, 2048], P('client', None, 'chan'), may hold values from -6 to 6
- labels: int32 [16, 64], P('client'), may hold values from 0 to 99
- mask: int32 [16], P('client'), may hold values 0 or 1
- base_master: float32 [32, 272, 512], P(('client', 'chan')), may hold values from -0.176776695 to 0.176776695, as said below
- base_momentum: float32 [32, 272, 512], P(('client', 'chan')), may hold values from -0.0234375 to 0.0234375
- global_base: float32 [32, 272, 512], P(('client', 'chan')), may hold values from -0.176776695 to 0.176776695, as said below
- norm_params: float32 [16, 2, 2, 1536], P('client', None, 'chan'), may hold values from -0.9 to 1.3, as said below
- norm_first: float32 [16, 2, 2, 1536], P('client', None, 'chan'), may hold values from -0.00061035156 to 0.00061035156
- norm_second: float32 [16, 2, 2, 1536], P('client', None, 'chan'), may hold values from 5.340576e-09 to 3.2043456e-08
- head: float32 [16, 2048, 100], P('client', 'chan'), may hold values from -0.25 to 0.25
- head_first: float32 [16, 2048, 100], P('client', 'chan'), may hold values from -0.015625 to 0.015625
- head_second: float32 [16, 2048, 100], P('client', 'chan'), may hold values from 4.6875e-06 to 1.5625e-05
Outputs:
- loss: float32 [2], replicated
- base_new: float32 [32, 272, 512], P(('client', 'chan'))
- base_momentum_new: float32 [32, 272, 512], P(('client', 'chan'))
- base_low: bfloat16 [32, 272, 512], P(('client', 'chan'))
- norm_new: float32 [16, 2, 2, 1536], P('client', None, 'chan')
- norm_first_new: float32 [16, 2, 2, 1536], P('client', None, 'chan')
- norm_second_new: float32 [16, 2, 2, 1536], P('client', None, 'chan')
- head_new: float32 [16, 2048, 100], P('client', 'chan')
- head_first_new: float32 [16, 2048, 100], P('client', 'chan')
- head_second_new: float32 [16, 2048, 100], P('client', 'chan')
Inputs may be any that keep to these rules, and one draw needn't show every extreme that they name: `base_master`: base weights with entries of about one over the root of each matrix's fan-in. `global_base`: drawn like base_master, independently. `norm_params`: gains near one, biases of both signs.
All inputs are finite; a program needn't handle non-finite values. No bound on the sum of `mask` on one device may be relied on, other than what follows from the above.
Results may differ from a plain program's by a relative error of at most 0.012.
Values may be sent and summed in bfloat16 or wider, within the bound.
A program may use at most 512 MiB of HBM per device.

v0:
```python
import functools

import jax
import jax.numpy as jnp
from jax import lax
from jax.experimental import pallas as pl
from jax.experimental.layout import Layout, with_layout_constraint
from jax.experimental.pallas import tpu as pltpu
from jax.sharding import PartitionSpec as P

NS_STEPS = 5
STEP = 10

low_type = jnp.bfloat16
wide = jnp.float32
MESH = pl.DeviceIdType.MESH
precise = lax.Precision.HIGHEST
norm_epsilon = 1e-05
prox_weight = 0.05
momentum_decay = 0.95
muon_rate = 0.3
muon_decay = 0.1
schulz_first = 3.4445
schulz_second = -4.775
schulz_third = 2.0315
adam_first = 0.9
adam_second = 0.95
adam_epsilon = 1e-08
head_rate = 0.01
head_decay = 0.05
norm_rate = 0.5

SIDE = 7
PIXELS = SIDE * SIDE
LANES = 128
SPOTS = (4, 2, 2)
VMEM_BYTES = 62 * 2**20


def when(condition, call):
    if isinstance(condition, bool):
        if condition:
            call()
    else:
        pl.when(condition)(call)


def dot_nn(left, right):
    return jnp.dot(left, right, preferred_element_type=wide)


def dot_nt(left, right):
    return lax.dot_general(left, right, (((1,), (1,)), ((), ())), preferred_element_type=wide)


def dot_tn(left, right):
    return lax.dot_general(left, right, (((0,), (0,)), ((), ())), preferred_element_type=wide)


def flat_rows(block):
    return block.reshape(-1, block.shape[-1])


def sigmoid(value):
    return 0.5 * jnp.tanh(0.5 * value) + 0.5


def fold_rows(value):
    return jnp.sum(value.reshape(value.shape[0] // 8, 8, value.shape[1]), axis=0)


def column_sum(value):
    return jnp.sum(value, axis=0, keepdims=True)


def remote(src, dst, send_sem, recv_sem, client, core):
    return pltpu.make_async_remote_copy(
        src_ref=src,
        dst_ref=dst,
        send_sem=send_sem,
        recv_sem=recv_sem,
        device_id=(client, core),
        device_id_type=MESH,
    )


class Place:
    def __init__(self):
        self.client = lax.axis_index("client")
        self.core = lax.axis_index("chan")
        self.z = self.client // 4
        self.y = (self.client // 2) % 2
        self.x = self.client % 2
        self.others = [
            self.z + 1 - 2 * (self.z % 2),
            (self.z + 2) % 4,
            3 - self.z,
        ]

    def at(self, z, y, x):
        return z * 4 + y * 2 + x

    def along_x(self):
        return self.at(self.z, self.y, 1 - self.x)

    def along_y(self):
        return self.at(self.z, 1 - self.y, self.x)

    def along_z(self, step):
        return self.at(self.others[step], self.y, self.x)

    def greet(self, whole):
        barrier = pltpu.get_barrier_semaphore()
        pairs = [(self.client, 1 - self.core)]
        if whole:
            pairs += [(self.along_x(), self.core), (self.along_y(), self.core)]
            pairs += [(self.along_z(step), self.core) for step in range(3)]
        for pair in pairs:
            pl.semaphore_signal(barrier, inc=1, device_id=pair, device_id_type=MESH)
        pl.semaphore_wait(barrier, len(pairs))


def cut_rows(counts):
    pieces = []
    for slot, rows in enumerate(counts):
        middle = (rows // 16 + 1) // 2 * 16
        pieces.append((slot, 0, middle, 0))
        pieces.append((slot, middle, rows - middle, 1))
    return pieces


class Spread:
    def __init__(self, place, weights, sems):
        self.place = place
        self.weights = weights
        self.pieces = cut_rows([weight.shape[-2] for weight in weights])
        self.z_sems, self.near_sems, self.far_sems, self.core_sems = sems
        self.order = [place.z] + place.others

    def z_copy(self, step, slot):
        p = self.place
        ref = self.weights[slot].at[p.z, p.y, p.x, p.core]
        sems = self.z_sems
        return remote(ref, ref, sems.at[0, step, slot], sems.at[1, step, slot], p.along_z(step), p.core)

    def near_copy(self, turn, number):
        p = self.place
        slot, start, count, way = self.pieces[number]
        ref = self.weights[slot].at[self.order[turn], p.y, p.x, p.core, pl.ds(start, count), :]
        sems = self.near_sems
        return remote(
            ref, ref, sems.at[0, turn, number], sems.at[1, turn, number], (p.along_x, p.along_y)[way](), p.core
        )

    def far_copy(self, turn, number):
        p = self.place
        slot, start, count, way = self.pieces[number]
        rows = pl.ds(start, count)
        spot = self.order[turn]
        if way == 0:
            ref = self.weights[slot].at[spot, p.y, :, p.core, rows, :]
        else:
            ref = self.weights[slot].at[spot, :, p.x, p.core, rows, :]
        sems = self.far_sems
        return remote(
            ref, ref, sems.at[0, turn, number], sems.at[1, turn, number], (p.along_y, p.along_x)[way](), p.core
        )

    def core_copy(self, turn, slot):
        p = self.place
        ref = self.weights[slot].at[self.order[turn], :, :, p.core]
        sems = self.core_sems
        return remote(ref, ref, sems.at[0, turn, slot], sems.at[1, turn, slot], p.client, 1 - p.core)

    def begin(self, master):
        p = self.place
        start = 0
        for slot in range(3):
            rows = self.weights[slot].shape[-2]
            self.weights[slot][p.z, p.y, p.x, p.core] = master[start : start + rows, :].astype(low_type)
            start += rows
        for step in range(3):
            self.z_copy(step, 0).start()
        self.near_start(0)

    def near_start(self, slot):
        for number in (2 * slot, 2 * slot + 1):
            self.near_copy(0, number).start()

    def steps(self):
        near, far, core, start = self.near_step, self.far_step, self.core_step, self.near_start
        groups = [
            [(far, 0, 0), (start, 1)],
            [(near, 1, 0)],
            [(near, 2, 0), (near, 3, 0)],
            [(far, 1, 0), (core, 0, 0), (far, 0, 1)],
            [(far, 2, 0), (far, 3, 0), (core, 1, 0)],
            [(core, 2, 0), (core, 3, 0), (near, 1, 1), (start, 2)],
            [(core, 0, 1), (near, 2, 1)],
            [(far, 1, 1), (near, 3, 1)],
            [(core, 1, 1), (far, 2, 1), (far, 0, 2)],
            [(far, 3, 1), (core, 2, 1), (near, 1, 2)],
            [(core, 3, 1), (core, 0, 2), (near, 2, 2)],
            [(far, 1, 2), (near, 3, 2)],
            [(core, 1, 2), (far, 2, 2)],
            [(far, 3, 2), (core, 2, 2)],
            [(core, 3, 2)],
        ]
        return [[functools.partial(*step) for step in group] for group in groups]

    def near_step(self, turn, slot):
        self.z_copy(turn - 1, slot).wait_recv()
        for number in (2 * slot, 2 * slot + 1):
            self.near_copy(turn, number).start()
        if slot < 2:
            self.z_copy(turn - 1, slot + 1).start()

    def far_step(self, turn, slot):
        for number in (2 * slot, 2 * slot + 1):
            self.near_copy(turn, number).wait_recv()
            self.far_copy(turn, number).start()

    def core_step(self, turn, slot):
        for number in (2 * slot, 2 * slot + 1):
            self.far_copy(turn, number).wait_recv()
        self.core_copy(turn, slot).start()

    def arrive(self, slot):
        for turn in range(4):
            self.core_copy(turn, slot).wait_recv()

    def drain(self):
        for slot in range(3):
            for step in range(3):
                self.z_copy(step, slot).wait_send()
            for turn in range(4):
                self.core_copy(turn, slot).wait_send()
        for number in range(6):
            for turn in range(4):
                self.near_copy(turn, number).wait_send()
                self.far_copy(turn, number).wait_send()


class Fold:
    def __init__(self, place, grads, counts, parts):
        self.place = place
        self.grads = grads
        self.counts = counts
        self.pieces = cut_rows(counts)
        self.core_boxes = [parts[1], parts[0], parts[1]]
        self.near_boxes, self.far_boxes, self.z_boxes = [parts[3 * k + 2 : 3 * k + 5] for k in range(3)]
        self.core_sems, self.near_sems, self.far_sems, self.z_sems = parts[11:]

    def core_copy(self, which, slot):
        p = self.place
        sems = self.core_sems
        return remote(
            self.grads[slot].at[which, :, :, 1 - p.core, pl.ds(0, self.counts[slot]), :],
            self.core_boxes[slot].at[which],
            sems.at[0, which, slot],
            sems.at[1, which, slot],
            p.client,
            1 - p.core,
        )

    def near_copy(self, which, number):
        p = self.place
        slot, start, count, way = self.pieces[number]
        rows = pl.ds(start, count)
        if way == 0:
            ref = self.grads[slot].at[which, :, 1 - p.x, p.core, rows, :]
        else:
            ref = self.grads[slot].at[which, 1 - p.y, :, p.core, rows, :]
        box = self.near_boxes[slot].at[which, :, rows, :]
        sems = self.near_sems
        return remote(
            ref, box, sems.at[0, which, number], sems.at[1, which, number], (p.along_x, p.along_y)[way](), p.core
        )

    def far_copy(self, which, number):
        p = self.place
        slot, start, count, way = self.pieces[number]
        rows = pl.ds(start, count)
        if way == 0:
            ref = self.grads[slot].at[which, 1 - p.y, p.x, p.core, rows, :]
        else:
            ref = self.grads[slot].at[which, p.y, 1 - p.x, p.core, rows, :]
        box = self.far_boxes[slot].at[which, rows, :]
        sems = self.far_sems
        return remote(
            ref, box, sems.at[0, which, number], sems.at[1, which, number], (p.along_y, p.along_x)[way](), p.core
        )

    def z_copy(self, which, sender, number):
        p = self.place
        slot, start, count, _ = self.pieces[number]
        rows = pl.ds(start, count)
        sems = self.z_sems
        return remote(
            self.grads[slot].at[which, p.y, p.x, p.core, rows, :],
            self.z_boxes[slot].at[sender, rows, :],
            sems.at[0, which, number],
            sems.at[1, sender, number],
            p.at(which, p.y, p.x),
            p.core,
        )

    def begin(self, which, slot):
        self.core_copy(which, slot).start()

    def turn(self, slot, turn):
        for lag, step in ((2, self.far_step), (1, self.near_step), (0, self.core_step)):
            when((turn >= lag) & (turn < lag + 4), functools.partial(step, turn - lag, slot))

    def core_step(self, which, slot):
        p = self.place
        rows = pl.ds(0, self.counts[slot])
        self.core_copy(which, slot).wait_recv()
        where = (which, slice(None), slice(None), p.core, rows, slice(None))
        both = self.grads[slot][where].astype(wide) + self.core_boxes[slot][which].astype(wide)
        self.grads[slot][where] = both.astype(low_type)
        for number in (2 * slot, 2 * slot + 1):
            self.near_copy(which, number).start()

    def near_step(self, which, slot):
        p = self.place
        for number in (2 * slot, 2 * slot + 1):
            _, start, count, way = self.pieces[number]
            rows = pl.ds(start, count)
            self.near_copy(which, number).wait_recv()
            if way == 0:
                where = (which, slice(None), p.x, p.core, rows, slice(None))
            else:
                where = (which, p.y, slice(None), p.core, rows, slice(None))
            both = self.grads[slot][where].astype(wide) + self.near_boxes[slot][which, :, rows, :].astype(wide)
            self.grads[slot][where] = both.astype(low_type)
            self.far_copy(which, number).start()

    def far_step(self, which, slot):
        p = self.place
        for number in (2 * slot, 2 * slot + 1):
            _, start, count, way = self.pieces[number]
            rows = pl.ds(start, count)
            self.far_copy(which, number).wait_recv()
            where = (which, p.y, p.x, p.core, rows, slice(None))
            both = self.grads[slot][where].astype(wide) + self.far_boxes[slot][which, rows, :].astype(wide)
            self.grads[slot][where] = both.astype(low_type)

            @pl.when(p.z != which)
            def _():
                self.z_copy(which, p.z, number).start()

    def result(self, slot):
        p = self.place
        rows = pl.ds(0, self.counts[slot])
        self.z_boxes[slot][p.z] = self.grads[slot][p.z, p.y, p.x, p.core, rows, :]
        for sender in range(4):

            @pl.when(p.z != sender)
            def _():
                for number in (2 * slot, 2 * slot + 1):
                    self.z_copy(sender, sender, number).wait_recv()

        total = self.z_boxes[slot][0].astype(wide)
        for sender in range(1, 4):
            total += self.z_boxes[slot][sender].astype(wide)
        return total

    def drain(self):
        for which in range(4):
            for slot in range(3):
                self.core_copy(which, slot).wait_send()
            for number in range(6):
                self.near_copy(which, number).wait_send()
                self.far_copy(which, number).wait_send()

            @pl.when(self.place.z != which)
            def _():
                for number in range(6):
                    self.z_copy(which, self.place.z, number).wait_send()


def norm_stats(mine, theirs, count):
    gap = mine[0:1] - theirs[0:1]
    mean = 0.5 * (mine[0:1] + theirs[0:1])
    spread = mine[1:2] + theirs[1:2] + gap * gap * (0.5 * count)
    return mean, lax.rsqrt(spread / (2.0 * count) + norm_epsilon)


def client_kernel(
    gather,
    images,
    classes,
    features,
    labels,
    flag,
    params,
    head,
    *rest,
):
    if gather:
        master, *rest = rest
    else:
        first_in, middle_in, last_in, *rest = rest
    if gather:
        grads_out, *rest = rest
    else:
        grads_out, rest = rest[:3], rest[3:]
    (
        grad_norm_out,
        grad_head_out,
        loss_out,
        x_all,
        mid_wide,
        w_first,
        w_middle,
        w_last,
        act_one,
        act_two,
        act_three,
        taps_one,
        taps_two,
        hidden_two,
        stage,
        params_all,
        head_all,
        grad_pool,
        pool_send,
        pool_all,
        logit_grads,
        sums_mine,
        sums_theirs,
        shift,
        fwd_stats,
        sem_local,
        sem_swap,
        sem_misc,
        *near_parts,
    ) = rest
    place = Place()
    core = place.core
    mate = (place.client, 1 - core)
    count_rows, channels = x_all.shape
    half = channels // 2
    width = act_one.shape[1]
    part = width // 2
    mine_images = images // 2
    line = SIDE * mine_images
    total_rows = 2.0 * count_rows

    def tile(index):
        return pl.ds(pl.multiple_of(index * line, line), line)

    def lanes(index, size):
        return pl.ds(pl.multiple_of(index * size, size), size)

    place.greet(gather)

    quarter = half // 2
    own_rows = pl.ds(pl.multiple_of(core * count_rows, count_rows), count_rows)
    mate_rows = pl.ds(pl.multiple_of((1 - core) * count_rows, count_rows), count_rows)
    top_rows = pl.ds(0, count_rows)
    own_copies = [
        pltpu.make_async_copy(
            features.at[own_rows, pl.ds(0, quarter)], hidden_two, sem_local.at[0]
        )
    ]
    for index in range(SIDE):
        rows = pl.ds(pl.multiple_of(core * count_rows + index * line, line), line)
        own_copies.append(
            pltpu.make_async_copy(
                features.at[rows, pl.ds(quarter, quarter)],
                mid_wide.at[0, index // 4, (index // 2) % 2, index % 2],
                sem_local.at[1 + index],
            )
        )
    per_kind = params.shape[0] // 2
    for kind in range(2):
        rows = [params[kind * per_kind + spot : kind * per_kind + spot + 1, :] for spot in range(per_kind)]
        params_all[core, kind : kind + 1, :] = jnp.concatenate(rows, axis=1)
    head_all[core] = jnp.zeros(head_all.shape[1:], low_type)
    for spot in range(half // LANES):
        head_all[core, 0:classes, spot * LANES : (spot + 1) * LANES] = head[
            pl.ds(spot, classes, stride=half // LANES), :
        ].astype(low_type)
    to_mate = [
        remote(params_all.at[core], params_all.at[core], sem_misc.at[0, 0], sem_misc.at[1, 0], *mate),
        remote(head_all.at[core], head_all.at[core], sem_misc.at[0, 1], sem_misc.at[1, 1], *mate),
    ]
    for side, buffer in enumerate((taps_one, taps_two)):
        to_mate.append(
            remote(
                features.at[mate_rows, pl.ds(side * quarter, quarter)],
                buffer.at[top_rows, :],
                sem_misc.at[0, 5 + side],
                sem_misc.at[1, 5 + side],
                *mate,
            )
        )
    for copy in to_mate + own_copies:
        copy.start()

    weights = (w_first, w_middle, w_last)
    if gather:
        spread = Spread(place, weights, near_parts[:4])
        held = act_three.at[pl.ds(0, master.shape[0]), pl.ds(0, width)]
        load = pltpu.make_async_copy(master, held, sem_local.at[8])
        load.start()
        load.wait()
        spread.begin(held)
        counts = [weight.shape[-2] for weight in weights]
        fold = Fold(place, (w_first, mid_wide, w_last), counts, near_parts[4:])
        due = spread.steps()
    else:
        loads = [
            pltpu.make_async_copy(src, dst, sem_local.at[8 + slot])
            for slot, (src, dst) in enumerate(zip((first_in, middle_in, last_in), weights))
        ]
        for load in loads:
            load.start()
        due = []

    def advance(count):
        for group in due[:count]:
            for step in group:
                step()
        del due[:count]

    def advance_at(index, spots):
        for spot, group in zip(spots, due):

            @pl.when(index == spot)
            def _():
                for step in group:
                    step()

    def arrive(slot, left):
        if gather:
            advance(len(due) - left)
            spread.arrive(slot)
        else:
            loads[slot].wait()

    def fold_turn(slot, turn):
        if gather:
            fold.turn(slot, turn)

    def fold_begin(which, slot):
        if gather:
            fold.begin(which, slot)

    def zero_edges(buffer):
        edge = jnp.zeros((line,) + buffer.shape[1:], low_type)
        buffer[0:line, :] = edge
        buffer[line + count_rows : 2 * line + count_rows, :] = edge

    advance(3)
    for copy in own_copies:
        copy.wait()

    def turn_from(source, base):
        def turn(index, carry):
            stage[...] = source(lanes(index, LANES)).astype(wide)

            def pixel(spot, inner):
                x_all[
                    pl.ds(pl.multiple_of(spot * mine_images, mine_images), mine_images),
                    pl.ds(pl.multiple_of(base + index * LANES, LANES), LANES),
                ] = stage[pl.ds(spot, mine_images, stride=PIXELS), :].astype(low_type)
                return inner

            return lax.fori_loop(0, PIXELS, pixel, carry, unroll=7)

        return turn

    quarters = quarter // LANES
    own_base, mate_base = core * half, (1 - core) * half
    lax.fori_loop(0, quarters, turn_from(lambda columns: hidden_two[:, columns], own_base), 0)
    advance(1)
    lax.fori_loop(
        0,
        quarters,
        turn_from(lambda columns: mid_wide[0, :, :, :, :, columns].reshape(8 * line, LANES)[:count_rows], own_base + quarter),
        0,
    )
    advance(1)
    for copy in to_mate:
        copy.wait_recv()
    lax.fori_loop(0, quarters, turn_from(lambda columns: taps_one[0:count_rows, columns], mate_base), 0)
    advance(1)
    lax.fori_loop(0, quarters, turn_from(lambda columns: taps_two[0:count_rows, columns], mate_base + quarter), 0)
    zero_edges(taps_one)
    zero_edges(taps_two)
    arrive(0, 9)

    def swap(slot, size):
        return remote(
            sums_mine.at[slot, :, pl.ds(0, size)],
            sums_theirs.at[slot, :, pl.ds(0, size)],
            sem_swap.at[0, slot],
            sem_swap.at[1, slot],
            *mate,
        )

    def gain_bias(lower, upper):
        rows = []
        for kind in range(2):
            pieces = [params_all[side, kind : kind + 1, lower:upper] for side in range(2)]
            rows.append(jnp.concatenate(pieces, axis=1))
        return rows

    def collect(index, value, columns, size):
        @pl.when(index == 0)
        def _():
            shift[0:1, pl.ds(0, size)] = column_sum(fold_rows(value)) / value.shape[0]
            shift[8:24, pl.ds(0, size)] = jnp.zeros((16, size), wide)

        gap = value - shift[0:1, pl.ds(0, size)]
        shift[8:16, pl.ds(0, size)] += fold_rows(gap)
        shift[16:24, pl.ds(0, size)] += fold_rows(gap * gap)

    def close_stats(slot, columns, size):
        sum_gap = column_sum(shift[8:16, pl.ds(0, size)])
        sum_square = column_sum(shift[16:24, pl.ds(0, size)])
        sums_mine[slot, 0:1, columns] = shift[0:1, pl.ds(0, size)] + sum_gap / count_rows
        sums_mine[slot, 1:2, columns] = sum_square - sum_gap * sum_gap / count_rows

    def settle(slot, size):
        mean, scale = norm_stats(
            sums_mine[slot, 0:2, pl.ds(0, size)], sums_theirs[slot, 0:2, pl.ds(0, size)], float(count_rows)
        )
        fwd_stats[slot, 0:1, pl.ds(0, size)] = mean
        fwd_stats[slot, 1:2, pl.ds(0, size)] = scale

    whole_width = pl.ds(0, width)

    def first_tile(index, carry):
        value = dot_nn(x_all[tile(index), :], flat_rows(w_first[...]))
        act_one[tile(index), :] = value
        collect(index, value, whole_width, width)
        advance_at(index, (1, 3, 5))
        return carry

    lax.fori_loop(0, SIDE, first_tile, 0)
    del due[:3]
    close_stats(0, whole_width, width)
    move = swap(0, width)
    move.start()
    move.wait()
    settle(0, width)

    gain_one, bias_one = gain_bias(0, part)
    gain_two, bias_two = gain_bias(part, width)
    gain_three, bias_three = gain_bias(width, width + half)

    def normal(act, slot, index):
        mean = fwd_stats[slot, 0:1, pl.ds(0, width)]
        return (act[tile(index), :] - mean) * fwd_stats[slot, 1:2, pl.ds(0, width)]

    def hide_one(index, carry):
        value = normal(act_one, 0, index) * gain_one + bias_one
        taps_one[pl.ds(pl.multiple_of((index + 1) * line, line), line), :] = (value * sigmoid(value)).astype(low_type)
        return carry

    lax.fori_loop(0, SIDE, hide_one, 0)
    arrive(1, 4)

    def shifted(buffer, index, down):
        return buffer[pl.ds(pl.multiple_of((index + down) * line, line), line), :]

    step = mine_images
    edge_rows = jnp.zeros((step, width), wide)

    def over_lines(lines, tap_of, multiply, axis):
        left = jnp.concatenate(lines, axis=1)
        value = multiply(left, jnp.concatenate([tap_of(down, 1) for down in range(3)], axis=axis))
        lower = multiply(left[: line - step], jnp.concatenate([tap_of(down, 0) for down in range(3)], axis=axis))
        upper = multiply(left[step:], jnp.concatenate([tap_of(down, 2) for down in range(3)], axis=axis))
        value += jnp.concatenate([edge_rows, lower], axis=0)
        return value + jnp.concatenate([upper, edge_rows], axis=0)

    def second_tile(index, carry):
        kernel = flat_rows(w_middle[...])

        def tap_of(down, over):
            tap = 3 * down + over
            return kernel[tap * width : (tap + 1) * width]

        value = over_lines([shifted(taps_one, index, down) for down in range(3)], tap_of, dot_nn, 0)
        act_two[tile(index), :] = value
        collect(index, value, whole_width, width)
        advance_at(index, (1, 3, 5))
        return carry

    lax.fori_loop(0, SIDE, second_tile, 0)
    del due[:3]
    close_stats(1, whole_width, width)
    move_two = swap(1, width)
    move_two.start()
    move_two.wait()
    settle(1, width)

    def hide_two(index, carry):
        value = normal(act_two, 1, index) * gain_two + bias_two
        hidden_two[tile(index), :] = (value * sigmoid(value)).astype(low_type)
        return carry

    lax.fori_loop(0, SIDE, hide_two, 0)

    arrive(2, 0)
    groups = w_last.shape[0]
    group = channels // groups

    def third_group(which, carry):
        columns = lanes(which, group)

        def third_tile(index, inner):
            value = dot_nt(hidden_two[tile(index), :], flat_rows(w_last[which]))
            act_three[tile(index), columns] = value
            collect(index, value, columns, group)
            return inner

        lax.fori_loop(0, SIDE, third_tile, 0)
        close_stats(2, columns, group)
        return carry

    lax.fori_loop(0, groups, third_group, 0)
    move_three = swap(2, channels)
    move_three.start()
    move_three.wait()
    settle(2, channels)
    fwd_stats[2, 2:3, :] = gain_three
    fwd_stats[2, 3:4, :] = bias_three

    per_group = group // LANES

    def block_of(spot):
        return pl.ds(pl.multiple_of(spot * mine_images, mine_images), mine_images)

    def mid_line(which, index):
        return which, index // 4, (index // 2) % 2, index % 2, pl.ds(0, line)

    kept = channels // LANES * mine_images

    def gathered(kind):
        starts = range(kind * kept, (kind + 1) * kept, mine_images)
        return jnp.concatenate([stage[start : start + mine_images, :] for start in starts], axis=1)

    def emit(index, carry):
        columns = lanes(index, LANES)
        mean, scale = fwd_stats[2, 0:1, columns], fwd_stats[2, 1:2, columns]
        gain, bias = fwd_stats[2, 2:3, columns], fwd_stats[2, 3:4, columns]

        def pixels(row, sums):
            pooled, slopes, slopes_normed = sums
            found = []
            for spot in range(SIDE):
                where = block_of(row * SIDE + spot)
                normed = (act_three[where, columns] - mean) * scale
                total = normed * gain + bias + x_all[where, columns].astype(wide)
                sig = sigmoid(total)
                out = total * sig
                slope = sig + out * (1.0 - sig)
                found.append(slope.astype(low_type))
                pooled, slopes, slopes_normed = pooled + out, slopes + slope, slopes_normed + slope * normed
            mid_wide[mid_line(index // per_group, row) + (lanes(index % per_group, LANES),)] = jnp.concatenate(
                found, axis=0
            )
            return pooled, slopes, slopes_normed

        zero = jnp.zeros((mine_images, LANES), wide)
        pooled, slopes, slopes_normed = lax.fori_loop(0, SIDE, pixels, (zero, zero, zero))
        for kind, value in enumerate((pooled, slopes, slopes_normed)):
            stage[pl.ds(pl.multiple_of(kind * kept + index * mine_images, mine_images), mine_images), :] = value
        return carry

    lax.fori_loop(0, channels // LANES, emit, 0)

    pooled = (gathered(0) / PIXELS).astype(low_type)
    head_full = jnp.concatenate([head_all[0], head_all[1]], axis=1)
    logits = dot_nt(head_full, pooled)
    spots = lax.broadcasted_iota(jnp.int32, logits.shape, 0)
    inside = spots < classes
    first_labels, second_labels = labels[0:1, 0:mine_images], labels[0:1, mine_images:]
    onehot = (spots == jnp.where(core == 0, first_labels, second_labels)).astype(wide)
    top = jnp.max(jnp.where(inside, logits, -jnp.inf), axis=0, keepdims=True)
    powers = jnp.where(inside, jnp.exp(logits - top), 0.0)
    power_sum = jnp.sum(powers, axis=0, keepdims=True)
    picked = jnp.sum(logits * onehot, axis=0, keepdims=True)
    each_loss = top + jnp.log(power_sum) - picked
    taking = flag[0].astype(wide)
    tile_spots = lax.broadcasted_iota(jnp.int32, loss_out.shape, 1)
    loss_out[...] = jnp.where(tile_spots == 0, taking * jnp.sum(each_loss), taking * mine_images)
    grads = (taking / images * (powers / power_sum - onehot)).astype(low_type)
    grad_pool[...] = dot_tn(grads, head_full) / PIXELS
    logit_grads[core] = grads
    pool_all[core] = pooled[:, 0:half]
    pool_send[...] = pooled[:, half:]

    @pl.when(core == 1)
    def _():
        pool_all[core] = pooled[:, half:]
        pool_send[...] = pooled[:, 0:half]

    head_moves = [
        remote(pool_send, pool_all.at[core], sem_misc.at[0, 3], sem_misc.at[1, 3], *mate),
        remote(logit_grads.at[core], logit_grads.at[core], sem_misc.at[0, 4], sem_misc.at[1, 4], *mate),
    ]

    sums_mine[3, 0:1, :] = column_sum(grad_pool[...] * gathered(1))
    sums_mine[3, 1:2, :] = column_sum(grad_pool[...] * gathered(2))
    move_back = swap(3, channels)
    move_back.start()
    for copy in head_moves:
        copy.start()
    move_back.wait()

    def back_terms(slot, layer, size, gain):
        columns = pl.ds(0, size)
        sums = sums_mine[slot, 0:2, columns] + sums_theirs[slot, 0:2, columns]
        sums_mine[slot, 2:4, columns] = sums
        scale = fwd_stats[layer, 1:2, columns]
        return (
            scale * gain,
            scale * gain * sums[0:1] / total_rows,
            scale * scale * gain * sums[1:2] / total_rows,
        )

    first, second, third = back_terms(3, 2, channels, gain_three)
    fwd_stats[2, 4:5, :] = first
    fwd_stats[2, 5:6, :] = second
    fwd_stats[2, 6:7, :] = third

    def pull(index, carry):
        columns = lanes(index, LANES)
        mean = fwd_stats[2, 0:1, columns]
        first, second = fwd_stats[2, 4:5, columns], fwd_stats[2, 5:6, columns]
        third = fwd_stats[2, 6:7, columns]
        reach = grad_pool[:, columns] * first

        def pixels(row, inner):
            where = mid_line(index // per_group, row) + (lanes(index % per_group, LANES),)
            slopes = mid_wide[where].astype(wide)
            found = []
            for spot in range(SIDE):
                slope = slopes[spot * mine_images : (spot + 1) * mine_images]
                gap = act_three[block_of(row * SIDE + spot), columns] - mean
                found.append((reach * slope - second - third * gap).astype(low_type))
            mid_wide[where] = jnp.concatenate(found, axis=0)
            return inner

        return lax.fori_loop(0, SIDE, pixels, carry)

    lax.fori_loop(0, channels // LANES, pull, 0)
    for copy in head_moves:
        copy.wait_recv()
    head_grad = dot_nn(logit_grads[0], pool_all[0]) + dot_nn(logit_grads[1], pool_all[1])
    for spot in range(half // LANES):
        stage[pl.ds(spot, classes, stride=half // LANES), :] = head_grad[
            0:classes, spot * LANES : (spot + 1) * LANES
        ]
    head_space = stage.at[pl.ds(0, grad_head_out.shape[0]), :]
    head_leave = pltpu.make_async_copy(head_space, grad_head_out, sem_local.at[0])
    head_leave.start()

    def drop_into(index, value, act, slot, gain, bias, columns):
        normed = normal(act, slot, index)
        norm = normed * gain + bias
        sig = sigmoid(norm)
        grad = value * (sig + norm * sig * (1.0 - sig))
        act_three[tile(index), columns] = grad
        size = pl.ds(0, width)

        @pl.when(index == 0)
        def _():
            shift[8:24, size] = jnp.zeros((16, width), wide)

        shift[8:16, size] += fold_rows(grad)
        shift[16:24, size] += fold_rows(grad * normed)

    def close_back(slot):
        size = pl.ds(0, width)
        sums_mine[slot, 0:1, size] = column_sum(shift[8:16, size])
        sums_mine[slot, 1:2, size] = column_sum(shift[16:24, size])

    space_two, space_one = pl.ds(0, width), pl.ds(width, width)

    def back_two(index, carry):
        kernel = flat_rows(w_last[...])
        left = jnp.concatenate([mid_wide[mid_line(which, index)] for which in range(groups)], axis=1)
        value = dot_nn(left, kernel)
        drop_into(index, value, act_two, 1, gain_two, bias_two, space_two)
        return carry

    lax.fori_loop(0, SIDE, back_two, 0)
    close_back(4)
    move_back_two = swap(4, width)
    move_back_two.start()

    if gather:
        spread.drain()

    def weight_rows(ref, which, rows):
        return ref.at[which, :, :, :, pl.ds(0, rows), :]

    def put(ref, which, value):
        rows = value.shape[0] // 8
        ref[which, :, :, :, pl.ds(0, rows), :] = value.astype(low_type).reshape(2, 2, 2, rows, width)

    def expand_group(which, carry):
        left = mid_wide[which].reshape(8 * line, group)[:count_rows]
        put(w_last, which, dot_tn(left, hidden_two[...]))
        fold_begin(which, 2)
        fold_turn(2, which - 1)
        return carry

    lax.fori_loop(0, groups, expand_group, 0)
    move_back_two.wait()
    terms_two = back_terms(4, 1, width, gain_two)

    def back_act(terms, act, layer, index, columns):
        first, second, third = terms
        gap = act[tile(index), :] - fwd_stats[layer, 0:1, pl.ds(0, width)]
        return (first * act_three[tile(index), columns] - second - third * gap).astype(low_type)

    def grad_two(index, carry):
        taps_two[pl.ds(pl.multiple_of((index + 1) * line, line), line), :] = back_act(
            terms_two, act_two, 1, index, space_two
        )
        return carry

    lax.fori_loop(0, SIDE, grad_two, 0)
    fold_turn(2, groups - 1)
    piece = width // 2
    middle_rows = 9 * width // groups
    grain = 48

    def middle_row(down, carry):
        def middle_piece(spot, inner):
            for over in range(3):
                left_start, right_start = (0, 0, step)[over], (step, 0, 0)[over]
                reach = line if over == 1 else line - step
                left = [
                    taps_one[
                        pl.ds(pl.multiple_of((down + row) * line + left_start, step), reach), lanes(spot, piece)
                    ]
                    for row in range(SIDE)
                ]
                right = [
                    taps_two[(row + 1) * line + right_start : (row + 1) * line + right_start + reach, :]
                    for row in range(SIDE)
                ]
                value = dot_tn(jnp.concatenate(left, axis=0), jnp.concatenate(right, axis=0))
                start = pl.multiple_of(over * width + spot * piece, piece)
                hidden_two[pl.ds(start, piece), :] = value.astype(low_type)
            return inner

        lax.fori_loop(0, 2, middle_piece, 0)
        grains = 3 * width // grain
        per_block = middle_rows // 8 // grain

        def lay_out(spot, inner):
            place_of = down * grains + spot
            block = place_of // per_block
            rows = pl.ds(pl.multiple_of((place_of % per_block) * grain, 16), grain)
            mid_wide[block // 8, (block // 4) % 2, (block // 2) % 2, block % 2, rows, :] = hidden_two[
                pl.ds(pl.multiple_of(spot * grain, 16), grain), :
            ]
            return inner

        lax.fori_loop(0, grains, lay_out, 0, unroll=4)
        fold_begin(down, 1)

        @pl.when(down == 2)
        def _():
            fold_begin(3, 1)

        fold_turn(2, groups + down)
        fold_turn(1, down - 1)
        return carry

    lax.fori_loop(0, 3, middle_row, 0)

    def back_one(index, carry):
        kernel = flat_rows(w_middle[...])

        def tap_of(down, over):
            tap = 3 * down + 2 - over
            return kernel[tap * width : (tap + 1) * width]

        value = over_lines([shifted(taps_two, index, 2 - down) for down in range(3)], tap_of, dot_nt, 1)
        drop_into(index, value, act_one, 0, gain_one, bias_one, space_one)

        @pl.when(index % 2 == 0)
        def _():
            fold_turn(1, 2 + index // 2)

        return carry

    lax.fori_loop(0, SIDE, back_one, 0)
    close_back(5)
    move_back_one = swap(5, width)
    move_back_one.start()

    move_back_one.wait()
    terms_one = back_terms(5, 0, width, gain_one)

    def grad_one(index, carry):
        hidden_two[tile(index), :] = back_act(terms_one, act_one, 0, index, space_one)
        return carry

    lax.fori_loop(0, SIDE, grad_one, 0)

    def reduce_group(which, carry):
        put(w_first, which, dot_tn(x_all[:, lanes(which, group)], hidden_two[...]))
        fold_begin(which, 0)
        fold_turn(0, which - 1)
        return carry

    lax.fori_loop(0, groups, reduce_group, 0)

    for kind in range(2):
        row = 3 - kind
        pieces = [
            sums_mine[5, row : row + 1, lanes(core, part)],
            sums_mine[4, row : row + 1, lanes(core, part)],
            sums_mine[3, row : row + 1, lanes(core, half)],
        ]
        whole = jnp.concatenate(pieces, axis=1)
        per_kind = whole.shape[1] // LANES
        for spot in range(per_kind):
            grad_norm_out[kind * per_kind + spot : kind * per_kind + spot + 1, :] = whole[
                :, spot * LANES : (spot + 1) * LANES
            ]
    for turn in range(groups - 1, groups + 2):
        fold_turn(0, turn)
    if gather:
        start = 0
        for slot in range(3):
            rows = fold.counts[slot]
            act_three[kept + start : kept + start + rows, half : half + width] = fold.result(slot)
            start += rows
        leave = pltpu.make_async_copy(
            act_three.at[pl.ds(kept, start), pl.ds(half, width)], grads_out, sem_local.at[3]
        )
        leave.start()
        leave.wait()
        fold.drain()
    else:
        outs = [
            pltpu.make_async_copy(weight_rows(ref, slice(None), rows), out, sem_local.at[slot])
            for slot, (ref, rows, out) in enumerate(
                zip((w_first, mid_wide, w_last), [weight.shape[-2] for weight in weights], grads_out)
            )
        ]
        for copy in outs:
            copy.start()
        for copy in outs:
            copy.wait()
    head_leave.wait()
    for copy in to_mate + head_moves:
        copy.wait_send()


def client_pass(gather, classes, features, labels, flag, params, head, weights):
    pixels, half = features.shape
    images = labels.shape[1]
    count_rows, channels = pixels // 2, 2 * half
    width = params.shape[0] // 2 * LANES - half
    head_rows = classes + -classes % 16
    mine_images = images // 2
    line = SIDE * mine_images
    middle = 9 * width
    blocks = 32
    group = channels // SPOTS[0]
    vmem = pl.BlockSpec(memory_space=pltpu.VMEM)
    smem = pl.BlockSpec(memory_space=pltpu.SMEM)
    spots = SPOTS + (2,)
    scratch = [
        pltpu.VMEM((count_rows, channels), low_type),
        pltpu.VMEM(spots + (line, group), low_type),
        pltpu.VMEM(spots + (channels // blocks, width), low_type),
        pltpu.VMEM(spots + (middle // blocks, width), low_type),
        pltpu.VMEM(spots + (channels // blocks, width), low_type),
        pltpu.VMEM((count_rows, width), wide),
        pltpu.VMEM((count_rows, width), wide),
        pltpu.VMEM((count_rows, channels), wide),
        pltpu.VMEM((count_rows + 2 * line, width), low_type),
        pltpu.VMEM((count_rows + 2 * line, width), low_type),
        pltpu.VMEM((count_rows, width), low_type),
        pltpu.VMEM((count_rows, LANES), wide),
        pltpu.VMEM((2, 2, half + width), wide),
        pltpu.VMEM((2, head_rows, half), low_type),
        pltpu.VMEM((mine_images, channels), wide),
        pltpu.VMEM((mine_images, half), low_type),
        pltpu.VMEM((2, mine_images, half), low_type),
        pltpu.VMEM((2, head_rows, mine_images), low_type),
        pltpu.VMEM((6, 8, channels), wide),
        pltpu.VMEM((6, 8, channels), wide),
        pltpu.VMEM((24, max(width, group)), wide),
        pltpu.VMEM((3, 8, channels), wide),
        pltpu.SemaphoreType.DMA((11,)),
        pltpu.SemaphoreType.DMA((2, 6)),
        pltpu.SemaphoreType.DMA((2, 7)),
    ]
    any_space = pl.BlockSpec(memory_space=pl.ANY)
    if gather:
        counts = (channels // blocks, middle // blocks, channels // blocks)
        scratch += [pltpu.SemaphoreType.DMA((2, 3, 3))]
        scratch += [pltpu.SemaphoreType.DMA((2, 4, 6)) for _ in range(2)]
        scratch += [pltpu.SemaphoreType.DMA((2, 4, 3))]
        scratch += [pltpu.VMEM((4, 2, 2, rows, width), low_type) for rows in counts[1:]]
        for lead in ((4, 2), (4,), (4,)):
            scratch += [pltpu.VMEM(lead + (rows, width), low_type) for rows in counts]
        scratch += [pltpu.SemaphoreType.DMA((2, 4, 3))]
        scratch += [pltpu.SemaphoreType.DMA((2, 4, 6)) for _ in range(3)]
        grads_shape = [jax.ShapeDtypeStruct((sum(counts), width), wide)]
        grads_specs = [any_space]
    else:
        grads_shape = [jax.ShapeDtypeStruct(weight.shape, low_type) for weight in weights]
        grads_specs = [any_space] * 3
    return pl.pallas_call(
        functools.partial(client_kernel, gather, images, classes),
        out_shape=grads_shape
        + [
            jax.ShapeDtypeStruct(params.shape, wide),
            jax.ShapeDtypeStruct((classes * half // LANES, LANES), wide),
            jax.ShapeDtypeStruct((8, LANES), wide),
        ],
        in_specs=[any_space, vmem, smem, vmem, vmem] + [any_space] * len(weights),
        out_specs=grads_specs + [vmem, any_space, vmem],
        scratch_shapes=scratch,
        compiler_params=pltpu.CompilerParams(
            collective_id=0, has_side_effects=True, vmem_limit_bytes=VMEM_BYTES
        ),
    )(features, labels, flag, params, head, *weights)


def adam_update(param, grad, first, second, rate, decay):
    first = adam_first * first + (1.0 - adam_first) * grad
    second = adam_second * second + (1.0 - adam_second) * grad * grad
    first_hat = first / (1.0 - adam_first**STEP)
    second_hat = second / (1.0 - adam_second**STEP)
    return (
        param - rate * (first_hat / (jnp.sqrt(second_hat) + adam_epsilon) + decay * param),
        first,
        second,
    )
class GramSum:
    def __init__(self, place, data, total, boxes, sems):
        self.place = place
        self.data = data
        self.total = total
        self.core_box, self.near_box, self.far_box, self.z_box = boxes
        self.sems = sems
        self.copies = []
        self.sizes = (data.shape[0] // 72 * 40 // 32, data.shape[0] // 72 * 32 // 32)

    def rows(self, kind, core, z=None, first=None, second=None):
        size = self.sizes[kind]
        start = core * (16 * (self.sizes[0] + self.sizes[1])) + kind * 16 * self.sizes[0]
        count = 16 * size
        for number, spot, parts in ((4 * size, z, 4), (2 * size, first, 2), (size, second, 2)):
            if spot is None:
                break
            start, count = start + spot * number, number
        return pl.ds(pl.multiple_of(start, 8), count)

    def ways(self, kind):
        p = self.place
        x_way, y_way = (p.x, p.along_x()), (p.y, p.along_y())
        return (x_way, y_way) if kind == 0 else (y_way, x_way)

    def copy(self, phase, kind, turn, src, dst, client, core):
        sems = self.sems
        return remote(
            src, dst, sems.at[0, phase, kind, turn], sems.at[1, phase, kind, turn], client, core
        )

    def launch(self, copy):
        copy.start()
        self.copies.append(copy)

    def down(self, phase, kind, turn):
        p = self.place
        z = (p.others[::-1] + [p.z])[turn]
        (first, first_to), (second, second_to) = self.ways(kind)
        base = self.sizes[0] * kind
        if phase == 0:
            src = self.data.at[self.rows(kind, 1 - p.core, z), :]
            box = self.core_box.at[turn, pl.ds(4 * base, 4 * self.sizes[kind]), :]
            return self.copy(0, kind, turn, src, box, p.client, 1 - p.core)
        if phase == 1:
            src = self.data.at[self.rows(kind, p.core, z, 1 - first), :]
            box = self.near_box.at[turn, pl.ds(2 * base, 2 * self.sizes[kind]), :]
            return self.copy(1, kind, turn, src, box, first_to, p.core)
        if phase == 2:
            src = self.data.at[self.rows(kind, p.core, z, first, 1 - second), :]
            box = self.far_box.at[turn, pl.ds(base, self.sizes[kind]), :]
            return self.copy(2, kind, turn, src, box, second_to, p.core)
        src = self.data.at[self.rows(kind, p.core, z, first, second), :]
        box = self.z_box.at[turn, pl.ds(base, self.sizes[kind]), :]
        return self.copy(3, kind, turn, src, box, p.along_z(2 - turn), p.core)

    def down_step(self, phase, kind, turn):
        p = self.place
        z = (p.others[::-1] + [p.z])[turn]
        (first, _), (second, _) = self.ways(kind)
        self.down(phase, kind, turn).wait_recv()
        spots = (z, first, second)[: phase + 1]
        where = self.rows(kind, p.core, *spots)
        scale = (4, 2, 1)[phase]
        box = (self.core_box, self.near_box, self.far_box)[phase]
        self.data[where, :] += box[turn, pl.ds(scale * self.sizes[0] * kind, scale * self.sizes[kind]), :]
        if phase < 2 or turn < 3:
            self.launch(self.down(phase + 1, kind, turn))

    def up(self, phase, kind, turn):
        p = self.place
        z = ([p.z] + p.others)[turn]
        (first, first_to), (second, second_to) = self.ways(kind)
        if phase == 0:
            ref, to = self.total.at[self.rows(kind, p.core, p.z, first, second), :], p.along_z(turn)
        elif phase == 1:
            ref, to = self.total.at[self.rows(kind, p.core, z, first, second), :], second_to
        elif phase == 2:
            ref, to = self.total.at[self.rows(kind, p.core, z, first), :], first_to
        else:
            ref, to = self.total.at[self.rows(kind, p.core, z), :], p.client
        return self.copy(4 + phase, kind, turn, ref, ref, to, 1 - p.core if phase == 3 else p.core)

    def run(self, extra):
        extra = list(extra)
        kinds = (0, 1)
        for turn in range(4):
            for kind in kinds:
                self.launch(self.down(0, kind, turn))
        for turn in range(6):
            if extra:
                extra.pop(0)()
            for kind in kinds:
                for phase in range(3):
                    if 0 <= turn - phase < 4:
                        self.down_step(phase, kind, turn - phase)
        p = self.place
        for kind in kinds:
            (first, _), (second, _) = self.ways(kind)
            where = self.rows(kind, p.core, p.z, first, second)
            value = self.data[where, :]
            for turn in range(3):
                self.down(3, kind, turn).wait_recv()
                value += self.z_box[turn, pl.ds(self.sizes[0] * kind, self.sizes[kind]), :]
            self.total[where, :] = value
            self.launch(self.up(1, kind, 0))
            for turn in range(3):
                self.launch(self.up(0, kind, turn))
        for turn in range(6):
            for kind in kinds:
                if 1 <= turn < 4:
                    self.up(0, kind, turn - 1).wait_recv()
                    self.launch(self.up(1, kind, turn))
                if 1 <= turn < 5:
                    self.up(1, kind, turn - 1).wait_recv()
                    self.launch(self.up(2, kind, turn - 1))
                if 2 <= turn:
                    self.up(2, kind, turn - 2).wait_recv()
                    self.launch(self.up(3, kind, turn - 2))
        for turn in range(4):
            for kind in kinds:
                self.up(3, kind, turn).wait_recv()

    def drain(self):
        for copy in self.copies:
            copy.wait_send()


class TileSum:
    def __init__(self, place, tiles, boxes, sems):
        self.place = place
        self.tiles = tiles
        self.boxes = boxes
        self.sems = sems

    def copy(self, stage, box):
        p = self.place
        to = (p.client, p.along_x(), p.along_y()) + tuple(p.along_z(step) for step in range(3))
        core = 1 - p.core if box == 0 else p.core
        return remote(
            self.tiles.at[stage], self.boxes.at[box], self.sems.at[0, box], self.sems.at[1, box], to[box], core
        )

    def steps(self):
        def start():
            self.copy(0, 0).start()

        def pair(stage):
            self.copy(stage, stage).wait_recv()
            self.tiles[stage + 1] = self.tiles[stage] + self.boxes[stage]
            if stage < 2:
                self.copy(stage + 1, stage + 1).start()
            else:
                for step in range(3):
                    self.copy(3, 3 + step).start()

        return [start] + [functools.partial(pair, stage) for stage in range(3)]

    def result(self):
        for step in range(3):
            self.copy(3, 3 + step).wait_recv()
        return (self.tiles[3] + self.boxes[3]) + (self.boxes[4] + self.boxes[5])

    def drain(self):
        for stage in range(3):
            self.copy(stage, stage).wait_send()
        for step in range(3):
            self.copy(3, 3 + step).wait_send()


def dot_high(left, right):
    return jnp.dot(left, right, precision=lax.Precision.HIGH, preferred_element_type=wide)


def base_kernel(
    ratios,
    sizes,
    master,
    momentum,
    anchor,
    loss_in,
    grads,
    *rest,
):
    place = Place()
    rest = list(rest)

    def take(count):
        taken = rest[:count]
        del rest[:count]
        return taken

    ortho_out, loss_out = take(2)
    gram, gram_total = take(2)
    gram_boxes = take(4)
    grams, iterate, tiles, tile_boxes = take(4)
    gram_sems, tile_sems = take(2)

    place.greet(True)
    tiles[0] = loss_in[...]
    tile_sum = TileSum(place, tiles, tile_boxes, tile_sems)
    extra = tile_sum.steps()
    extra.pop(0)()

    bounds = [0]
    for size in sizes:
        bounds.append(bounds[-1] + size)
    width = master.shape[1]
    part = width // 2
    for slot in range(3):
        rows = slice(bounds[slot], bounds[slot + 1])
        grad = grads[rows, :] + prox_weight * (master[rows, :] - anchor[rows, :])
        fresh = momentum_decay * momentum[rows, :] + grad
        ortho_out[rows, :] = fresh
        partial = lax.dot_general(
            fresh, fresh, (((0,), (0,)), ((), ())), precision=precise, preferred_element_type=wide
        )
        start = 3 * part * slot
        gram[start : start + part, :] = partial[:part, :part]
        gram[start + part : start + 2 * part, :] = partial[:part, part:]
        gram[start + 2 * part : start + 3 * part, :] = partial[part:, part:]

    gram_sum = GramSum(place, gram, gram_total, gram_boxes, gram_sems)

    gram_sum.run(extra)
    loss_out[...] = tile_sum.result()

    spots = lax.broadcasted_iota(jnp.int32, (part, part), 0)
    diagonal = spots == lax.broadcasted_iota(jnp.int32, (part, part), 1)
    iterate[...] = jnp.zeros_like(iterate)
    for slot in range(3):
        start = 3 * part * slot
        corner = gram_total[start : start + part, :]
        side = gram_total[start + part : start + 2 * part, :]
        end = gram_total[start + 2 * part : start + 3 * part, :]
        trace = jnp.sum(jnp.where(diagonal, corner + end, 0.0))
        factor = 1.0 / (jnp.sqrt(trace) + 1e-07)
        square = factor * factor
        grams[slot, :part, :part] = corner * square
        grams[slot, :part, part:] = side * square
        grams[slot, part:, :part] = side.T * square
        grams[slot, part:, part:] = end * square
        rows = slice(bounds[slot], bounds[slot + 1])
        iterate[slot, : bounds[slot + 1] - bounds[slot], :] = ortho_out[rows, :] * factor

    def turn(count, carry):
        slot = lax.rem(count, 3)
        current = grams[slot]
        mixed = schulz_second * current + schulz_third * dot_high(current, current)
        held = iterate[slot]
        iterate[slot] = schulz_first * held + dot_high(held, mixed)

        @pl.when(count < 3 * (NS_STEPS - 1))
        def _():
            once = schulz_first * current + dot_high(current, mixed)
            grams[slot] = schulz_first * once + dot_high(once, mixed)

        return carry

    lax.fori_loop(0, 3 * NS_STEPS, turn, 0)
    for slot in range(3):
        ortho_out[bounds[slot] : bounds[slot + 1], :] = (
            iterate[slot, : bounds[slot + 1] - bounds[slot], :] * ratios[slot]
        )
    gram_sum.drain()
    tile_sum.drain()


def base_pass(ratios, sizes, master, momentum, anchor, loss_tile, grads):
    rows, width = master.shape
    part = width // 2
    vmem = pl.BlockSpec(memory_space=pltpu.VMEM)
    share = 9 * part // 32
    scratch = [pltpu.VMEM((9 * part, part), wide)] * 2
    scratch += [pltpu.VMEM((4, size, part), wide) for size in (4 * share, 2 * share, share)]
    scratch += [pltpu.VMEM((3, share, part), wide)]
    scratch += [
        pltpu.VMEM((3, width, width), wide),
        pltpu.VMEM((3, max(sizes), width), wide),
        pltpu.VMEM((4, 8, LANES), wide),
        pltpu.VMEM((6, 8, LANES), wide),
        pltpu.SemaphoreType.DMA((2, 8, 2, 4)),
        pltpu.SemaphoreType.DMA((2, 6)),
    ]
    block = jax.ShapeDtypeStruct((rows, width), wide)
    outs = [block, jax.ShapeDtypeStruct((8, LANES), wide)]
    operands = [master, momentum, anchor, loss_tile, grads]
    return pl.pallas_call(
        functools.partial(base_kernel, ratios, sizes),
        out_shape=outs,
        in_specs=[vmem] * len(operands),
        out_specs=[vmem] * len(outs),
        scratch_shapes=scratch,
        compiler_params=pltpu.CompilerParams(
            collective_id=1, has_side_effects=True, vmem_limit_bytes=VMEM_BYTES
        ),
    )(*operands)


def update_kernel(master, momentum, anchor, grads, ortho, *rest):
    norms, grad_norm, heads, grad_head, outs = rest[0:3], rest[3], rest[4:7], rest[7], rest[8:]
    momentum_out, base_out, low_out = outs[0:3]
    held = master[...]
    momentum_out[...] = momentum_decay * momentum[...] + (grads[...] + prox_weight * (held - anchor[...]))
    fresh = held - muon_rate * (ortho[...] + muon_decay * held)
    base_out[...] = fresh
    low_out[...] = fresh.astype(low_type)
    for targets, values, grad, rate, decay in (
        (outs[3:6], norms, grad_norm, norm_rate, 0.0),
        (outs[6:9], heads, grad_head, head_rate, head_decay),
    ):
        updates = adam_update(values[0][...], grad[...], values[1][...], values[2][...], rate, decay)
        for target, value in zip(targets, updates):
            target[...] = value


def update_pass(master, momentum, anchor, grads, ortho, norms, grad_norm, heads, grad_head):
    vmem = pl.BlockSpec(memory_space=pltpu.VMEM)
    operands = [master, momentum, anchor, grads, ortho, *norms, grad_norm, *heads, grad_head]
    outs = [master.shape, master.shape, master.shape] + [grad_norm.shape] * 3 + [grad_head.shape] * 3
    types = [wide, wide, low_type] + [wide] * 6
    return pl.pallas_call(
        update_kernel,
        out_shape=[jax.ShapeDtypeStruct(shape, kind) for shape, kind in zip(outs, types)],
        in_specs=[vmem] * len(operands),
        out_specs=[vmem] * len(outs),
        compiler_params=pltpu.CompilerParams(vmem_limit_bytes=VMEM_BYTES),
    )(*operands)


def gram_of(section):
    return lax.dot_general(section, section, (((0,), (0,)), ((), ())), precision=precise)


def square(gram):
    return jnp.dot(gram, gram, precision=precise)


def times_poly(left, mixed):
    return schulz_first * left + jnp.dot(left, mixed, precision=precise)


def schulz(sections):
    raw_grams = lax.psum(tuple(gram_of(section) for section in sections), ("client", "chan"))
    factors = [1.0 / (jnp.sqrt(jnp.trace(gram)) + 1e-07) for gram in raw_grams]
    current = [section * factor for section, factor in zip(sections, factors)]
    grams = [gram * (factor * factor) for gram, factor in zip(raw_grams, factors)]
    for turn in range(NS_STEPS):
        mixed = [schulz_second * gram + schulz_third * square(gram) for gram in grams]
        current = [times_poly(current[slot], mixed[slot]) for slot in range(3)]
        if turn + 1 < NS_STEPS:
            grams = [
                times_poly(times_poly(grams[slot], mixed[slot]), mixed[slot]) for slot in range(3)
            ]
    return current


def base_far(ratios, bounds, master, momentum, anchor, loss_tile, grads):
    sums = [
        lax.psum_scatter(flat_rows(grad).astype(wide), ("client", "chan"), scatter_dimension=0, tiled=True)
        for grad in grads
    ]
    grad_base = jnp.concatenate(sums, axis=0)
    momentum_new = momentum_decay * momentum + (grad_base + prox_weight * (master - anchor))
    current = schulz([momentum_new[bounds[slot] : bounds[slot + 1]] for slot in range(3)])
    ortho = jnp.concatenate([current[slot] * ratios[slot] for slot in range(3)], axis=0)
    return grad_base, ortho, lax.psum(loss_tile, ("client", "chan"))


def as_stored(rows, shape):
    return with_layout_constraint(rows.reshape(shape), Layout(major_to_minor=tuple(range(len(shape)))))


def on_device(
    features,
    labels,
    mask,
    base_master,
    base_momentum,
    global_base,
    norm_params,
    norm_first,
    norm_second,
    head,
    head_first,
    head_second,
):
    halves = lax.axis_size("chan")
    blocks = lax.axis_size("client") * halves
    half = features.shape[2]
    width = base_master.shape[2]
    channels = half * halves
    classes = head.shape[2]
    rows_first = channels // blocks
    rows_mid = 9 * width // blocks
    sizes = (rows_first, rows_mid, rows_first)
    bounds = (0, rows_first, rows_first + rows_mid, base_master.shape[1])
    ratio = (channels / width) ** 0.5
    ratios = (ratio, 3.0, ratio)
    master, momentum, anchor = base_master[0], base_momentum[0], global_base[0]
    norms = [value.reshape(-1, LANES) for value in (norm_params, norm_first, norm_second)]
    heads = [jnp.transpose(value, (2, 0, 1)).reshape(-1, LANES) for value in (head, head_first, head_second)]
    near = lax.axis_size("client") == SPOTS[0] * SPOTS[1] * SPOTS[2]
    if near:
        weights = [master]
    else:
        low_master = master.astype(low_type)
        weights = [
            lax.all_gather(low_master[bounds[slot] : bounds[slot + 1]], ("client", "chan"), axis=0, tiled=True)
            for slot in range(3)
        ]
        weights = [weight.reshape(SPOTS + (2, weight.shape[0] // 32, width)) for weight in weights]
    *grads, grad_norm, grad_head, loss_tile = client_pass(
        near, classes, features[0], labels, mask, norms[0], heads[0], weights
    )
    if near:
        (grad_base,) = grads
        ortho, loss_tile = base_pass(ratios, sizes, master, momentum, anchor, loss_tile, grad_base)
    else:
        grad_base, ortho, loss_tile = base_far(ratios, bounds, master, momentum, anchor, loss_tile, grads)
    momentum_new, base_new, base_low, *fresh = update_pass(
        master, momentum, anchor, grad_base, ortho, norms, grad_norm, heads, grad_head
    )
    fresh_norms = [as_stored(value, norm_params.shape) for value in fresh[:3]]
    fresh_heads = [jnp.transpose(as_stored(value, (classes, 1, half)), (1, 2, 0)) for value in fresh[3:]]
    return (
        loss_tile[0, 0:2],
        base_new[None],
        momentum_new[None],
        base_low[None],
        *fresh_norms,
        *fresh_heads,
    )


def solution(mesh):
    wide_block = P(("client", "chan"), None, None)
    norm_block = P("client", None, "chan", None)
    head_block = P("client", "chan", None)
    return jax.shard_map(
        on_device,
        mesh=mesh,
        in_specs=(P("client", None, "chan"), P("client", None), P("client"))
        + (wide_block,) * 3
        + (norm_block,) * 3
        + (head_block,) * 3,
        out_specs=(P(),) + (wide_block,) * 3 + (norm_block,) * 3 + (head_block,) * 3,
        check_vma=False,
    )
```

profile of v0, /device:TPU:0, one launch (start us, length us, event | category | flops | bytes accessed | tf_op | source)
XLA Modules:
  0.0 271.2 jit_solution(7097274413927106913)
XLA Ops:
  1.3 175.3 %shard_map.195 = (f32[272,512]{1,0:T(8,128)}, f32[24,128]{1,0:T(8,128)}, f32[800,128]{1,0:T(8,128)}, f32[8,128]{1,0:T(8,128)}) custom-call(bf16[3136,1024]{1,0:T(8,128)(2,1)} %bitcast.33, s32[1,64]{1,0:T(1,128)} %labels.1, s32[1]{0:T(128)S(6)} %copy.22.flag, f32[24,128]{1,0:T(8,128)} %bitcast.45, f32[800,128]{1,0:T(8,128)} %bitcast.41, f32[272,512]{1,0:T(8,128)} %bitcast.34), custom_call_target="tpu_custom_call" | custom-call | tf_op jit(solution)/shard_map/pallas_call | solution.py:1122
  176.6 89.4 %shard_map.196 = (f32[272,512]{1,0:T(8,128)}, f32[8,128]{1,0:T(8,128)}) custom-call(f32[272,512]{1,0:T(8,128)} %bitcast.35, f32[272,512]{1,0:T(8,128)} %bitcast.37, f32[272,512]{1,0:T(8,128)} %bitcast.39, f32[8,128]{1,0:T(8,128)} %get-tuple-element.25.loss_in, f32[272,512]{1,0:T(8,128)} %get-tuple-element.26.grads), custom_call_target="tpu_custom_call" | custom-call | tf_op jit(solution)/shard_map/pallas_call | solution.py:1436
  266.0 1.2 slice_bitcast_fusion
  267.2 4.0 %shard_map.197 = (f32[272,512]{1,0:T(8,128)}, f32[272,512]{1,0:T(8,128)}, bf16[272,512]{1,0:T(8,128)(2,1)}, f32[24,128]{1,0:T(8,128)}, f32[24,128]{1,0:T(8,128)}...) custom-call(f32[272,512]{1,0:T(8,128)} %bitcast.36, f32[272,512]{1,0:T(8,128)} %bitcast.38, ...), custom_call_target="tpu_custom_call" | custom-call | tf_op jit(solution)/shard_map/pallas_call | solution.py:1470
where the time goes:
time: 273 us; the launch traced here: 271 us
  Pallas kernels  269 us (99%)
    pallas_call x1, Pallas kernels, client_pass(): pl.pallas_call(functools.partial(client_kernel, gather, images, classes),...  175 us
    pallas_call x1, Pallas kernels, base_pass(): pl.pallas_call(functools.partial(base_kernel, ratios, sizes), out_shape=o...  89.4 us

commit v1 on v0

--- a/solution.py
+++ b/solution.py
@@ -129,55 +129,69 @@
     return pieces
 
 
+def block_ref(ref, size, z, y, x, core, start, count):
+    if len(ref.shape) == 2:
+        first = (((z * 2 + y) * 2 + x) * 2 + core) * size + start
+        return ref.at[pl.ds(pl.multiple_of(first, 16), count), :]
+    return ref.at[z, y, x, core, pl.ds(start, count), :]
+
+
 class Spread:
-    def __init__(self, place, weights, sems):
+    def __init__(self, place, weights, counts, sems):
         self.place = place
         self.weights = weights
-        self.pieces = cut_rows([weight.shape[-2] for weight in weights])
+        self.counts = counts
+        self.pieces = cut_rows(counts)
         self.z_sems, self.near_sems, self.far_sems, self.core_sems = sems
         self.order = [place.z] + place.others
 
     def z_copy(self, step, slot):
         p = self.place
-        ref = self.weights[slot].at[p.z, p.y, p.x, p.core]
+        ref = block_ref(self.weights[slot], self.counts[slot], p.z, p.y, p.x, p.core, 0, self.counts[slot])
         sems = self.z_sems
         return remote(ref, ref, sems.at[0, step, slot], sems.at[1, step, slot], p.along_z(step), p.core)
 
     def near_copy(self, turn, number):
         p = self.place
         slot, start, count, way = self.pieces[number]
-        ref = self.weights[slot].at[self.order[turn], p.y, p.x, p.core, pl.ds(start, count), :]
+        ref = block_ref(self.weights[slot], self.counts[slot], self.order[turn], p.y, p.x, p.core, start, count)
         sems = self.near_sems
         return remote(
             ref, ref, sems.at[0, turn, number], sems.at[1, turn, number], (p.along_x, p.along_y)[way](), p.core
         )
 
-    def far_copy(self, turn, number):
+    def far_copies(self, turn, number):
         p = self.place
         slot, start, count, way = self.pieces[number]
-        rows = pl.ds(start, count)
         spot = self.order[turn]
-        if way == 0:
-            ref = self.weights[slot].at[spot, p.y, :, p.core, rows, :]
-        else:
-            ref = self.weights[slot].at[spot, :, p.x, p.core, rows, :]
         sems = self.far_sems
-        return remote(
-            ref, ref, sems.at[0, turn, number], sems.at[1, turn, number], (p.along_y, p.along_x)[way](), p.core
-        )
-
-    def core_copy(self, turn, slot):
-        p = self.place
-        ref = self.weights[slot].at[self.order[turn], :, :, p.core]
+        copies = []
+        for part, other in enumerate((0, 1) if slot == 1 else (slice(None),)):
+            y, x = (p.y, other) if way == 0 else (other, p.x)
+            ref = block_ref(self.weights[slot], self.counts[slot], spot, y, x, p.core, start, count)
+            sem = number + 4 * part
+            to = (p.along_y, p.along_x)[way]()
+            copies.append(remote(ref, ref, sems.at[0, turn, sem], sems.at[1, turn, sem], to, p.core))
+        return copies
+
+    def core_copies(self, turn, slot):
+        p = self.place
         sems = self.core_sems
-        return remote(ref, ref, sems.at[0, turn, slot], sems.at[1, turn, slot], p.client, 1 - p.core)
+        copies = []
+        pairs = [(y, x) for y in (0, 1) for x in (0, 1)] if slot == 1 else [(slice(None), slice(None))]
+        for part, (y, x) in enumerate(pairs):
+            ref = block_ref(self.weights[slot], self.counts[slot], self.order[turn], y, x, p.core, 0, self.counts[slot])
+            sem = (0, 2 + part, 1)[slot]
+            copies.append(remote(ref, ref, sems.at[0, turn, sem], sems.at[1, turn, sem], p.client, 1 - p.core))
+        return copies
 
     def begin(self, master):
         p = self.place
         start = 0
         for slot in range(3):
-            rows = self.weights[slot].shape[-2]
-            self.weights[slot][p.z, p.y, p.x, p.core] = master[start : start + rows, :].astype(low_type)
+            rows = self.counts[slot]
+            own = block_ref(self.weights[slot], self.counts[slot], p.z, p.y, p.x, p.core, 0, rows)
+            own[...] = master[start : start + rows, :].astype(low_type)
             start += rows
         for step in range(3):
             self.z_copy(step, 0).start()
@@ -218,27 +232,33 @@
     def far_step(self, turn, slot):
         for number in (2 * slot, 2 * slot + 1):
             self.near_copy(turn, number).wait_recv()
-            self.far_copy(turn, number).start()
+            for copy in self.far_copies(turn, number):
+                copy.start()
 
     def core_step(self, turn, slot):
         for number in (2 * slot, 2 * slot + 1):
-            self.far_copy(turn, number).wait_recv()
-        self.core_copy(turn, slot).start()
+            for copy in self.far_copies(turn, number):
+                copy.wait_recv()
+        for copy in self.core_copies(turn, slot):
+            copy.start()
 
     def arrive(self, slot):
         for turn in range(4):
-            self.core_copy(turn, slot).wait_recv()
+            for copy in self.core_copies(turn, slot):
+                copy.wait_recv()
 
     def drain(self):
         for slot in range(3):
             for step in range(3):
                 self.z_copy(step, slot).wait_send()
             for turn in range(4):
-                self.core_copy(turn, slot).wait_send()
+                for copy in self.core_copies(turn, slot):
+                    copy.wait_send()
         for number in range(6):
             for turn in range(4):
                 self.near_copy(turn, number).wait_send()
-                self.far_copy(turn, number).wait_send()
+                for copy in self.far_copies(turn, number):
+                    copy.wait_send()
 
 
 class Fold:
@@ -251,41 +271,38 @@
         self.near_boxes, self.far_boxes, self.z_boxes = [parts[3 * k + 2 : 3 * k + 5] for k in range(3)]
         self.core_sems, self.near_sems, self.far_sems, self.z_sems = parts[11:]
 
-    def core_copy(self, which, slot):
+    def core_copies(self, which, slot):
         p = self.place
         sems = self.core_sems
-        return remote(
-            self.grads[slot].at[which, :, :, 1 - p.core, pl.ds(0, self.counts[slot]), :],
-            self.core_boxes[slot].at[which],
-            sems.at[0, which, slot],
-            sems.at[1, which, slot],
-            p.client,
-            1 - p.core,
-        )
-
-    def near_copy(self, which, number):
+        copies = []
+        pairs = [(y, x) for y in (0, 1) for x in (0, 1)] if slot == 1 else [(slice(None), slice(None))]
+        for part, (y, x) in enumerate(pairs):
+            ref = block_ref(self.grads[slot], self.counts[slot], which, y, x, 1 - p.core, 0, self.counts[slot])
+            box = self.core_boxes[slot].at[which, y, x]
+            sem = (0, 2 + part, 1)[slot]
+            copies.append(remote(ref, box, sems.at[0, which, sem], sems.at[1, which, sem], p.client, 1 - p.core))
+        return copies
+
+    def near_copies(self, which, number):
         p = self.place
         slot, start, count, way = self.pieces[number]
-        rows = pl.ds(start, count)
-        if way == 0:
-            ref = self.grads[slot].at[which, :, 1 - p.x, p.core, rows, :]
-        else:
-            ref = self.grads[slot].at[which, 1 - p.y, :, p.core, rows, :]
-        box = self.near_boxes[slot].at[which, :, rows, :]
         sems = self.near_sems
-        return remote(
-            ref, box, sems.at[0, which, number], sems.at[1, which, number], (p.along_x, p.along_y)[way](), p.core
-        )
+        copies = []
+        for part, other in enumerate((0, 1) if slot == 1 else (slice(None),)):
+            y, x = (other, 1 - p.x) if way == 0 else (1 - p.y, other)
+            ref = block_ref(self.grads[slot], self.counts[slot], which, y, x, p.core, start, count)
+            box = self.near_boxes[slot].at[which, other, pl.ds(start, count), :]
+            sem = number + 4 * part
+            to = (p.along_x, p.along_y)[way]()
+            copies.append(remote(ref, box, sems.at[0, which, sem], sems.at[1, which, sem], to, p.core))
+        return copies
 
     def far_copy(self, which, number):
         p = self.place
         slot, start, count, way = self.pieces[number]
-        rows = pl.ds(start, count)
-        if way == 0:
-            ref = self.grads[slot].at[which, 1 - p.y, p.x, p.core, rows, :]
-        else:
-            ref = self.grads[slot].at[which, p.y, 1 - p.x, p.core, rows, :]
-        box = self.far_boxes[slot].at[which, rows, :]
+        y, x = (1 - p.y, p.x) if way == 0 else (p.y, 1 - p.x)
+        ref = block_ref(self.grads[slot], self.counts[slot], which, y, x, p.core, start, count)
+        box = self.far_boxes[slot].at[which, pl.ds(start, count), :]
         sems = self.far_sems
         return remote(
             ref, box, sems.at[0, which, number], sems.at[1, which, number], (p.along_y, p.along_x)[way](), p.core
@@ -297,7 +314,7 @@
         rows = pl.ds(start, count)
         sems = self.z_sems
         return remote(
-            self.grads[slot].at[which, p.y, p.x, p.core, rows, :],
+            block_ref(self.grads[slot], self.counts[slot], which, p.y, p.x, p.core, start, count),
             self.z_boxes[slot].at[sender, rows, :],
             sems.at[0, which, number],
             sems.at[1, sender, number],
@@ -306,45 +323,46 @@
         )
 
     def begin(self, which, slot):
-        self.core_copy(which, slot).start()
+        for copy in self.core_copies(which, slot):
+            copy.start()
+
+    def add(self, slot, spots, start, count, box):
+        ref = block_ref(self.grads[slot], self.counts[slot], *spots, self.place.core, start, count)
+        ref[...] = (ref[...].astype(wide) + box.astype(wide)).astype(low_type)
 
     def turn(self, slot, turn):
         for lag, step in ((2, self.far_step), (1, self.near_step), (0, self.core_step)):
             when((turn >= lag) & (turn < lag + 4), functools.partial(step, turn - lag, slot))
 
     def core_step(self, which, slot):
-        p = self.place
-        rows = pl.ds(0, self.counts[slot])
-        self.core_copy(which, slot).wait_recv()
-        where = (which, slice(None), slice(None), p.core, rows, slice(None))
-        both = self.grads[slot][where].astype(wide) + self.core_boxes[slot][which].astype(wide)
-        self.grads[slot][where] = both.astype(low_type)
+        for copy in self.core_copies(which, slot):
+            copy.wait_recv()
+        pairs = [(y, x) for y in (0, 1) for x in (0, 1)] if slot == 1 else [(slice(None), slice(None))]
+        for y, x in pairs:
+            self.add(slot, (which, y, x), 0, self.counts[slot], self.core_boxes[slot][which, y, x])
         for number in (2 * slot, 2 * slot + 1):
-            self.near_copy(which, number).start()
+            for copy in self.near_copies(which, number):
+                copy.start()
 
     def near_step(self, which, slot):
         p = self.place
         for number in (2 * slot, 2 * slot + 1):
             _, start, count, way = self.pieces[number]
-            rows = pl.ds(start, count)
-            self.near_copy(which, number).wait_recv()
-            if way == 0:
-                where = (which, slice(None), p.x, p.core, rows, slice(None))
-            else:
-                where = (which, p.y, slice(None), p.core, rows, slice(None))
-            both = self.grads[slot][where].astype(wide) + self.near_boxes[slot][which, :, rows, :].astype(wide)
-            self.grads[slot][where] = both.astype(low_type)
+            for copy in self.near_copies(which, number):
+                copy.wait_recv()
+            for other in (0, 1) if slot == 1 else (slice(None),):
+                y, x = (other, p.x) if way == 0 else (p.y, other)
+                box = self.near_boxes[slot][which, other, pl.ds(start, count), :]
+                self.add(slot, (which, y, x), start, count, box)
             self.far_copy(which, number).start()
 
     def far_step(self, which, slot):
         p = self.place
         for number in (2 * slot, 2 * slot + 1):
             _, start, count, way = self.pieces[number]
-            rows = pl.ds(start, count)
             self.far_copy(which, number).wait_recv()
-            where = (which, p.y, p.x, p.core, rows, slice(None))
-            both = self.grads[slot][where].astype(wide) + self.far_boxes[slot][which, rows, :].astype(wide)
-            self.grads[slot][where] = both.astype(low_type)
+            box = self.far_boxes[slot][which, pl.ds(start, count), :]
+            self.add(slot, (which, p.y, p.x), start, count, box)
 
             @pl.when(p.z != which)
             def _():
@@ -352,8 +370,7 @@
 
     def result(self, slot):
         p = self.place
-        rows = pl.ds(0, self.counts[slot])
-        self.z_boxes[slot][p.z] = self.grads[slot][p.z, p.y, p.x, p.core, rows, :]
+        self.z_boxes[slot][p.z] = block_ref(self.grads[slot], self.counts[slot], p.z, p.y, p.x, p.core, 0, self.counts[slot])[...]
         for sender in range(4):
 
             @pl.when(p.z != sender)
@@ -369,9 +386,11 @@
     def drain(self):
         for which in range(4):
             for slot in range(3):
-                self.core_copy(which, slot).wait_send()
+                for copy in self.core_copies(which, slot):
+                    copy.wait_send()
             for number in range(6):
-                self.near_copy(which, number).wait_send()
+                for copy in self.near_copies(which, number):
+                    copy.wait_send()
                 self.far_copy(which, number).wait_send()
 
             @pl.when(self.place.z != which)
@@ -462,18 +481,10 @@
     top_rows = pl.ds(0, count_rows)
     own_copies = [
         pltpu.make_async_copy(
-            features.at[own_rows, pl.ds(0, quarter)], hidden_two, sem_local.at[0]
+            features.at[own_rows, pl.ds(side * quarter, quarter)], buffer, sem_local.at[side]
         )
+        for side, buffer in enumerate((hidden_two, mid_wide.at[top_rows, :]))
     ]
-    for index in range(SIDE):
-        rows = pl.ds(pl.multiple_of(core * count_rows + index * line, line), line)
-        own_copies.append(
-            pltpu.make_async_copy(
-                features.at[rows, pl.ds(quarter, quarter)],
-                mid_wide.at[0, index // 4, (index // 2) % 2, index % 2],
-                sem_local.at[1 + index],
-            )
-        )
     per_kind = params.shape[0] // 2
     for kind in range(2):
         rows = [params[kind * per_kind + spot : kind * per_kind + spot + 1, :] for spot in range(per_kind)]
@@ -502,13 +513,13 @@
 
     weights = (w_first, w_middle, w_last)
     if gather:
-        spread = Spread(place, weights, near_parts[:4])
+        counts = [channels // 32, 9 * width // 32, channels // 32]
+        spread = Spread(place, weights, counts, near_parts[:4])
         held = act_three.at[pl.ds(0, master.shape[0]), pl.ds(0, width)]
         load = pltpu.make_async_copy(master, held, sem_local.at[8])
         load.start()
         load.wait()
         spread.begin(held)
-        counts = [weight.shape[-2] for weight in weights]
         fold = Fold(place, (w_first, mid_wide, w_last), counts, near_parts[4:])
         due = spread.steps()
     else:
@@ -580,7 +591,7 @@
     lax.fori_loop(
         0,
         quarters,
-        turn_from(lambda columns: mid_wide[0, :, :, :, :, columns].reshape(8 * line, LANES)[:count_rows], own_base + quarter),
+        turn_from(lambda columns: mid_wide[0:count_rows, columns], own_base + quarter),
         0,
     )
     advance(1)
@@ -625,6 +636,16 @@
         sums_mine[slot, 0:1, columns] = shift[0:1, pl.ds(0, size)] + sum_gap / count_rows
         sums_mine[slot, 1:2, columns] = sum_square - sum_gap * sum_gap / count_rows
 
+    def look_over(act, columns):
+        def look(index, carry):
+            collect(index, act[tile(index), columns], None, width)
+            return carry
+
+        lax.fori_loop(0, SIDE, look, 0)
+
+    groups = SPOTS[0]
+    group = channels // groups
+
     def settle(slot, size):
         mean, scale = norm_stats(
             sums_mine[slot, 0:2, pl.ds(0, size)], sums_theirs[slot, 0:2, pl.ds(0, size)], float(count_rows)
@@ -634,15 +655,15 @@
 
     whole_width = pl.ds(0, width)
 
-    def first_tile(index, carry):
-        value = dot_nn(x_all[tile(index), :], flat_rows(w_first[...]))
-        act_one[tile(index), :] = value
-        collect(index, value, whole_width, width)
-        advance_at(index, (1, 3, 5))
+    def first_part(index, carry):
+        act_one[...] += dot_nn(x_all[:, lanes(index, group)], flat_rows(w_first[index]))
+        advance_at(index, (0, 1, 2))
         return carry
 
-    lax.fori_loop(0, SIDE, first_tile, 0)
+    act_one[...] = jnp.zeros_like(act_one)
+    lax.fori_loop(0, groups, first_part, 0)
     del due[:3]
+    look_over(act_one, whole_width)
     close_stats(0, whole_width, width)
     move = swap(0, width)
     move.start()
@@ -665,35 +686,37 @@
     lax.fori_loop(0, SIDE, hide_one, 0)
     arrive(1, 4)
 
-    def shifted(buffer, index, down):
-        return buffer[pl.ds(pl.multiple_of((index + down) * line, line), line), :]
-
     step = mine_images
-    edge_rows = jnp.zeros((step, width), wide)
-
-    def over_lines(lines, tap_of, multiply, axis):
-        left = jnp.concatenate(lines, axis=1)
-        value = multiply(left, jnp.concatenate([tap_of(down, 1) for down in range(3)], axis=axis))
-        lower = multiply(left[: line - step], jnp.concatenate([tap_of(down, 0) for down in range(3)], axis=axis))
-        upper = multiply(left[step:], jnp.concatenate([tap_of(down, 2) for down in range(3)], axis=axis))
-        value += jnp.concatenate([edge_rows, lower], axis=0)
-        return value + jnp.concatenate([upper, edge_rows], axis=0)
-
-    def second_tile(index, carry):
-        kernel = flat_rows(w_middle[...])
-
-        def tap_of(down, over):
-            tap = 3 * down + over
-            return kernel[tap * width : (tap + 1) * width]
-
-        value = over_lines([shifted(taps_one, index, down) for down in range(3)], tap_of, dot_nn, 0)
-        act_two[tile(index), :] = value
-        collect(index, value, whole_width, width)
+    piece = width // 2
+
+    def row_windows(buffer, down, start, reach):
+        if reach == line:
+            return buffer[pl.ds(pl.multiple_of(down * line, line), count_rows), :]
+        windows = [
+            buffer[pl.ds(pl.multiple_of((down + row) * line + start, step), reach), :] for row in range(SIDE)
+        ]
+        return jnp.concatenate(windows, axis=0)
+
+    def add_windows(target, columns, value, start, reach):
+        for row in range(SIDE):
+            rows = slice(row * line + start, row * line + start + reach)
+            target[rows, columns] += value[row * reach : (row + 1) * reach]
+
+    low_start, high_start, reaches = (0, 0, step), (step, 0, 0), (line - step, line, line - step)
+
+    def second_part(index, carry):
+        down, columns = index // 2, lanes(index % 2, piece)
+        for over in range(3):
+            left = row_windows(taps_one, down, low_start[over], reaches[over])
+            kernel = w_middle[pl.ds(pl.multiple_of((3 * down + over) * width, width), width), columns]
+            add_windows(act_two, columns, dot_nn(left, kernel), high_start[over], reaches[over])
         advance_at(index, (1, 3, 5))
         return carry
 
-    lax.fori_loop(0, SIDE, second_tile, 0)
+    act_two[...] = jnp.zeros_like(act_two)
+    lax.fori_loop(0, 6, second_part, 0)
     del due[:3]
+    look_over(act_two, whole_width)
     close_stats(1, whole_width, width)
     move_two = swap(1, width)
     move_two.start()
@@ -708,19 +731,11 @@
     lax.fori_loop(0, SIDE, hide_two, 0)
 
     arrive(2, 0)
-    groups = w_last.shape[0]
-    group = channels // groups
 
     def third_group(which, carry):
         columns = lanes(which, group)
-
-        def third_tile(index, inner):
-            value = dot_nt(hidden_two[tile(index), :], flat_rows(w_last[which]))
-            act_three[tile(index), columns] = value
-            collect(index, value, columns, group)
-            return inner
-
-        lax.fori_loop(0, SIDE, third_tile, 0)
+        act_three[:, columns] = dot_nt(hidden_two[...], flat_rows(w_last[which]))
+        look_over(act_three, columns)
         close_stats(2, columns, group)
         return carry
 
@@ -738,7 +753,7 @@
         return pl.ds(pl.multiple_of(spot * mine_images, mine_images), mine_images)
 
     def mid_line(which, index):
-        return which, index // 4, (index // 2) % 2, index % 2, pl.ds(0, line)
+        return pl.ds(pl.multiple_of(which * count_rows + index * line, line), line)
 
     kept = channels // LANES * mine_images
 
@@ -763,7 +778,7 @@
                 slope = sig + out * (1.0 - sig)
                 found.append(slope.astype(low_type))
                 pooled, slopes, slopes_normed = pooled + out, slopes + slope, slopes_normed + slope * normed
-            mid_wide[mid_line(index // per_group, row) + (lanes(index % per_group, LANES),)] = jnp.concatenate(
+            mid_wide[mid_line(index // per_group, row), lanes(index % per_group, LANES)] = jnp.concatenate(
                 found, axis=0
             )
             return pooled, slopes, slopes_normed
@@ -839,7 +854,7 @@
         reach = grad_pool[:, columns] * first
 
         def pixels(row, inner):
-            where = mid_line(index // per_group, row) + (lanes(index % per_group, LANES),)
+            where = (mid_line(index // per_group, row), lanes(index % per_group, LANES))
             slopes = mid_wide[where].astype(wide)
             found = []
             for spot in range(SIDE):
@@ -863,20 +878,21 @@
     head_leave = pltpu.make_async_copy(head_space, grad_head_out, sem_local.at[0])
     head_leave.start()
 
-    def drop_into(index, value, act, slot, gain, bias, columns):
-        normed = normal(act, slot, index)
-        norm = normed * gain + bias
-        sig = sigmoid(norm)
-        grad = value * (sig + norm * sig * (1.0 - sig))
-        act_three[tile(index), columns] = grad
+    def drop_into(act, slot, gain, bias, columns):
         size = pl.ds(0, width)
-
-        @pl.when(index == 0)
-        def _():
-            shift[8:24, size] = jnp.zeros((16, width), wide)
-
-        shift[8:16, size] += fold_rows(grad)
-        shift[16:24, size] += fold_rows(grad * normed)
+        shift[8:24, size] = jnp.zeros((16, width), wide)
+
+        def drop(index, carry):
+            normed = normal(act, slot, index)
+            norm = normed * gain + bias
+            sig = sigmoid(norm)
+            grad = act_three[tile(index), columns] * (sig + norm * sig * (1.0 - sig))
+            act_three[tile(index), columns] = grad
+            shift[8:16, size] += fold_rows(grad)
+            shift[16:24, size] += fold_rows(grad * normed)
+            return carry
+
+        lax.fori_loop(0, SIDE, drop, 0)
 
     def close_back(slot):
         size = pl.ds(0, width)
@@ -885,14 +901,16 @@
 
     space_two, space_one = pl.ds(0, width), pl.ds(width, width)
 
-    def back_two(index, carry):
-        kernel = flat_rows(w_last[...])
-        left = jnp.concatenate([mid_wide[mid_line(which, index)] for which in range(groups)], axis=1)
-        value = dot_nn(left, kernel)
-        drop_into(index, value, act_two, 1, gain_two, bias_two, space_two)
+    def mid_group(which):
+        return mid_wide[pl.ds(pl.multiple_of(which * count_rows, count_rows), count_rows), :]
+
+    def back_two(which, carry):
+        act_three[:, space_two] += dot_nn(mid_group(which), flat_rows(w_last[which]))
         return carry
 
-    lax.fori_loop(0, SIDE, back_two, 0)
+    act_three[:, space_two] = jnp.zeros((count_rows, width), wide)
+    lax.fori_loop(0, groups, back_two, 0)
+    drop_into(act_two, 1, gain_two, bias_two, space_two)
     close_back(4)
     move_back_two = swap(4, width)
     move_back_two.start()
@@ -900,16 +918,11 @@
     if gather:
         spread.drain()
 
-    def weight_rows(ref, which, rows):
-        return ref.at[which, :, :, :, pl.ds(0, rows), :]
-
     def put(ref, which, value):
-        rows = value.shape[0] // 8
-        ref[which, :, :, :, pl.ds(0, rows), :] = value.astype(low_type).reshape(2, 2, 2, rows, width)
+        ref[which] = value.astype(low_type).reshape(ref.shape[1:])
 
     def expand_group(which, carry):
-        left = mid_wide[which].reshape(8 * line, group)[:count_rows]
-        put(w_last, which, dot_tn(left, hidden_two[...]))
+        put(w_last, which, dot_tn(mid_group(which), hidden_two[...]))
         fold_begin(which, 2)
         fold_turn(2, which - 1)
         return carry
@@ -931,44 +944,12 @@
 
     lax.fori_loop(0, SIDE, grad_two, 0)
     fold_turn(2, groups - 1)
-    piece = width // 2
-    middle_rows = 9 * width // groups
-    grain = 48
-
     def middle_row(down, carry):
-        def middle_piece(spot, inner):
-            for over in range(3):
-                left_start, right_start = (0, 0, step)[over], (step, 0, 0)[over]
-                reach = line if over == 1 else line - step
-                left = [
-                    taps_one[
-                        pl.ds(pl.multiple_of((down + row) * line + left_start, step), reach), lanes(spot, piece)
-                    ]
-                    for row in range(SIDE)
-                ]
-                right = [
-                    taps_two[(row + 1) * line + right_start : (row + 1) * line + right_start + reach, :]
-                    for row in range(SIDE)
-                ]
-                value = dot_tn(jnp.concatenate(left, axis=0), jnp.concatenate(right, axis=0))
-                start = pl.multiple_of(over * width + spot * piece, piece)
-                hidden_two[pl.ds(start, piece), :] = value.astype(low_type)
-            return inner
-
-        lax.fori_loop(0, 2, middle_piece, 0)
-        grains = 3 * width // grain
-        per_block = middle_rows // 8 // grain
-
-        def lay_out(spot, inner):
-            place_of = down * grains + spot
-            block = place_of // per_block
-            rows = pl.ds(pl.multiple_of((place_of % per_block) * grain, 16), grain)
-            mid_wide[block // 8, (block // 4) % 2, (block // 2) % 2, block % 2, rows, :] = hidden_two[
-                pl.ds(pl.multiple_of(spot * grain, 16), grain), :
-            ]
-            return inner
-
-        lax.fori_loop(0, grains, lay_out, 0, unroll=4)
+        for over in range(3):
+            left = row_windows(taps_one, down, low_start[over], reaches[over])
+            right = row_windows(taps_two, 1, high_start[over], reaches[over])
+            rows = pl.ds(pl.multiple_of((3 * down + over) * width, width), width)
+            mid_wide[rows, :] = dot_tn(left, right).astype(low_type)
         fold_begin(down, 1)
 
         @pl.when(down == 2)
@@ -982,22 +963,19 @@
     lax.fori_loop(0, 3, middle_row, 0)
 
     def back_one(index, carry):
-        kernel = flat_rows(w_middle[...])
-
-        def tap_of(down, over):
-            tap = 3 * down + 2 - over
-            return kernel[tap * width : (tap + 1) * width]
-
-        value = over_lines([shifted(taps_two, index, 2 - down) for down in range(3)], tap_of, dot_nt, 1)
-        drop_into(index, value, act_one, 0, gain_one, bias_one, space_one)
-
-        @pl.when(index % 2 == 0)
-        def _():
-            fold_turn(1, 2 + index // 2)
-
+        down, side = index // 2, index % 2
+        columns = lanes(2 + side, piece)
+        for over in range(3):
+            left = row_windows(taps_two, 2 - down, high_start[over], reaches[over])
+            start = pl.multiple_of((3 * down + over) * width + side * piece, piece)
+            value = dot_nt(left, w_middle[pl.ds(start, piece), :])
+            add_windows(act_three, columns, value, low_start[over], reaches[over])
+        when(index < 4, functools.partial(fold_turn, 1, 2 + index))
         return carry
 
-    lax.fori_loop(0, SIDE, back_one, 0)
+    act_three[:, space_one] = jnp.zeros((count_rows, width), wide)
+    lax.fori_loop(0, 6, back_one, 0)
+    drop_into(act_one, 0, gain_one, bias_one, space_one)
     close_back(5)
     move_back_one = swap(5, width)
     move_back_one.start()
@@ -1048,10 +1026,8 @@
         fold.drain()
     else:
         outs = [
-            pltpu.make_async_copy(weight_rows(ref, slice(None), rows), out, sem_local.at[slot])
-            for slot, (ref, rows, out) in enumerate(
-                zip((w_first, mid_wide, w_last), [weight.shape[-2] for weight in weights], grads_out)
-            )
+            pltpu.make_async_copy(ref, out, sem_local.at[slot])
+            for slot, (ref, out) in enumerate(zip((w_first, mid_wide.at[pl.ds(0, 9 * width), :], w_last), grads_out))
         ]
         for copy in outs:
             copy.start()
@@ -1078,9 +1054,9 @@
     spots = SPOTS + (2,)
     scratch = [
         pltpu.VMEM((count_rows, channels), low_type),
-        pltpu.VMEM(spots + (line, group), low_type),
+        pltpu.VMEM((SPOTS[0] * count_rows, group), low_type),
         pltpu.VMEM(spots + (channels // blocks, width), low_type),
-        pltpu.VMEM(spots + (middle // blocks, width), low_type),
+        pltpu.VMEM((middle, width), low_type),
         pltpu.VMEM(spots + (channels // blocks, width), low_type),
         pltpu.VMEM((count_rows, width), wide),
         pltpu.VMEM((count_rows, width), wide),
@@ -1107,13 +1083,11 @@
     if gather:
         counts = (channels // blocks, middle // blocks, channels // blocks)
         scratch += [pltpu.SemaphoreType.DMA((2, 3, 3))]
-        scratch += [pltpu.SemaphoreType.DMA((2, 4, 6)) for _ in range(2)]
-        scratch += [pltpu.SemaphoreType.DMA((2, 4, 3))]
+        scratch += [pltpu.SemaphoreType.DMA((2, 4, size)) for size in (6, 8, 6)]
         scratch += [pltpu.VMEM((4, 2, 2, rows, width), low_type) for rows in counts[1:]]
         for lead in ((4, 2), (4,), (4,)):
             scratch += [pltpu.VMEM(lead + (rows, width), low_type) for rows in counts]
-        scratch += [pltpu.SemaphoreType.DMA((2, 4, 3))]
-        scratch += [pltpu.SemaphoreType.DMA((2, 4, 6)) for _ in range(3)]
+        scratch += [pltpu.SemaphoreType.DMA((2, 4, size)) for size in (6, 8, 6, 6)]
         grads_shape = [jax.ShapeDtypeStruct((sum(counts), width), wide)]
         grads_specs = [any_space]
     else:
@@ -1557,7 +1531,8 @@
             lax.all_gather(low_master[bounds[slot] : bounds[slot + 1]], ("client", "chan"), axis=0, tiled=True)
             for slot in range(3)
         ]
-        weights = [weight.reshape(SPOTS + (2, weight.shape[0] // 32, width)) for weight in weights]
+        split = SPOTS + (2, channels // 32, width)
+        weights = [weights[0].reshape(split), weights[1], weights[2].reshape(split)]
     *grads, grad_norm, grad_head, loss_tile = client_pass(
         near, classes, features[0], labels, mask, norms[0], heads[0], weights
     )

time: 273 us -> 275 us (level)
    pallas_call x1, Pallas kernels: 89.4 us -> 92.6 us  [base_pass(): pl.pallas_call(functools.partial(base_kernel, ratios, sizes), out_shape=o...]
where the time goes in v1:
time: 275 us; the launch traced here: 273 us
  Pallas kernels  271 us (99%)
    pallas_call x1, Pallas kernels, client_pass(): pl.pallas_call(functools.partial(client_kernel, gather, images, classes),...  174 us
    pallas_call x1, Pallas kernels, base_pass(): pl.pallas_call(functools.partial(base_kernel, ratios, sizes), out_shape=o...  92.6 us

profile of v1, /device:TPU:0, one launch (start us, length us, event | category | flops | bytes accessed | tf_op | source)
XLA Modules:
  0.0 273.5 jit_solution(13113501395818809212)
XLA Ops:
  1.3 174.4 %shard_map.195 = (f32[272,512]{1,0:T(8,128)}, f32[24,128]{1,0:T(8,128)}, f32[800,128]{1,0:T(8,128)}, f32[8,128]{1,0:T(8,128)}) custom-call(bf16[3136,1024]{1,0:T(8,128)(2,1)} %bitcast.33, s32[1,64]{1,0:T(1,128)} %labels.1, s32[1]{0:T(128)S(6)} %copy.22.flag, f32[24,128]{1,0:T(8,128)} %bitcast.45, f32[800,128]{1,0:T(8,128)} %bitcast.41, f32[272,512]{1,0:T(8,128)} %bitcast.34), custom_call_target="tpu_custom_call" | custom-call | tf_op jit(solution)/shard_map/pallas_call | solution.py:1096
  175.7 92.6 %shard_map.196 = (f32[272,512]{1,0:T(8,128)}, f32[8,128]{1,0:T(8,128)}) custom-call(f32[272,512]{1,0:T(8,128)} %bitcast.35, f32[272,512]{1,0:T(8,128)} %bitcast.37, f32[272,512]{1,0:T(8,128)} %bitcast.39, f32[8,128]{1,0:T(8,128)} %get-tuple-element.25.loss_in, f32[272,512]{1,0:T(8,128)} %get-tuple-element.26.grads), custom_call_target="tpu_custom_call" | custom-call | tf_op jit(solution)/shard_map/pallas_call | solution.py:1410
  268.3 1.2 slice_bitcast_fusion
  269.4 4.0 %shard_map.197 = (f32[272,512]{1,0:T(8,128)}, f32[272,512]{1,0:T(8,128)}, bf16[272,512]{1,0:T(8,128)(2,1)}, f32[24,128]{1,0:T(8,128)}, f32[24,128]{1,0:T(8,128)}...) custom-call(f32[272,512]{1,0:T(8,128)} %bitcast.36, f32[272,512]{1,0:T(8,128)} %bitcast.38, ...), custom_call_target="tpu_custom_call" | custom-call | tf_op jit(solution)/shard_map/pallas_call | solution.py:1444

commit v2 on v1

--- a/solution.py
+++ b/solution.py
@@ -109,12 +109,14 @@
     def along_z(self, step):
         return self.at(self.others[step], self.y, self.x)
 
-    def greet(self, whole):
+    def greet(self, whole, across=False):
         barrier = pltpu.get_barrier_semaphore()
         pairs = [(self.client, 1 - self.core)]
         if whole:
             pairs += [(self.along_x(), self.core), (self.along_y(), self.core)]
             pairs += [(self.along_z(step), self.core) for step in range(3)]
+        if across:
+            pairs += [(self.along_x(), 1 - self.core)]
         for pair in pairs:
             pl.semaphore_signal(barrier, inc=1, device_id=pair, device_id_type=MESH)
         pl.semaphore_wait(barrier, len(pairs))
@@ -556,6 +558,16 @@
         if gather:
             fold.turn(slot, turn)
 
+    def fold_step(kind, slot, which):
+        if gather:
+            (fold.core_step, fold.near_step, fold.far_step)[kind](which, slot)
+
+    def fold_at(index, spot, *steps):
+        @pl.when(index == spot)
+        def _():
+            for step in steps:
+                fold_step(*step)
+
     def fold_begin(which, slot):
         if gather:
             fold.begin(which, slot)
@@ -667,6 +679,7 @@
     close_stats(0, whole_width, width)
     move = swap(0, width)
     move.start()
+    advance(1)
     move.wait()
     settle(0, width)
 
@@ -957,7 +970,8 @@
             fold_begin(3, 1)
 
         fold_turn(2, groups + down)
-        fold_turn(1, down - 1)
+        fold_at(down, 1, (0, 1, 0))
+        fold_at(down, 2, (1, 1, 0), (0, 1, 1))
         return carry
 
     lax.fori_loop(0, 3, middle_row, 0)
@@ -970,12 +984,18 @@
             start = pl.multiple_of((3 * down + over) * width + side * piece, piece)
             value = dot_nt(left, w_middle[pl.ds(start, piece), :])
             add_windows(act_three, columns, value, low_start[over], reaches[over])
-        when(index < 4, functools.partial(fold_turn, 1, 2 + index))
+        fold_at(index, 0, (0, 1, 2))
+        fold_at(index, 1, (0, 1, 3))
+        fold_at(index, 2, (1, 1, 1))
+        fold_at(index, 3, (2, 1, 0))
+        fold_at(index, 4, (1, 1, 2))
+        fold_at(index, 5, (2, 1, 1))
         return carry
 
     act_three[:, space_one] = jnp.zeros((count_rows, width), wide)
     lax.fori_loop(0, 6, back_one, 0)
     drop_into(act_one, 0, gain_one, bias_one, space_one)
+    fold_step(1, 1, 3)
     close_back(5)
     move_back_one = swap(5, width)
     move_back_one.start()
@@ -988,11 +1008,13 @@
         return carry
 
     lax.fori_loop(0, SIDE, grad_one, 0)
+    fold_step(2, 1, 2)
 
     def reduce_group(which, carry):
         put(w_first, which, dot_tn(x_all[:, lanes(which, group)], hidden_two[...]))
         fold_begin(which, 0)
         fold_turn(0, which - 1)
+        fold_at(which, 1, (2, 1, 3))
         return carry
 
     lax.fori_loop(0, groups, reduce_group, 0)
@@ -1294,6 +1316,122 @@
     return jnp.dot(left, right, precision=lax.Precision.HIGH, preferred_element_type=wide)
 
 
+class Share:
+    def __init__(self, place, sizes, buffers, sems):
+        self.place = place
+        self.sizes = sizes
+        self.fresh, self.rows_in, self.rows_out, self.back = buffers
+        self.sems = sems
+        self.bounds = [0, sizes[0], sizes[0] + sizes[1], sum(sizes)]
+        p = place
+        self.duty = jnp.where(p.x == 1, 1, 2 * p.core)
+        self.mine = p.x * 2 + p.core
+
+    def section(self, slot):
+        return pl.ds(self.bounds[slot], self.sizes[slot])
+
+    def spot(self, slot, x, core):
+        number = x if slot == 1 else x * 2 + core
+        return pl.ds(pl.multiple_of(number * self.sizes[slot], 16), self.sizes[slot])
+
+    def doer(self, slot):
+        return (0, 0) if slot == 0 else (0, 1) if slot == 2 else (1, self.place.core)
+
+    def out_copy(self, slot):
+        p = self.place
+        x, core = self.doer(slot)
+        return remote(
+            self.fresh.at[self.section(slot), :],
+            self.rows_in.at[self.spot(slot, p.x, p.core), :],
+            self.sems.at[0, slot],
+            self.sems.at[1, self.mine],
+            p.at(p.z, p.y, x),
+            core,
+        )
+
+    def in_copy(self, slot, x, core):
+        p = self.place
+        return remote(
+            self.fresh.at[self.section(slot), :],
+            self.rows_in.at[self.spot(slot, x, core), :],
+            self.sems.at[0, slot],
+            self.sems.at[1, x * 2 + core],
+            p.at(p.z, p.y, x),
+            core,
+        )
+
+    def back_copy(self, slot, x, core):
+        p = self.place
+        return remote(
+            self.rows_out.at[self.spot(slot, x, core), :],
+            self.back.at[self.section(slot), :],
+            self.sems.at[0, 3 + x * 2 + core],
+            self.sems.at[1, 4 + slot],
+            p.at(p.z, p.y, x),
+            core,
+        )
+
+    def users(self, slot):
+        p = self.place
+        if slot == 1:
+            return [(0, p.core), (1, p.core)]
+        return [(x, core) for x in (0, 1) for core in (0, 1)]
+
+    def send(self):
+        for slot in range(3):
+
+            @pl.when(self.duty != slot)
+            def _():
+                self.out_copy(slot).start()
+
+            @pl.when(self.duty == slot)
+            def _():
+                self.rows_in[self.spot(slot, self.place.x, self.place.core), :] = self.fresh[self.section(slot), :]
+
+    def gather(self):
+        p = self.place
+        for slot in range(3):
+
+            @pl.when(self.duty == slot)
+            def _():
+                for x, core in self.users(slot):
+
+                    @pl.when((p.x != x) | (p.core != core))
+                    def _():
+                        self.in_copy(slot, x, core).wait_recv()
+
+    def give_back(self):
+        p = self.place
+        for slot in range(3):
+
+            @pl.when(self.duty == slot)
+            def _():
+                for x, core in self.users(slot):
+
+                    @pl.when((p.x != x) | (p.core != core))
+                    def _():
+                        self.back_copy(slot, x, core).start()
+
+                self.back[self.section(slot), :] = self.rows_out[self.spot(slot, p.x, p.core), :]
+
+    def finish(self):
+        p = self.place
+        for slot in range(3):
+
+            @pl.when(self.duty != slot)
+            def _():
+                self.back_copy(slot, p.x, p.core).wait_recv()
+                self.out_copy(slot).wait_send()
+
+            @pl.when(self.duty == slot)
+            def _():
+                for x, core in self.users(slot):
+
+                    @pl.when((p.x != x) | (p.core != core))
+                    def _():
+                        self.back_copy(slot, x, core).wait_send()
+
+
 def base_kernel(
     ratios,
     sizes,
@@ -1315,27 +1453,25 @@
     ortho_out, loss_out = take(2)
     gram, gram_total = take(2)
     gram_boxes = take(4)
-    grams, iterate, tiles, tile_boxes = take(4)
-    gram_sems, tile_sems = take(2)
-
-    place.greet(True)
+    grams, fresh, rows_in, rows_out, back, tiles, tile_boxes = take(7)
+    gram_sems, tile_sems, share_sems = take(3)
+
+    rows_in[...] = jnp.zeros_like(rows_in)
+    place.greet(True, True)
+    fresh[...] = momentum_decay * momentum[...] + (grads[...] + prox_weight * (master[...] - anchor[...]))
+    share = Share(place, sizes, (fresh, rows_in, rows_out, back), share_sems)
+    share.send()
     tiles[0] = loss_in[...]
     tile_sum = TileSum(place, tiles, tile_boxes, tile_sems)
     extra = tile_sum.steps()
     extra.pop(0)()
 
-    bounds = [0]
-    for size in sizes:
-        bounds.append(bounds[-1] + size)
     width = master.shape[1]
     part = width // 2
     for slot in range(3):
-        rows = slice(bounds[slot], bounds[slot + 1])
-        grad = grads[rows, :] + prox_weight * (master[rows, :] - anchor[rows, :])
-        fresh = momentum_decay * momentum[rows, :] + grad
-        ortho_out[rows, :] = fresh
+        section = fresh[share.section(slot), :]
         partial = lax.dot_general(
-            fresh, fresh, (((0,), (0,)), ((), ())), precision=precise, preferred_element_type=wide
+            section, section, (((0,), (0,)), ((), ())), precision=precise, preferred_element_type=wide
         )
         start = 3 * part * slot
         gram[start : start + part, :] = partial[:part, :part]
@@ -1343,47 +1479,44 @@
         gram[start + 2 * part : start + 3 * part, :] = partial[part:, part:]
 
     gram_sum = GramSum(place, gram, gram_total, gram_boxes, gram_sems)
-
     gram_sum.run(extra)
     loss_out[...] = tile_sum.result()
 
     spots = lax.broadcasted_iota(jnp.int32, (part, part), 0)
     diagonal = spots == lax.broadcasted_iota(jnp.int32, (part, part), 1)
-    iterate[...] = jnp.zeros_like(iterate)
-    for slot in range(3):
-        start = 3 * part * slot
-        corner = gram_total[start : start + part, :]
-        side = gram_total[start + part : start + 2 * part, :]
-        end = gram_total[start + 2 * part : start + 3 * part, :]
-        trace = jnp.sum(jnp.where(diagonal, corner + end, 0.0))
-        factor = 1.0 / (jnp.sqrt(trace) + 1e-07)
-        square = factor * factor
-        grams[slot, :part, :part] = corner * square
-        grams[slot, :part, part:] = side * square
-        grams[slot, part:, :part] = side.T * square
-        grams[slot, part:, part:] = end * square
-        rows = slice(bounds[slot], bounds[slot + 1])
-        iterate[slot, : bounds[slot + 1] - bounds[slot], :] = ortho_out[rows, :] * factor
+    start = 3 * part * share.duty
+    corner = gram_total[pl.ds(pl.multiple_of(start, part), part), :]
+    side = gram_total[pl.ds(pl.multiple_of(start + part, part), part), :]
+    end = gram_total[pl.ds(pl.multiple_of(start + 2 * part, part), part), :]
+    trace = jnp.sum(jnp.where(diagonal, corner + end, 0.0))
+    factor = 1.0 / (jnp.sqrt(trace) + 1e-07)
+    square = factor * factor
+    grams[:part, :part] = corner * square
+    grams[:part, part:] = side * square
+    grams[part:, :part] = side.T * square
+    grams[part:, part:] = end * square
+    share.gather()
+    rows_in[...] = rows_in[...] * factor
 
     def turn(count, carry):
-        slot = lax.rem(count, 3)
-        current = grams[slot]
+        current = grams[...]
         mixed = schulz_second * current + schulz_third * dot_high(current, current)
-        held = iterate[slot]
-        iterate[slot] = schulz_first * held + dot_high(held, mixed)
-
-        @pl.when(count < 3 * (NS_STEPS - 1))
+        held = rows_in[...]
+        rows_in[...] = schulz_first * held + dot_high(held, mixed)
+
+        @pl.when(count < NS_STEPS - 1)
         def _():
             once = schulz_first * current + dot_high(current, mixed)
-            grams[slot] = schulz_first * once + dot_high(once, mixed)
+            grams[...] = schulz_first * once + dot_high(once, mixed)
 
         return carry
 
-    lax.fori_loop(0, 3 * NS_STEPS, turn, 0)
-    for slot in range(3):
-        ortho_out[bounds[slot] : bounds[slot + 1], :] = (
-            iterate[slot, : bounds[slot + 1] - bounds[slot], :] * ratios[slot]
-        )
+    lax.fori_loop(0, NS_STEPS, turn, 0)
+    ratio = jnp.where(share.duty == 1, ratios[1], ratios[0])
+    rows_out[...] = (rows_in[...] * ratio).astype(low_type)
+    share.give_back()
+    share.finish()
+    ortho_out[...] = back[...].astype(wide)
     gram_sum.drain()
     tile_sum.drain()
 
@@ -1397,12 +1530,16 @@
     scratch += [pltpu.VMEM((4, size, part), wide) for size in (4 * share, 2 * share, share)]
     scratch += [pltpu.VMEM((3, share, part), wide)]
     scratch += [
-        pltpu.VMEM((3, width, width), wide),
-        pltpu.VMEM((3, max(sizes), width), wide),
+        pltpu.VMEM((width, width), wide),
+        pltpu.VMEM((rows, width), wide),
+        pltpu.VMEM((max(4 * sizes[0], 2 * sizes[1]), width), wide),
+        pltpu.VMEM((max(4 * sizes[0], 2 * sizes[1]), width), low_type),
+        pltpu.VMEM((rows, width), low_type),
         pltpu.VMEM((4, 8, LANES), wide),
         pltpu.VMEM((6, 8, LANES), wide),
         pltpu.SemaphoreType.DMA((2, 8, 2, 4)),
         pltpu.SemaphoreType.DMA((2, 6)),
+        pltpu.SemaphoreType.DMA((2, 7)),
     ]
     block = jax.ShapeDtypeStruct((rows, width), wide)
     outs = [block, jax.ShapeDtypeStruct((8, LANES), wide)]

time: 275 us -> 237 us (0.86)
  Pallas kernels: 271 us -> 234 us
    pallas_call x1, Pallas kernels: 92.6 us -> 68.7 us  [base_pass(): pl.pallas_call(functools.partial(base_kernel, ratios, sizes), out_shape=o...]
    pallas_call x1, Pallas kernels: 174 us -> 162 us  [client_pass(): pl.pallas_call(functools.partial(client_kernel, gather, images, classes),...]
where the time goes in v2:
time: 237 us
  Pallas kernels  234 us (99%)
    pallas_call x1, Pallas kernels, client_pass(): pl.pallas_call(functools.partial(client_kernel, gather, images, classes),...  162 us
    pallas_call x1, Pallas kernels, base_pass(): pl.pallas_call(functools.partial(base_kernel, ratios, sizes), out_shape=o...  68.7 us

profile of v2, /device:TPU:0, one launch (start us, length us, event | category | flops | bytes accessed | tf_op | source)
XLA Modules:
  0.0 236.9 jit_solution(18294000313403329652)
XLA Ops:
  1.3 161.7 %shard_map.195 = (f32[272,512]{1,0:T(8,128)}, f32[24,128]{1,0:T(8,128)}, f32[800,128]{1,0:T(8,128)}, f32[8,128]{1,0:T(8,128)}) custom-call(bf16[3136,1024]{1,0:T(8,128)(2,1)} %bitcast.33, s32[1,64]{1,0:T(1,128)} %labels.1, s32[1]{0:T(128)S(6)} %copy.22.flag, f32[24,128]{1,0:T(8,128)} %bitcast.45, f32[800,128]{1,0:T(8,128)} %bitcast.41, f32[272,512]{1,0:T(8,128)} %bitcast.34), custom_call_target="tpu_custom_call" | custom-call | tf_op jit(solution)/shard_map/pallas_call | solution.py:1118
  163.0 68.7 %shard_map.196 = (f32[272,512]{1,0:T(8,128)}, f32[8,128]{1,0:T(8,128)}) custom-call(f32[272,512]{1,0:T(8,128)} %bitcast.35, f32[272,512]{1,0:T(8,128)} %bitcast.37, f32[272,512]{1,0:T(8,128)} %bitcast.39, f32[8,128]{1,0:T(8,128)} %get-tuple-element.25.loss_in, f32[272,512]{1,0:T(8,128)} %get-tuple-element.26.grads), custom_call_target="tpu_custom_call" | custom-call | tf_op jit(solution)/shard_map/pallas_call | solution.py:1547
  231.7 1.2 slice_bitcast_fusion
  232.9 4.0 %shard_map.197 = (f32[272,512]{1,0:T(8,128)}, f32[272,512]{1,0:T(8,128)}, bf16[272,512]{1,0:T(8,128)(2,1)}, f32[24,128]{1,0:T(8,128)}, f32[24,128]{1,0:T(8,128)}...) custom-call(f32[272,512]{1,0:T(8,128)} %bitcast.36, f32[272,512]{1,0:T(8,128)} %bitcast.38, ...), custom_call_target="tpu_custom_call" | custom-call | tf_op jit(solution)/shard_map/pallas_call | solution.py:1581

commit v3 on v2

--- a/solution.py
+++ b/solution.py
@@ -736,29 +736,28 @@
     move_two.wait()
     settle(1, width)
 
-    def hide_two(index, carry):
+    arrive(2, 0)
+
+    def third_line(index, carry):
         value = normal(act_two, 1, index) * gain_two + bias_two
-        hidden_two[tile(index), :] = (value * sigmoid(value)).astype(low_type)
+        hidden = (value * sigmoid(value)).astype(low_type)
+        hidden_two[tile(index), :] = hidden
+        value = dot_nt(hidden, flat_rows(w_last[...]))
+        act_three[tile(index), :] = value
+        start = jnp.where(index == 0, column_sum(value[0:8]) / 8.0, shift[0:1, :])
+        gap = value - start
+        kept_sums = jnp.where(index == 0, 0.0, shift[8:24, :])
+        shift[0:1, :] = start
+        shift[8:16, :] = kept_sums[0:8] + fold_rows(gap)
+        shift[16:24, :] = kept_sums[8:16] + fold_rows(gap * gap)
         return carry
 
-    lax.fori_loop(0, SIDE, hide_two, 0)
-
-    arrive(2, 0)
-
-    def third_group(which, carry):
-        columns = lanes(which, group)
-        act_three[:, columns] = dot_nt(hidden_two[...], flat_rows(w_last[which]))
-        look_over(act_three, columns)
-        close_stats(2, columns, group)
-        return carry
-
-    lax.fori_loop(0, groups, third_group, 0)
+    lax.fori_loop(0, SIDE, third_line, 0)
+    close_stats(2, pl.ds(0, channels), channels)
     move_three = swap(2, channels)
     move_three.start()
     move_three.wait()
     settle(2, channels)
-    fwd_stats[2, 2:3, :] = gain_three
-    fwd_stats[2, 3:4, :] = bias_three
 
     per_group = group // LANES
 
@@ -774,31 +773,33 @@
         starts = range(kind * kept, (kind + 1) * kept, mine_images)
         return jnp.concatenate([stage[start : start + mine_images, :] for start in starts], axis=1)
 
+    fwd_stats[2, 4:5, :] = fwd_stats[2, 1:2, :] * gain_three
+    fwd_stats[2, 5:6, :] = bias_three - fwd_stats[2, 0:1, :] * fwd_stats[2, 4:5, :]
+
     def emit(index, carry):
         columns = lanes(index, LANES)
-        mean, scale = fwd_stats[2, 0:1, columns], fwd_stats[2, 1:2, columns]
-        gain, bias = fwd_stats[2, 2:3, columns], fwd_stats[2, 3:4, columns]
+        slant, level = fwd_stats[2, 4:5, columns], fwd_stats[2, 5:6, columns]
 
         def pixels(row, sums):
-            pooled, slopes, slopes_normed = sums
+            pooled, steeps, steeps_act = sums
             found = []
             for spot in range(SIDE):
                 where = block_of(row * SIDE + spot)
-                normed = (act_three[where, columns] - mean) * scale
-                total = normed * gain + bias + x_all[where, columns].astype(wide)
-                sig = sigmoid(total)
-                out = total * sig
-                slope = sig + out * (1.0 - sig)
-                found.append(slope.astype(low_type))
-                pooled, slopes, slopes_normed = pooled + out, slopes + slope, slopes_normed + slope * normed
+                act = act_three[where, columns]
+                half_total = 0.5 * (act * slant + level + x_all[where, columns].astype(wide))
+                rise = 1.0 + jnp.tanh(half_total)
+                out = half_total * rise
+                steep = rise + out * (2.0 - rise)
+                found.append(steep.astype(low_type))
+                pooled, steeps, steeps_act = pooled + out, steeps + steep, steeps_act + steep * act
             mid_wide[mid_line(index // per_group, row), lanes(index % per_group, LANES)] = jnp.concatenate(
                 found, axis=0
             )
-            return pooled, slopes, slopes_normed
+            return pooled, steeps, steeps_act
 
         zero = jnp.zeros((mine_images, LANES), wide)
-        pooled, slopes, slopes_normed = lax.fori_loop(0, SIDE, pixels, (zero, zero, zero))
-        for kind, value in enumerate((pooled, slopes, slopes_normed)):
+        sums = lax.fori_loop(0, SIDE, pixels, (zero, zero, zero))
+        for kind, value in enumerate(sums):
             stage[pl.ds(pl.multiple_of(kind * kept + index * mine_images, mine_images), mine_images), :] = value
         return carry
 
@@ -820,7 +821,7 @@
     tile_spots = lax.broadcasted_iota(jnp.int32, loss_out.shape, 1)
     loss_out[...] = jnp.where(tile_spots == 0, taking * jnp.sum(each_loss), taking * mine_images)
     grads = (taking / images * (powers / power_sum - onehot)).astype(low_type)
-    grad_pool[...] = dot_tn(grads, head_full) / PIXELS
+    grad_pool[...] = dot_tn(grads, head_full) * (0.5 / PIXELS)
     logit_grads[core] = grads
     pool_all[core] = pooled[:, 0:half]
     pool_send[...] = pooled[:, half:]
@@ -835,8 +836,10 @@
         remote(logit_grads.at[core], logit_grads.at[core], sem_misc.at[0, 4], sem_misc.at[1, 4], *mate),
     ]
 
-    sums_mine[3, 0:1, :] = column_sum(grad_pool[...] * gathered(1))
-    sums_mine[3, 1:2, :] = column_sum(grad_pool[...] * gathered(2))
+    steeps = gathered(1)
+    steeps_normed = (gathered(2) - fwd_stats[2, 0:1, :] * steeps) * fwd_stats[2, 1:2, :]
+    sums_mine[3, 0:1, :] = column_sum(grad_pool[...] * steeps)
+    sums_mine[3, 1:2, :] = column_sum(grad_pool[...] * steeps_normed)
     move_back = swap(3, channels)
     move_back.start()
     for copy in head_moves:
@@ -855,31 +858,20 @@
         )
 
     first, second, third = back_terms(3, 2, channels, gain_three)
-    fwd_stats[2, 4:5, :] = first
-    fwd_stats[2, 5:6, :] = second
-    fwd_stats[2, 6:7, :] = third
-
-    def pull(index, carry):
-        columns = lanes(index, LANES)
-        mean = fwd_stats[2, 0:1, columns]
-        first, second = fwd_stats[2, 4:5, columns], fwd_stats[2, 5:6, columns]
-        third = fwd_stats[2, 6:7, columns]
-        reach = grad_pool[:, columns] * first
-
-        def pixels(row, inner):
-            where = (mid_line(index // per_group, row), lanes(index % per_group, LANES))
-            slopes = mid_wide[where].astype(wide)
-            found = []
-            for spot in range(SIDE):
-                slope = slopes[spot * mine_images : (spot + 1) * mine_images]
-                gap = act_three[block_of(row * SIDE + spot), columns] - mean
-                found.append((reach * slope - second - third * gap).astype(low_type))
-            mid_wide[where] = jnp.concatenate(found, axis=0)
-            return inner
-
-        return lax.fori_loop(0, SIDE, pixels, carry)
-
-    lax.fori_loop(0, channels // LANES, pull, 0)
+    fwd_stats[2, 4:5, :] = second - third * fwd_stats[2, 0:1, :]
+    fwd_stats[2, 5:6, :] = third
+    grad_pool[...] = grad_pool[...] * first
+
+    def pull(index):
+        for which in range(groups):
+            columns = slice(which * group, (which + 1) * group)
+            reach = grad_pool[:, columns]
+            steep = mid_wide[mid_line(which, index), :].astype(wide)
+            value = jnp.concatenate([reach] * SIDE, axis=0) * steep
+            value = value - fwd_stats[2, 4:5, columns] - fwd_stats[2, 5:6, columns] * act_three[tile(index), columns]
+            mid_wide[mid_line(which, index), :] = value.astype(low_type)
+
+    pull(0)
     for copy in head_moves:
         copy.wait_recv()
     head_grad = dot_nn(logit_grads[0], pool_all[0]) + dot_nn(logit_grads[1], pool_all[1])
@@ -917,13 +909,26 @@
     def mid_group(which):
         return mid_wide[pl.ds(pl.multiple_of(which * count_rows, count_rows), count_rows), :]
 
-    def back_two(which, carry):
-        act_three[:, space_two] += dot_nn(mid_group(which), flat_rows(w_last[which]))
+    def back_two(index):
+        left = jnp.concatenate([mid_wide[mid_line(which, index), :] for which in range(groups)], axis=1)
+        value = dot_nn(left, flat_rows(w_last[...]))
+        normed = normal(act_two, 1, index)
+        norm = normed * gain_two + bias_two
+        sig = sigmoid(norm)
+        grad = value * (sig + norm * sig * (1.0 - sig))
+        act_three[tile(index), space_two] = grad
+        size = pl.ds(0, width)
+        shift[8:16, size] += fold_rows(grad)
+        shift[16:24, size] += fold_rows(grad * normed)
+
+    def back_two_line(index, carry):
+        pull(index + 1)
+        back_two(index)
         return carry
 
-    act_three[:, space_two] = jnp.zeros((count_rows, width), wide)
-    lax.fori_loop(0, groups, back_two, 0)
-    drop_into(act_two, 1, gain_two, bias_two, space_two)
+    shift[8:24, :] = jnp.zeros((16, channels), wide)
+    lax.fori_loop(0, SIDE - 1, back_two_line, 0)
+    back_two(SIDE - 1)
     close_back(4)
     move_back_two = swap(4, width)
     move_back_two.start()
@@ -1095,7 +1100,7 @@
         pltpu.VMEM((2, head_rows, mine_images), low_type),
         pltpu.VMEM((6, 8, channels), wide),
         pltpu.VMEM((6, 8, channels), wide),
-        pltpu.VMEM((24, max(width, group)), wide),
+        pltpu.VMEM((24, channels), wide),
         pltpu.VMEM((3, 8, channels), wide),
         pltpu.SemaphoreType.DMA((11,)),
         pltpu.SemaphoreType.DMA((2, 6)),
@@ -1551,13 +1556,16 @@
         out_specs=[vmem] * len(outs),
         scratch_shapes=scratch,
         compiler_params=pltpu.CompilerParams(
-            collective_id=1, has_side_effects=True, vmem_limit_bytes=VMEM_BYTES
+            collective_id=1, has_side_effects=True, vmem_limit_bytes=VMEM_BYTES // 2
         ),
     )(*operands)
 
 
-def update_kernel(master, momentum, anchor, grads, ortho, *rest):
+def update_kernel(loss_tile, master, momentum, anchor, grads, ortho, *rest):
     norms, grad_norm, heads, grad_head, outs = rest[0:3], rest[3], rest[4:7], rest[7], rest[8:]
+    loss_out, *outs = outs
+    loss_out[0] = loss_tile[0, 0]
+    loss_out[1] = loss_tile[0, 1]
     momentum_out, base_out, low_out = outs[0:3]
     held = master[...]
     momentum_out[...] = momentum_decay * momentum[...] + (grads[...] + prox_weight * (held - anchor[...]))
@@ -1573,17 +1581,18 @@
             target[...] = value
 
 
-def update_pass(master, momentum, anchor, grads, ortho, norms, grad_norm, heads, grad_head):
+def update_pass(loss_tile, master, momentum, anchor, grads, ortho, norms, grad_norm, heads, grad_head):
     vmem = pl.BlockSpec(memory_space=pltpu.VMEM)
-    operands = [master, momentum, anchor, grads, ortho, *norms, grad_norm, *heads, grad_head]
-    outs = [master.shape, master.shape, master.shape] + [grad_norm.shape] * 3 + [grad_head.shape] * 3
-    types = [wide, wide, low_type] + [wide] * 6
+    smem = pl.BlockSpec(memory_space=pltpu.SMEM)
+    operands = [loss_tile, master, momentum, anchor, grads, ortho, *norms, grad_norm, *heads, grad_head]
+    outs = [(2,), master.shape, master.shape, master.shape] + [grad_norm.shape] * 3 + [grad_head.shape] * 3
+    types = [wide, wide, wide, low_type] + [wide] * 6
     return pl.pallas_call(
         update_kernel,
         out_shape=[jax.ShapeDtypeStruct(shape, kind) for shape, kind in zip(outs, types)],
-        in_specs=[vmem] * len(operands),
-        out_specs=[vmem] * len(outs),
-        compiler_params=pltpu.CompilerParams(vmem_limit_bytes=VMEM_BYTES),
+        in_specs=[smem] + [vmem] * (len(operands) - 1),
+        out_specs=[smem] + [vmem] * (len(outs) - 1),
+        compiler_params=pltpu.CompilerParams(vmem_limit_bytes=VMEM_BYTES // 4),
     )(*operands)
 
 
@@ -1678,13 +1687,13 @@
         ortho, loss_tile = base_pass(ratios, sizes, master, momentum, anchor, loss_tile, grad_base)
     else:
         grad_base, ortho, loss_tile = base_far(ratios, bounds, master, momentum, anchor, loss_tile, grads)
-    momentum_new, base_new, base_low, *fresh = update_pass(
-        master, momentum, anchor, grad_base, ortho, norms, grad_norm, heads, grad_head
+    loss, momentum_new, base_new, base_low, *fresh = update_pass(
+        loss_tile, master, momentum, anchor, grad_base, ortho, norms, grad_norm, heads, grad_head
     )
     fresh_norms = [as_stored(value, norm_params.shape) for value in fresh[:3]]
     fresh_heads = [jnp.transpose(as_stored(value, (classes, 1, half)), (1, 2, 0)) for value in fresh[3:]]
     return (
-        loss_tile[0, 0:2],
+        loss,
         base_new[None],
         momentum_new[None],
         base_low[None],

time: 237 us -> 236 us (level)
  Pallas kernels: 234 us -> 227 us
  local copies, waits for them, and re-layouts: 1.18 us -> 6.46 us
    unnamed x0 -> x26, local copies, waits for them, and re-layouts: none -> 6.46 us
    pallas_call x1, Pallas kernels: 162 us -> 158 us  [client_pass(): pl.pallas_call(functools.partial(client_kernel, gather, images, classes),...]
where the time goes in v3:
time: 236 us; the launch traced here: 235 us
  Pallas kernels  227 us (96%)
  local copies, waits for them, and re-layouts  6.46 us (3%)
    pallas_call x1, Pallas kernels, client_pass(): pl.pallas_call(functools.partial(client_kernel, gather, images, classes),...  158 us
    pallas_call x1, Pallas kernels, base_pass(): pl.pallas_call(functools.partial(base_kernel, ratios, sizes), out_shape=o...  66.3 us
    unnamed x26, local copies, waits for them, and re-layouts  6.46 us

profile of v3, /device:TPU:0, one launch (start us, length us, event | category | flops | bytes accessed | tf_op | source)
XLA Modules:
  0.0 234.9 jit_solution(4690983217441046153)
XLA Ops:
  0.6 0.0 copy-start.10
  0.7 0.0 copy-start.9
  0.7 0.0 copy-start.8
  0.7 0.0 copy-start.2
  0.7 0.0 copy-start.1
  0.7 0.0 copy-start
  1.5 157.9 %shard_map.195 = (f32[272,512]{1,0:T(8,128)}, f32[24,128]{1,0:T(8,128)}, f32[800,128]{1,0:T(8,128)}, f32[8,128]{1,0:T(8,128)}) custom-call(bf16[3136,1024]{1,0:T(8,128)(2,1)} %bitcast.46, s32[1,64]{1,0:T(1,128)} %labels.1, s32[1]{0:T(128)S(6)} %copy.22.flag, f32[24,128]{1,0:T(8,128)} %bitcast.42, f32[800,128]{1,0:T(8,128)} %bitcast.38, f32[272,512]{1,0:T(8,128)} %bitcast.31), custom_call_target="tpu_custom_call" | custom-call | tf_op jit(solution)/shard_map/pallas_call | solution.py:1123
  159.4 0.0 copy-done.2
  159.4 0.0 copy-done.1
  159.4 0.0 copy-done
  159.4 0.0 copy-start.3
  159.4 1.0 copy-done.3
  160.5 0.0 copy-start.12
  160.5 0.7 copy-done.12
  161.2 66.3 %shard_map.196 = (f32[272,512]{1,0:T(8,128)S(1)}, f32[8,128]{1,0:T(8,128)S(1)}) custom-call(f32[272,512]{1,0:T(8,128)S(1)} %bitcast.32, f32[272,512]{1,0:T(8,128)S(1)} %bitcast.34, f32[272,512]{1,0:T(8,128)S(1)} %bitcast.36, f32[8,128]{1,0:T(8,128)S(1)} %copy-done.12, f32[272,512]{1,0:T(8,128)S(1)} %copy-done.3), custom_call_target="tpu_custom_call" | custom-call | tf_op jit(solution)/shard_map/pallas_call | solution.py:1552
  227.5 0.0 copy-done.10
  227.5 0.0 copy-done.9
  227.5 0.0 copy-done.8
  227.5 0.0 copy-start.4
  227.6 1.0 copy-done.4
  228.6 0.0 copy-start.5
  228.6 1.0 copy-done.5
  229.6 0.0 copy-start.6
  229.6 1.0 copy-done.6
  230.6 0.0 copy-start.7
  230.6 1.0 copy-done.7
  231.6 0.0 copy-start.11
  231.6 0.7 copy-done.11
  232.3 2.5 %shard_map.197 = (f32[2]{0:T(128)}, f32[272,512]{1,0:T(8,128)}, f32[272,512]{1,0:T(8,128)}, bf16[272,512]{1,0:T(8,128)(2,1)}, f32[24,128]{1,0:T(8,128)}, /*index...) custom-call(f32[8,128]{1,0:T(8,128)S(1)} %get-tuple-element.28.loss_tile, ...), custom_call_target="tpu_custom_call" | custom-call | tf_op jit(solution)/shard_map/pallas_call | solution.py:1590
Async XLA Ops:
  0.6 226.9 %copy-start.10 = (f32[1,2,1,1536]{3,2,1,0:T(1,128)S(1)}, f32[1,2,1,1536]{3,2,1,0:T(1,128)}, u32[]{:S(2)}) copy-start(f32[1,2,1,1536]{3,2,1,0:T(1,128)} %param.20) | copy-start | bytes 36868
  0.7 226.9 %copy-start.9 = (f32[1,2,1,1536]{3,2,1,0:T(1,128)S(1)}, f32[1,2,1,1536]{3,2,1,0:T(1,128)}, u32[]{:S(2)}) copy-start(f32[1,2,1,1536]{3,2,1,0:T(1,128)} %param.19) | copy-start | bytes 36868
  0.7 226.9 %copy-start.8 = (f32[1,2,1,1536]{3,2,1,0:T(1,128)S(1)}, f32[1,2,1,1536]{3,2,1,0:T(1,128)}, u32[]{:S(2)}) copy-start(f32[1,2,1,1536]{3,2,1,0:T(1,128)} %param.18) | copy-start | bytes 36868
  0.7 158.7 %copy-start.2 = (f32[1,272,512]{2,1,0:T(8,128)S(1)}, f32[1,272,512]{2,1,0:T(8,128)}, u32[]{:S(2)}) copy-start(f32[1,272,512]{2,1,0:T(8,128)} %param.17) | copy-start | bytes 1671172
  0.7 158.7 %copy-start.1 = (f32[1,272,512]{2,1,0:T(8,128)S(1)}, f32[1,272,512]{2,1,0:T(8,128)}, u32[]{:S(2)}) copy-start(f32[1,272,512]{2,1,0:T(8,128)} %param.16) | copy-start | bytes 1671172
  0.7 158.7 %copy-start = (f32[1,272,512]{2,1,0:T(8,128)S(1)}, f32[1,272,512]{2,1,0:T(8,128)}, u32[]{:S(2)}) copy-start(f32[1,272,512]{2,1,0:T(8,128)} %param.15) | copy-start | bytes 1671172
  159.4 1.1 copy-start.3
  160.5 0.7 copy-start.12
  227.5 1.0 copy-start.4
  228.6 1.0 copy-start.5
  229.6 1.0 copy-start.6
  230.6 1.0 copy-start.7
  231.6 0.7 copy-start.11

commit v4 on v3

--- a/solution.py
+++ b/solution.py
@@ -1152,127 +1152,72 @@
         self.place = place
         self.data = data
         self.total = total
-        self.core_box, self.near_box, self.far_box, self.z_box = boxes
+        self.y_box, self.z_box = boxes
         self.sems = sems
-        self.copies = []
-        self.sizes = (data.shape[0] // 72 * 40 // 32, data.shape[0] // 72 * 32 // 32)
-
-    def rows(self, kind, core, z=None, first=None, second=None):
-        size = self.sizes[kind]
-        start = core * (16 * (self.sizes[0] + self.sizes[1])) + kind * 16 * self.sizes[0]
-        count = 16 * size
-        for number, spot, parts in ((4 * size, z, 4), (2 * size, first, 2), (size, second, 2)):
-            if spot is None:
-                break
-            start, count = start + spot * number, number
-        return pl.ds(pl.multiple_of(start, 8), count)
-
-    def ways(self, kind):
-        p = self.place
-        x_way, y_way = (p.x, p.along_x()), (p.y, p.along_y())
-        return (x_way, y_way) if kind == 0 else (y_way, x_way)
-
-    def copy(self, phase, kind, turn, src, dst, client, core):
+        self.share = data.shape[0] // 8
+        self.down_order = place.others[::-1] + [place.z]
+
+    def rows(self, z, y):
+        return pl.ds(pl.multiple_of((z * 2 + y) * self.share, 8), self.share)
+
+    def copy(self, number, src, dst, to):
         sems = self.sems
-        return remote(
-            src, dst, sems.at[0, phase, kind, turn], sems.at[1, phase, kind, turn], client, core
-        )
-
-    def launch(self, copy):
-        copy.start()
-        self.copies.append(copy)
-
-    def down(self, phase, kind, turn):
-        p = self.place
-        z = (p.others[::-1] + [p.z])[turn]
-        (first, first_to), (second, second_to) = self.ways(kind)
-        base = self.sizes[0] * kind
-        if phase == 0:
-            src = self.data.at[self.rows(kind, 1 - p.core, z), :]
-            box = self.core_box.at[turn, pl.ds(4 * base, 4 * self.sizes[kind]), :]
-            return self.copy(0, kind, turn, src, box, p.client, 1 - p.core)
-        if phase == 1:
-            src = self.data.at[self.rows(kind, p.core, z, 1 - first), :]
-            box = self.near_box.at[turn, pl.ds(2 * base, 2 * self.sizes[kind]), :]
-            return self.copy(1, kind, turn, src, box, first_to, p.core)
-        if phase == 2:
-            src = self.data.at[self.rows(kind, p.core, z, first, 1 - second), :]
-            box = self.far_box.at[turn, pl.ds(base, self.sizes[kind]), :]
-            return self.copy(2, kind, turn, src, box, second_to, p.core)
-        src = self.data.at[self.rows(kind, p.core, z, first, second), :]
-        box = self.z_box.at[turn, pl.ds(base, self.sizes[kind]), :]
-        return self.copy(3, kind, turn, src, box, p.along_z(2 - turn), p.core)
-
-    def down_step(self, phase, kind, turn):
-        p = self.place
-        z = (p.others[::-1] + [p.z])[turn]
-        (first, _), (second, _) = self.ways(kind)
-        self.down(phase, kind, turn).wait_recv()
-        spots = (z, first, second)[: phase + 1]
-        where = self.rows(kind, p.core, *spots)
-        scale = (4, 2, 1)[phase]
-        box = (self.core_box, self.near_box, self.far_box)[phase]
-        self.data[where, :] += box[turn, pl.ds(scale * self.sizes[0] * kind, scale * self.sizes[kind]), :]
-        if phase < 2 or turn < 3:
-            self.launch(self.down(phase + 1, kind, turn))
-
-    def up(self, phase, kind, turn):
-        p = self.place
-        z = ([p.z] + p.others)[turn]
-        (first, first_to), (second, second_to) = self.ways(kind)
-        if phase == 0:
-            ref, to = self.total.at[self.rows(kind, p.core, p.z, first, second), :], p.along_z(turn)
-        elif phase == 1:
-            ref, to = self.total.at[self.rows(kind, p.core, z, first, second), :], second_to
-        elif phase == 2:
-            ref, to = self.total.at[self.rows(kind, p.core, z, first), :], first_to
-        else:
-            ref, to = self.total.at[self.rows(kind, p.core, z), :], p.client
-        return self.copy(4 + phase, kind, turn, ref, ref, to, 1 - p.core if phase == 3 else p.core)
+        return remote(src, dst, sems.at[0, number], sems.at[1, number], to, self.place.core)
+
+    def y_down(self, turn):
+        p = self.place
+        src = self.data.at[self.rows(self.down_order[turn], 1 - p.y), :]
+        return self.copy(turn, src, self.y_box.at[turn], p.along_y())
+
+    def z_down(self, step):
+        p = self.place
+        src = self.data.at[self.rows(p.others[step], p.y), :]
+        return self.copy(4 + step, src, self.z_box.at[step], p.along_z(step))
+
+    def z_up(self, step):
+        p = self.place
+        ref = self.total.at[self.rows(p.z, p.y), :]
+        return self.copy(7 + step, ref, ref, p.along_z(step))
+
+    def y_up(self, turn):
+        p = self.place
+        ref = self.total.at[self.rows(([p.z] + p.others)[turn], p.y), :]
+        return self.copy(10 + turn, ref, ref, p.along_y())
 
     def run(self, extra):
         extra = list(extra)
-        kinds = (0, 1)
+        p = self.place
         for turn in range(4):
-            for kind in kinds:
-                self.launch(self.down(0, kind, turn))
-        for turn in range(6):
+            self.y_down(turn).start()
+        for turn in range(4):
+            self.y_down(turn).wait_recv()
+            self.data[self.rows(self.down_order[turn], p.y), :] += self.y_box[turn]
+            if turn < 3:
+                self.z_down(2 - turn).start()
             if extra:
                 extra.pop(0)()
-            for kind in kinds:
-                for phase in range(3):
-                    if 0 <= turn - phase < 4:
-                        self.down_step(phase, kind, turn - phase)
-        p = self.place
-        for kind in kinds:
-            (first, _), (second, _) = self.ways(kind)
-            where = self.rows(kind, p.core, p.z, first, second)
-            value = self.data[where, :]
-            for turn in range(3):
-                self.down(3, kind, turn).wait_recv()
-                value += self.z_box[turn, pl.ds(self.sizes[0] * kind, self.sizes[kind]), :]
-            self.total[where, :] = value
-            self.launch(self.up(1, kind, 0))
-            for turn in range(3):
-                self.launch(self.up(0, kind, turn))
-        for turn in range(6):
-            for kind in kinds:
-                if 1 <= turn < 4:
-                    self.up(0, kind, turn - 1).wait_recv()
-                    self.launch(self.up(1, kind, turn))
-                if 1 <= turn < 5:
-                    self.up(1, kind, turn - 1).wait_recv()
-                    self.launch(self.up(2, kind, turn - 1))
-                if 2 <= turn:
-                    self.up(2, kind, turn - 2).wait_recv()
-                    self.launch(self.up(3, kind, turn - 2))
+        mine = self.rows(p.z, p.y)
+        value = self.data[mine, :]
+        for step in (2, 1, 0):
+            self.z_down(step).wait_recv()
+            value += self.z_box[step]
+        self.total[mine, :] = value
+        for step in range(3):
+            self.z_up(step).start()
+        self.y_up(0).start()
+        for step in range(3):
+            self.z_up(step).wait_recv()
+            self.y_up(1 + step).start()
         for turn in range(4):
-            for kind in kinds:
-                self.up(3, kind, turn).wait_recv()
+            self.y_up(turn).wait_recv()
 
     def drain(self):
-        for copy in self.copies:
-            copy.wait_send()
+        for turn in range(4):
+            self.y_down(turn).wait_send()
+            self.y_up(turn).wait_send()
+        for step in range(3):
+            self.z_down(step).wait_send()
+            self.z_up(step).wait_send()
 
 
 class TileSum:
@@ -1457,7 +1402,8 @@
 
     ortho_out, loss_out = take(2)
     gram, gram_total = take(2)
-    gram_boxes = take(4)
+    gram_boxes = take(2)
+    (mate_gram,) = take(1)
     grams, fresh, rows_in, rows_out, back, tiles, tile_boxes = take(7)
     gram_sems, tile_sems, share_sems = take(3)
 
@@ -1473,15 +1419,21 @@
 
     width = master.shape[1]
     part = width // 2
-    for slot in range(3):
-        section = fresh[share.section(slot), :]
-        partial = lax.dot_general(
-            section, section, (((0,), (0,)), ((), ())), precision=precise, preferred_element_type=wide
-        )
-        start = 3 * part * slot
-        gram[start : start + part, :] = partial[:part, :part]
-        gram[start + part : start + 2 * part, :] = partial[:part, part:]
-        gram[start + 2 * part : start + 3 * part, :] = partial[part:, part:]
+    share.gather()
+    held = rows_in[...]
+    partial = lax.dot_general(
+        held, held, (((0,), (0,)), ((), ())), precision=precise, preferred_element_type=wide
+    )
+    gram[0:part, :] = partial[:part, :part]
+    gram[part : 2 * part, :] = partial[:part, part:]
+    gram[2 * part :, :] = partial[part:, part:]
+
+    @pl.when(place.x == 1)
+    def _():
+        swap = remote(gram, mate_gram, share_sems.at[0, 7], share_sems.at[1, 7], place.client, 1 - place.core)
+        swap.start()
+        swap.wait()
+        gram[...] += mate_gram[...]
 
     gram_sum = GramSum(place, gram, gram_total, gram_boxes, gram_sems)
     gram_sum.run(extra)
@@ -1489,10 +1441,7 @@
 
     spots = lax.broadcasted_iota(jnp.int32, (part, part), 0)
     diagonal = spots == lax.broadcasted_iota(jnp.int32, (part, part), 1)
-    start = 3 * part * share.duty
-    corner = gram_total[pl.ds(pl.multiple_of(start, part), part), :]
-    side = gram_total[pl.ds(pl.multiple_of(start + part, part), part), :]
-    end = gram_total[pl.ds(pl.multiple_of(start + 2 * part, part), part), :]
+    corner, side, end = [gram_total[start * part : (start + 1) * part, :] for start in range(3)]
     trace = jnp.sum(jnp.where(diagonal, corner + end, 0.0))
     factor = 1.0 / (jnp.sqrt(trace) + 1e-07)
     square = factor * factor
@@ -1500,7 +1449,6 @@
     grams[:part, part:] = side * square
     grams[part:, :part] = side.T * square
     grams[part:, part:] = end * square
-    share.gather()
     rows_in[...] = rows_in[...] * factor
 
     def turn(count, carry):
@@ -1530,10 +1478,9 @@
     rows, width = master.shape
     part = width // 2
     vmem = pl.BlockSpec(memory_space=pltpu.VMEM)
-    share = 9 * part // 32
-    scratch = [pltpu.VMEM((9 * part, part), wide)] * 2
-    scratch += [pltpu.VMEM((4, size, part), wide) for size in (4 * share, 2 * share, share)]
-    scratch += [pltpu.VMEM((3, share, part), wide)]
+    scratch = [pltpu.VMEM((3 * part, part), wide)] * 2
+    scratch += [pltpu.VMEM((count, 3 * part // 8, part), wide) for count in (4, 3)]
+    scratch += [pltpu.VMEM((3 * part, part), wide)]
     scratch += [
         pltpu.VMEM((width, width), wide),
         pltpu.VMEM((rows, width), wide),
@@ -1542,9 +1489,9 @@
         pltpu.VMEM((rows, width), low_type),
         pltpu.VMEM((4, 8, LANES), wide),
         pltpu.VMEM((6, 8, LANES), wide),
-        pltpu.SemaphoreType.DMA((2, 8, 2, 4)),
+        pltpu.SemaphoreType.DMA((2, 14)),
         pltpu.SemaphoreType.DMA((2, 6)),
-        pltpu.SemaphoreType.DMA((2, 7)),
+        pltpu.SemaphoreType.DMA((2, 8)),
     ]
     block = jax.ShapeDtypeStruct((rows, width), wide)
     outs = [block, jax.ShapeDtypeStruct((8, LANES), wide)]
@@ -1556,7 +1503,7 @@
         out_specs=[vmem] * len(outs),
         scratch_shapes=scratch,
         compiler_params=pltpu.CompilerParams(
-            collective_id=1, has_side_effects=True, vmem_limit_bytes=VMEM_BYTES // 2
+            collective_id=1, has_side_effects=True, vmem_limit_bytes=VMEM_BYTES
         ),
     )(*operands)
 
@@ -1592,7 +1539,7 @@
         out_shape=[jax.ShapeDtypeStruct(shape, kind) for shape, kind in zip(outs, types)],
         in_specs=[smem] + [vmem] * (len(operands) - 1),
         out_specs=[smem] + [vmem] * (len(outs) - 1),
-        compiler_params=pltpu.CompilerParams(vmem_limit_bytes=VMEM_BYTES // 4),
+        compiler_params=pltpu.CompilerParams(vmem_limit_bytes=VMEM_BYTES),
     )(*operands)
 
 

time: 236 us -> 231 us (0.979)
  local copies, waits for them, and re-layouts: 6.46 us -> 0 us
  Pallas kernels: 227 us -> 230 us
    unnamed x26 -> x0, local copies, waits for them, and re-layouts: 6.46 us -> none
where the time goes in v4:
time: 231 us
  Pallas kernels  230 us (100%)
    pallas_call x1, Pallas kernels, client_pass(): pl.pallas_call(functools.partial(client_kernel, gather, images, classes),...  158 us
    pallas_call x1, Pallas kernels, base_pass(): pl.pallas_call(functools.partial(base_kernel, ratios, sizes), out_shape=o...  67.8 us

profile of v4, /device:TPU:0, one launch (start us, length us, event | category | flops | bytes accessed | tf_op | source)
XLA Modules:
  0.0 231.1 jit_solution(15197394268975332246)
XLA Ops:
  1.3 157.9 %shard_map.195 = (f32[272,512]{1,0:T(8,128)}, f32[24,128]{1,0:T(8,128)}, f32[800,128]{1,0:T(8,128)}, f32[8,128]{1,0:T(8,128)}) custom-call(bf16[3136,1024]{1,0:T(8,128)(2,1)} %bitcast.31, s32[1,64]{1,0:T(1,128)} %labels.1, s32[1]{0:T(128)S(6)} %copy.22.flag, f32[24,128]{1,0:T(8,128)} %bitcast.43, f32[800,128]{1,0:T(8,128)} %bitcast.39, f32[272,512]{1,0:T(8,128)} %bitcast.32), custom_call_target="tpu_custom_call" | custom-call | tf_op jit(solution)/shard_map/pallas_call | solution.py:1123
  159.2 67.8 %shard_map.196 = (f32[272,512]{1,0:T(8,128)}, f32[8,128]{1,0:T(8,128)}) custom-call(f32[272,512]{1,0:T(8,128)} %bitcast.33, f32[272,512]{1,0:T(8,128)} %bitcast.35, f32[272,512]{1,0:T(8,128)} %bitcast.37, f32[8,128]{1,0:T(8,128)} %get-tuple-element.26.loss_in, f32[272,512]{1,0:T(8,128)} %get-tuple-element.27.grads), custom_call_target="tpu_custom_call" | custom-call | tf_op jit(solution)/shard_map/pallas_call | solution.py:1499
  227.0 3.9 %shard_map.197 = (f32[2]{0:T(128)}, f32[272,512]{1,0:T(8,128)}, f32[272,512]{1,0:T(8,128)}, bf16[272,512]{1,0:T(8,128)(2,1)}, f32[24,128]{1,0:T(8,128)}, /*index...) custom-call(f32[8,128]{1,0:T(8,128)} %get-tuple-element.28.loss_tile, ...), custom_call_target="tpu_custom_call" | custom-call | tf_op jit(solution)/shard_map/pallas_call | solution.py:1537

commit v5 on v4

--- a/solution.py
+++ b/solution.py
@@ -34,15 +34,8 @@
 PIXELS = SIDE * SIDE
 LANES = 128
 SPOTS = (4, 2, 2)
+CUTS = 4
 VMEM_BYTES = 62 * 2**20
-
-
-def when(condition, call):
-    if isinstance(condition, bool):
-        if condition:
-            call()
-    else:
-        pl.when(condition)(call)
 
 
 def dot_nn(left, right):
@@ -187,7 +180,7 @@
             copies.append(remote(ref, ref, sems.at[0, turn, sem], sems.at[1, turn, sem], p.client, 1 - p.core))
         return copies
 
-    def begin(self, master):
+    def fill(self, master):
         p = self.place
         start = 0
         for slot in range(3):
@@ -195,6 +188,8 @@
             own = block_ref(self.weights[slot], self.counts[slot], p.z, p.y, p.x, p.core, 0, rows)
             own[...] = master[start : start + rows, :].astype(low_type)
             start += rows
+
+    def begin(self):
         for step in range(3):
             self.z_copy(step, 0).start()
         self.near_start(0)
@@ -331,10 +326,6 @@
     def add(self, slot, spots, start, count, box):
         ref = block_ref(self.grads[slot], self.counts[slot], *spots, self.place.core, start, count)
         ref[...] = (ref[...].astype(wide) + box.astype(wide)).astype(low_type)
-
-    def turn(self, slot, turn):
-        for lag, step in ((2, self.far_step), (1, self.near_step), (0, self.core_step)):
-            when((turn >= lag) & (turn < lag + 4), functools.partial(step, turn - lag, slot))
 
     def core_step(self, which, slot):
         for copy in self.core_copies(which, slot):
@@ -475,7 +466,28 @@
     def lanes(index, size):
         return pl.ds(pl.multiple_of(index * size, size), size)
 
-    place.greet(gather)
+    weights = (w_first, w_middle, w_last)
+    if gather:
+        held = act_three.at[pl.ds(0, master.shape[0]), pl.ds(0, width)]
+        load = pltpu.make_async_copy(master, held, sem_local.at[8])
+        load.start()
+        counts = [channels // 32, 9 * width // 32, channels // 32]
+        spread = Spread(place, weights, counts, near_parts[:4])
+        fold = Fold(place, (w_first, mid_wide, w_last), counts, near_parts[4:])
+        due = spread.steps()
+        load.wait()
+        spread.fill(held)
+        place.greet(True)
+        spread.begin()
+    else:
+        place.greet(False)
+        loads = [
+            pltpu.make_async_copy(src, dst, sem_local.at[8 + slot])
+            for slot, (src, dst) in enumerate(zip((first_in, middle_in, last_in), weights))
+        ]
+        for load in loads:
+            load.start()
+        due = []
 
     quarter = half // 2
     own_rows = pl.ds(pl.multiple_of(core * count_rows, count_rows), count_rows)
@@ -513,26 +525,6 @@
     for copy in to_mate + own_copies:
         copy.start()
 
-    weights = (w_first, w_middle, w_last)
-    if gather:
-        counts = [channels // 32, 9 * width // 32, channels // 32]
-        spread = Spread(place, weights, counts, near_parts[:4])
-        held = act_three.at[pl.ds(0, master.shape[0]), pl.ds(0, width)]
-        load = pltpu.make_async_copy(master, held, sem_local.at[8])
-        load.start()
-        load.wait()
-        spread.begin(held)
-        fold = Fold(place, (w_first, mid_wide, w_last), counts, near_parts[4:])
-        due = spread.steps()
-    else:
-        loads = [
-            pltpu.make_async_copy(src, dst, sem_local.at[8 + slot])
-            for slot, (src, dst) in enumerate(zip((first_in, middle_in, last_in), weights))
-        ]
-        for load in loads:
-            load.start()
-        due = []
-
     def advance(count):
         for group in due[:count]:
             for step in group:
@@ -554,9 +546,11 @@
         else:
             loads[slot].wait()
 
-    def fold_turn(slot, turn):
+    def arrive_turns(slot, turns):
         if gather:
-            fold.turn(slot, turn)
+            for turn in turns:
+                for copy in spread.core_copies(turn, slot):
+                    copy.wait_recv()
 
     def fold_step(kind, slot, which):
         if gather:
@@ -697,7 +691,10 @@
         return carry
 
     lax.fori_loop(0, SIDE, hide_one, 0)
-    arrive(1, 4)
+    if gather:
+        arrive_turns(1, (0, 1))
+    else:
+        arrive(1, 0)
 
     step = mine_images
     piece = width // 2
@@ -717,18 +714,30 @@
 
     low_start, high_start, reaches = (0, 0, step), (step, 0, 0), (line - step, line, line - step)
 
+    early, taps = 4, 9
+
     def second_part(index, carry):
-        down, columns = index // 2, lanes(index % 2, piece)
+        tap = jnp.where(place.z < 2, index, (index + taps - early) % taps) if gather else index
+
+        @pl.when(index == early)
+        def _():
+            arrive_turns(1, (2, 3))
+
+        down = tap // 3
         for over in range(3):
-            left = row_windows(taps_one, down, low_start[over], reaches[over])
-            kernel = w_middle[pl.ds(pl.multiple_of((3 * down + over) * width, width), width), columns]
-            add_windows(act_two, columns, dot_nn(left, kernel), high_start[over], reaches[over])
-        advance_at(index, (1, 3, 5))
+
+            @pl.when(tap % 3 == over)
+            def _():
+                left = row_windows(taps_one, down, low_start[over], reaches[over])
+                kernel = w_middle[pl.ds(pl.multiple_of(tap * width, width), width), :]
+                add_windows(act_two, slice(None), dot_nn(left, kernel), high_start[over], reaches[over])
+
+        advance_at(index, (2, 5, 6, 8))
         return carry
 
     act_two[...] = jnp.zeros_like(act_two)
-    lax.fori_loop(0, 6, second_part, 0)
-    del due[:3]
+    lax.fori_loop(0, taps, second_part, 0)
+    del due[:4]
     look_over(act_two, whole_width)
     close_stats(1, whole_width, width)
     move_two = swap(1, width)
@@ -942,7 +951,8 @@
     def expand_group(which, carry):
         put(w_last, which, dot_tn(mid_group(which), hidden_two[...]))
         fold_begin(which, 2)
-        fold_turn(2, which - 1)
+        fold_at(which, 2, (0, 2, 0))
+        fold_at(which, 3, (0, 2, 1))
         return carry
 
     lax.fori_loop(0, groups, expand_group, 0)
@@ -961,22 +971,35 @@
         return carry
 
     lax.fori_loop(0, SIDE, grad_two, 0)
-    fold_turn(2, groups - 1)
+    fold_step(0, 2, 2)
+    fold_step(1, 2, 0)
+    core_step, near_step, far_step = 0, 1, 2
+    plan = {
+        0: [(core_step, 2, 3)],
+        1: [(near_step, 2, 1)],
+        2: [(far_step, 2, 0), (near_step, 2, 2)],
+        3: [(far_step, 2, 1), (near_step, 2, 3)],
+        4: [(far_step, 2, 2)],
+        5: [(far_step, 2, 3), (core_step, 1, 0)],
+        7: [(core_step, 1, 1)],
+    }
+
     def middle_row(down, carry):
         for over in range(3):
             left = row_windows(taps_one, down, low_start[over], reaches[over])
             right = row_windows(taps_two, 1, high_start[over], reaches[over])
             rows = pl.ds(pl.multiple_of((3 * down + over) * width, width), width)
             mid_wide[rows, :] = dot_tn(left, right).astype(low_type)
-        fold_begin(down, 1)
-
-        @pl.when(down == 2)
-        def _():
-            fold_begin(3, 1)
-
-        fold_turn(2, groups + down)
-        fold_at(down, 1, (0, 1, 0))
-        fold_at(down, 2, (1, 1, 0), (0, 1, 1))
+            for row in range(3):
+                tap = 3 * row + over
+
+                @pl.when(down == row)
+                def _():
+                    if tap >= 2 and tap % 2 == 0:
+                        fold_begin(tap // 2 - 1, 1)
+                    for step in plan.get(tap, ()):
+                        fold_step(*step)
+
         return carry
 
     lax.fori_loop(0, 3, middle_row, 0)
@@ -989,18 +1012,17 @@
             start = pl.multiple_of((3 * down + over) * width + side * piece, piece)
             value = dot_nt(left, w_middle[pl.ds(start, piece), :])
             add_windows(act_three, columns, value, low_start[over], reaches[over])
-        fold_at(index, 0, (0, 1, 2))
-        fold_at(index, 1, (0, 1, 3))
-        fold_at(index, 2, (1, 1, 1))
-        fold_at(index, 3, (2, 1, 0))
-        fold_at(index, 4, (1, 1, 2))
-        fold_at(index, 5, (2, 1, 1))
+        fold_at(index, 0, (core_step, 1, 2), (near_step, 1, 0))
+        fold_at(index, 1, (core_step, 1, 3))
+        fold_at(index, 2, (near_step, 1, 1), (far_step, 1, 0))
+        fold_at(index, 4, (far_step, 1, 1))
+        fold_at(index, 5, (near_step, 1, 2))
         return carry
 
     act_three[:, space_one] = jnp.zeros((count_rows, width), wide)
     lax.fori_loop(0, 6, back_one, 0)
     drop_into(act_one, 0, gain_one, bias_one, space_one)
-    fold_step(1, 1, 3)
+    fold_step(near_step, 1, 3)
     close_back(5)
     move_back_one = swap(5, width)
     move_back_one.start()
@@ -1013,13 +1035,14 @@
         return carry
 
     lax.fori_loop(0, SIDE, grad_one, 0)
-    fold_step(2, 1, 2)
+    fold_step(far_step, 1, 2)
 
     def reduce_group(which, carry):
         put(w_first, which, dot_tn(x_all[:, lanes(which, group)], hidden_two[...]))
         fold_begin(which, 0)
-        fold_turn(0, which - 1)
-        fold_at(which, 1, (2, 1, 3))
+        fold_at(which, 0, (far_step, 1, 3))
+        fold_at(which, 2, (core_step, 0, 0))
+        fold_at(which, 3, (core_step, 0, 1), (near_step, 0, 0))
         return carry
 
     lax.fori_loop(0, groups, reduce_group, 0)
@@ -1037,8 +1060,18 @@
             grad_norm_out[kind * per_kind + spot : kind * per_kind + spot + 1, :] = whole[
                 :, spot * LANES : (spot + 1) * LANES
             ]
-    for turn in range(groups - 1, groups + 2):
-        fold_turn(0, turn)
+    for step in (
+        (core_step, 0, 2),
+        (core_step, 0, 3),
+        (far_step, 0, 0),
+        (near_step, 0, 1),
+        (near_step, 0, 2),
+        (far_step, 0, 1),
+        (near_step, 0, 3),
+        (far_step, 0, 2),
+        (far_step, 0, 3),
+    ):
+        fold_step(*step)
     if gather:
         start = 0
         for slot in range(3):
@@ -1382,6 +1415,11 @@
                         self.back_copy(slot, x, core).wait_send()
 
 
+def corner_spot(number, part):
+    row, column = number // 2, number % 2
+    return slice(row * part, (row + 1) * part), slice(column * part, (column + 1) * part)
+
+
 def base_kernel(
     ratios,
     sizes,
@@ -1418,15 +1456,17 @@
     extra.pop(0)()
 
     width = master.shape[1]
-    part = width // 2
+    part = width // CUTS
+    corners = [(row, column) for row in range(CUTS) for column in range(row, CUTS)]
     share.gather()
     held = rows_in[...]
     partial = lax.dot_general(
         held, held, (((0,), (0,)), ((), ())), precision=precise, preferred_element_type=wide
     )
-    gram[0:part, :] = partial[:part, :part]
-    gram[part : 2 * part, :] = partial[:part, part:]
-    gram[2 * part :, :] = partial[part:, part:]
+    for number, (row, column) in enumerate(corners):
+        gram[corner_spot(number, part)] = partial[
+            row * part : (row + 1) * part, column * part : (column + 1) * part
+        ]
 
     @pl.when(place.x == 1)
     def _():
@@ -1441,14 +1481,17 @@
 
     spots = lax.broadcasted_iota(jnp.int32, (part, part), 0)
     diagonal = spots == lax.broadcasted_iota(jnp.int32, (part, part), 1)
-    corner, side, end = [gram_total[start * part : (start + 1) * part, :] for start in range(3)]
-    trace = jnp.sum(jnp.where(diagonal, corner + end, 0.0))
+    blocks = [gram_total[corner_spot(number, part)] for number in range(len(corners))]
+    trace = sum(
+        jnp.sum(jnp.where(diagonal, block, 0.0)) for block, (row, column) in zip(blocks, corners) if row == column
+    )
     factor = 1.0 / (jnp.sqrt(trace) + 1e-07)
     square = factor * factor
-    grams[:part, :part] = corner * square
-    grams[:part, part:] = side * square
-    grams[part:, :part] = side.T * square
-    grams[part:, part:] = end * square
+    for block, (row, column) in zip(blocks, corners):
+        rows, columns = slice(row * part, (row + 1) * part), slice(column * part, (column + 1) * part)
+        grams[rows, columns] = block * square
+        if row < column:
+            grams[columns, rows] = block.T * square
     rows_in[...] = rows_in[...] * factor
 
     def turn(count, carry):
@@ -1476,11 +1519,12 @@
 
 def base_pass(ratios, sizes, master, momentum, anchor, loss_tile, grads):
     rows, width = master.shape
-    part = width // 2
+    part = width // CUTS
+    gram_rows = CUTS * (CUTS + 1) // 4 * part
     vmem = pl.BlockSpec(memory_space=pltpu.VMEM)
-    scratch = [pltpu.VMEM((3 * part, part), wide)] * 2
-    scratch += [pltpu.VMEM((count, 3 * part // 8, part), wide) for count in (4, 3)]
-    scratch += [pltpu.VMEM((3 * part, part), wide)]
+    scratch = [pltpu.VMEM((gram_rows, 2 * part), wide)] * 2
+    scratch += [pltpu.VMEM((count, gram_rows // 8, 2 * part), wide) for count in (4, 3)]
+    scratch += [pltpu.VMEM((gram_rows, 2 * part), wide)]
     scratch += [
         pltpu.VMEM((width, width), wide),
         pltpu.VMEM((rows, width), wide),

time: 231 us -> 217 us (0.939)
  Pallas kernels: 230 us -> 216 us
    pallas_call x1, Pallas kernels: 158 us -> 150 us  [client_pass(): pl.pallas_call(functools.partial(client_kernel, gather, images, classes),...]
    pallas_call x1, Pallas kernels: 67.8 us -> 62.1 us  [base_pass(): pl.pallas_call(functools.partial(base_kernel, ratios, sizes), out_shape=o...]
where the time goes in v5:
time: 217 us
  Pallas kernels  216 us (100%)
    pallas_call x1, Pallas kernels, client_pass(): pl.pallas_call(functools.partial(client_kernel, gather, images, classes),...  150 us
    pallas_call x1, Pallas kernels, base_pass(): pl.pallas_call(functools.partial(base_kernel, ratios, sizes), out_shape=o...  62.1 us

profile of v5, /device:TPU:0, one launch (start us, length us, event | category | flops | bytes accessed | tf_op | source)
XLA Modules:
  0.0 217.1 jit_solution(190323931479145234)
XLA Ops:
  1.3 149.7 %shard_map.195 = (f32[272,512]{1,0:T(8,128)}, f32[24,128]{1,0:T(8,128)}, f32[800,128]{1,0:T(8,128)}, f32[8,128]{1,0:T(8,128)}) custom-call(bf16[3136,1024]{1,0:T(8,128)(2,1)} %bitcast.31, s32[1,64]{1,0:T(1,128)} %labels.1, s32[1]{0:T(128)S(6)} %copy.22.flag, f32[24,128]{1,0:T(8,128)} %bitcast.43, f32[800,128]{1,0:T(8,128)} %bitcast.39, f32[272,512]{1,0:T(8,128)} %bitcast.32), custom_call_target="tpu_custom_call" | custom-call | tf_op jit(solution)/shard_map/pallas_call | solution.py:1156
  150.9 62.1 %shard_map.196 = (f32[272,512]{1,0:T(8,128)}, f32[8,128]{1,0:T(8,128)}) custom-call(f32[272,512]{1,0:T(8,128)} %bitcast.33, f32[272,512]{1,0:T(8,128)} %bitcast.35, f32[272,512]{1,0:T(8,128)} %bitcast.37, f32[8,128]{1,0:T(8,128)} %get-tuple-element.26.loss_in, f32[272,512]{1,0:T(8,128)} %get-tuple-element.27.grads), custom_call_target="tpu_custom_call" | custom-call | tf_op jit(solution)/shard_map/pallas_call | solution.py:1543
  213.1 3.9 %shard_map.197 = (f32[2]{0:T(128)}, f32[272,512]{1,0:T(8,128)}, f32[272,512]{1,0:T(8,128)}, bf16[272,512]{1,0:T(8,128)(2,1)}, f32[24,128]{1,0:T(8,128)}, /*index...) custom-call(f32[8,128]{1,0:T(8,128)} %get-tuple-element.28.loss_tile, ...), custom_call_target="tpu_custom_call" | custom-call | tf_op jit(solution)/shard_map/pallas_call | solution.py:1581

commit v6 on v5

--- a/solution.py
+++ b/solution.py
@@ -390,6 +390,370 @@
             def _():
                 for number in range(6):
                     self.z_copy(which, self.place.z, number).wait_send()
+class GramSum:
+    def __init__(self, place, data, total, boxes, sems):
+        self.place = place
+        self.data = data
+        self.total = total
+        self.y_box, self.z_box = boxes
+        self.sems = sems
+        self.share = data.shape[0] // 8
+        self.down_order = place.others[::-1] + [place.z]
+
+    def rows(self, z, y):
+        return pl.ds(pl.multiple_of((z * 2 + y) * self.share, 8), self.share)
+
+    def copy(self, number, src, dst, to):
+        sems = self.sems
+        return remote(src, dst, sems.at[0, number], sems.at[1, number], to, self.place.core)
+
+    def y_down(self, turn):
+        p = self.place
+        src = self.data.at[self.rows(self.down_order[turn], 1 - p.y), :]
+        return self.copy(turn, src, self.y_box.at[turn], p.along_y())
+
+    def z_down(self, step):
+        p = self.place
+        src = self.data.at[self.rows(p.others[step], p.y), :]
+        return self.copy(4 + step, src, self.z_box.at[step], p.along_z(step))
+
+    def z_up(self, step):
+        p = self.place
+        ref = self.total.at[self.rows(p.z, p.y), :]
+        return self.copy(7 + step, ref, ref, p.along_z(step))
+
+    def y_up(self, turn):
+        p = self.place
+        ref = self.total.at[self.rows(([p.z] + p.others)[turn], p.y), :]
+        return self.copy(10 + turn, ref, ref, p.along_y())
+
+    def run(self):
+        p = self.place
+        for turn in range(4):
+            self.y_down(turn).start()
+        for turn in range(4):
+            self.y_down(turn).wait_recv()
+            self.data[self.rows(self.down_order[turn], p.y), :] += self.y_box[turn]
+            if turn < 3:
+                self.z_down(2 - turn).start()
+        mine = self.rows(p.z, p.y)
+        value = self.data[mine, :]
+        for step in (2, 1, 0):
+            self.z_down(step).wait_recv()
+            value += self.z_box[step]
+        self.total[mine, :] = value
+        for step in range(3):
+            self.z_up(step).start()
+        self.y_up(0).start()
+        for step in range(3):
+            self.z_up(step).wait_recv()
+            self.y_up(1 + step).start()
+        for turn in range(4):
+            self.y_up(turn).wait_recv()
+
+    def drain(self):
+        for turn in range(4):
+            self.y_down(turn).wait_send()
+            self.y_up(turn).wait_send()
+        for step in range(3):
+            self.z_down(step).wait_send()
+            self.z_up(step).wait_send()
+
+
+class TileSum:
+    def __init__(self, place, tiles, boxes, sems):
+        self.place = place
+        self.tiles = tiles
+        self.boxes = boxes
+        self.sems = sems
+
+    def copy(self, stage, box):
+        p = self.place
+        to = (p.client, p.along_x(), p.along_y()) + tuple(p.along_z(step) for step in range(3))
+        core = 1 - p.core if box == 0 else p.core
+        return remote(
+            self.tiles.at[stage], self.boxes.at[box], self.sems.at[0, box], self.sems.at[1, box], to[box], core
+        )
+
+    def start(self):
+        self.copy(0, 0).start()
+
+    def pair(self, stage):
+        self.copy(stage, stage).wait_recv()
+        self.tiles[stage + 1] = self.tiles[stage] + self.boxes[stage]
+        if stage < 2:
+            self.copy(stage + 1, stage + 1).start()
+        else:
+            for step in range(3):
+                self.copy(3, 3 + step).start()
+
+    def result(self):
+        for step in range(3):
+            self.copy(3, 3 + step).wait_recv()
+        return (self.tiles[3] + self.boxes[3]) + (self.boxes[4] + self.boxes[5])
+
+    def drain(self):
+        for stage in range(3):
+            self.copy(stage, stage).wait_send()
+        for step in range(3):
+            self.copy(3, 3 + step).wait_send()
+
+
+def halves_of(value):
+    high = value.astype(low_type)
+    return high, (value - high.astype(wide)).astype(low_type)
+
+
+class Share:
+    def __init__(self, place, sizes, buffers, sems):
+        self.place = place
+        self.sizes = sizes
+        self.fresh, self.rows_in, self.rows_out, self.back = buffers
+        self.sems = sems
+        self.bounds = [0, sizes[0], sizes[0] + sizes[1], sum(sizes)]
+        p = place
+        self.duty = jnp.where(p.x == 1, 1, 2 * p.core)
+        self.mine = p.x * 2 + p.core
+
+    def section(self, slot):
+        return pl.ds(self.bounds[slot], self.sizes[slot])
+
+    def spot(self, slot, x, core):
+        number = x if slot == 1 else x * 2 + core
+        return pl.ds(pl.multiple_of(number * self.sizes[slot], 16), self.sizes[slot])
+
+    def doer(self, slot):
+        return (0, 0) if slot == 0 else (0, 1) if slot == 2 else (1, self.place.core)
+
+    def out_copy(self, slot):
+        p = self.place
+        x, core = self.doer(slot)
+        return remote(
+            self.fresh.at[self.section(slot), :],
+            self.rows_in.at[self.spot(slot, p.x, p.core), :],
+            self.sems.at[0, slot],
+            self.sems.at[1, self.mine],
+            p.at(p.z, p.y, x),
+            core,
+        )
+
+    def in_copy(self, slot, x, core):
+        p = self.place
+        return remote(
+            self.fresh.at[self.section(slot), :],
+            self.rows_in.at[self.spot(slot, x, core), :],
+            self.sems.at[0, slot],
+            self.sems.at[1, x * 2 + core],
+            p.at(p.z, p.y, x),
+            core,
+        )
+
+    def back_copy(self, slot, x, core):
+        p = self.place
+        return remote(
+            self.rows_out.at[self.spot(slot, x, core), :],
+            self.back.at[self.section(slot), :],
+            self.sems.at[0, 3 + x * 2 + core],
+            self.sems.at[1, 4 + slot],
+            p.at(p.z, p.y, x),
+            core,
+        )
+
+    def users(self, slot):
+        p = self.place
+        if slot == 1:
+            return [(0, p.core), (1, p.core)]
+        return [(x, core) for x in (0, 1) for core in (0, 1)]
+
+    def send(self, slot):
+        @pl.when(self.duty != slot)
+        def _():
+            self.out_copy(slot).start()
+
+        @pl.when(self.duty == slot)
+        def _():
+            self.rows_in[self.spot(slot, self.place.x, self.place.core), :] = self.fresh[self.section(slot), :]
+
+    def gather(self):
+        p = self.place
+        for slot in range(3):
+
+            @pl.when(self.duty == slot)
+            def _():
+                for x, core in self.users(slot):
+
+                    @pl.when((p.x != x) | (p.core != core))
+                    def _():
+                        self.in_copy(slot, x, core).wait_recv()
+
+    def give_back(self):
+        p = self.place
+        for slot in range(3):
+
+            @pl.when(self.duty == slot)
+            def _():
+                for x, core in self.users(slot):
+
+                    @pl.when((p.x != x) | (p.core != core))
+                    def _():
+                        self.back_copy(slot, x, core).start()
+
+                self.back[self.section(slot), :] = self.rows_out[self.spot(slot, p.x, p.core), :]
+
+    def finish(self):
+        p = self.place
+        for slot in range(3):
+
+            @pl.when(self.duty != slot)
+            def _():
+                self.back_copy(slot, p.x, p.core).wait_recv()
+                self.out_copy(slot).wait_send()
+
+            @pl.when(self.duty == slot)
+            def _():
+                for x, core in self.users(slot):
+
+                    @pl.when((p.x != x) | (p.core != core))
+                    def _():
+                        self.back_copy(slot, x, core).wait_send()
+
+
+def corner_spot(number, part):
+    row, column = number // 2, number % 2
+    return slice(row * part, (row + 1) * part), slice(column * part, (column + 1) * part)
+
+
+def orthogonal(place, ratios, share, share_sems, gram, gram_total, mate_gram, gram_sum, squares, rows_in, low_rows):
+    grams, mixed, once = squares
+    count, width = rows_in.shape
+    part = width // CUTS
+    corners = [(row, column) for row in range(CUTS) for column in range(row, CUTS)]
+    right_high, right_low = [low_rows.at[pl.ds(count + spot * width, width), :] for spot in range(2)]
+
+    def set_right(value_ref):
+        for start in range(0, width, part):
+            rows = slice(start, start + part)
+            right_high[rows, :], right_low[rows, :] = halves_of(value_ref[rows, :])
+
+    def times_right(value):
+        high, low = halves_of(value)
+        left = jnp.concatenate([high, high, low], axis=1)
+        right = jnp.concatenate([right_high[...], right_low[...], right_high[...]], axis=0)
+        return dot_nn(left, right)
+
+    def by_rows(rows, step, call):
+        def body(index, carry):
+            call(pl.ds(pl.multiple_of(index * step, step), step))
+            return carry
+
+        lax.fori_loop(0, rows // step, body, 0)
+
+    share.gather()
+    high, low = halves_of(rows_in[...])
+    left = jnp.concatenate([high, high, low], axis=0)
+    right = jnp.concatenate([high, low, high], axis=0)
+    for row in range(CUTS):
+        strip = dot_tn(left[:, row * part : (row + 1) * part], right[:, row * part :])
+        for column in range(row, CUTS):
+            gram[corner_spot(corners.index((row, column)), part)] = strip[
+                :, (column - row) * part : (column - row + 1) * part
+            ]
+
+    @pl.when(place.x == 1)
+    def _():
+        swap = remote(gram, mate_gram, share_sems.at[0, 7], share_sems.at[1, 7], place.client, 1 - place.core)
+        swap.start()
+        swap.wait()
+        gram[...] += mate_gram[...]
+
+    gram_sum.run()
+    spots = lax.broadcasted_iota(jnp.int32, (part, part), 0)
+    diagonal = spots == lax.broadcasted_iota(jnp.int32, (part, part), 1)
+    trace = 0.0
+    for number, (row, column) in enumerate(corners):
+        if row == column:
+            trace += jnp.sum(jnp.where(diagonal, gram_total[corner_spot(number, part)], 0.0))
+    factor = 1.0 / (jnp.sqrt(trace) + 1e-07)
+    square = factor * factor
+    for number, (row, column) in enumerate(corners):
+        rows, columns = slice(row * part, (row + 1) * part), slice(column * part, (column + 1) * part)
+        block = gram_total[corner_spot(number, part)] * square
+        grams[rows, columns] = block
+        if row < column:
+            grams[columns, rows] = block.T
+    rows_in[...] = rows_in[...] * factor
+    step = width // 2
+
+    def turn(number, carry):
+        set_right(grams)
+
+        def mix(rows):
+            current = grams[rows, :]
+            mixed[rows, :] = schulz_second * current + schulz_third * times_right(current)
+
+        by_rows(width, step, mix)
+        set_right(mixed)
+
+        def move(rows):
+            held = rows_in[rows, :]
+            rows_in[rows, :] = schulz_first * held + times_right(held)
+
+        by_rows(count, count // 2, move)
+
+        @pl.when(number < NS_STEPS - 1)
+        def _():
+            def first(rows):
+                current = grams[rows, :]
+                once[rows, :] = schulz_first * current + times_right(current)
+
+            def second(rows):
+                current = once[rows, :]
+                grams[rows, :] = schulz_first * current + times_right(current)
+
+            by_rows(width, step, first)
+            by_rows(width, step, second)
+
+        return carry
+
+    lax.fori_loop(0, NS_STEPS, turn, 0)
+    ratio = jnp.where(share.duty == 1, ratios[1], ratios[0])
+    low_rows[0:count, :] = (rows_in[...] * ratio).astype(low_type)
+    share.give_back()
+
+
+def update_kernel(loss_tile, master, fresh_momentum, ortho, *rest):
+    norms, grad_norm, heads, grad_head, outs = rest[0:3], rest[3], rest[4:7], rest[7], rest[8:]
+    loss_out, *outs = outs
+    loss_out[0] = loss_tile[0, 0]
+    loss_out[1] = loss_tile[0, 1]
+    momentum_out, base_out, low_out = outs[0:3]
+    held = master[...]
+    momentum_out[...] = fresh_momentum[...]
+    fresh = held - muon_rate * (ortho[...].astype(wide) + muon_decay * held)
+    base_out[...] = fresh
+    low_out[...] = fresh.astype(low_type)
+    for targets, values, grad, rate, decay in (
+        (outs[3:6], norms, grad_norm, norm_rate, 0.0),
+        (outs[6:9], heads, grad_head, head_rate, head_decay),
+    ):
+        updates = adam_update(values[0][...], grad[...], values[1][...], values[2][...], rate, decay)
+        for target, value in zip(targets, updates):
+            target[...] = value
+
+
+def update_pass(loss_tile, master, fresh_momentum, ortho, norms, grad_norm, heads, grad_head):
+    vmem = pl.BlockSpec(memory_space=pltpu.VMEM)
+    smem = pl.BlockSpec(memory_space=pltpu.SMEM)
+    operands = [loss_tile, master, fresh_momentum, ortho, *norms, grad_norm, *heads, grad_head]
+    outs = [(2,), master.shape, master.shape, master.shape] + [grad_norm.shape] * 3 + [grad_head.shape] * 3
+    types = [wide, wide, wide, low_type] + [wide] * 6
+    return pl.pallas_call(
+        update_kernel,
+        out_shape=[jax.ShapeDtypeStruct(shape, kind) for shape, kind in zip(outs, types)],
+        in_specs=[smem] + [vmem] * (len(operands) - 1),
+        out_specs=[smem] + [vmem] * (len(outs) - 1),
+        compiler_params=pltpu.CompilerParams(vmem_limit_bytes=VMEM_BYTES),
+    )(*operands)
 
 
 def norm_stats(mine, theirs, count):
@@ -401,6 +765,7 @@
 
 def client_kernel(
     gather,
+    ratios,
     images,
     classes,
     features,
@@ -411,11 +776,11 @@
     *rest,
 ):
     if gather:
-        master, *rest = rest
+        master, momentum, anchor, *rest = rest
     else:
         first_in, middle_in, last_in, *rest = rest
     if gather:
-        grads_out, *rest = rest
+        fresh_out, ortho_out, *rest = rest
     else:
         grads_out, rest = rest[:3], rest[3:]
     (
@@ -473,11 +838,21 @@
         load.start()
         counts = [channels // 32, 9 * width // 32, channels // 32]
         spread = Spread(place, weights, counts, near_parts[:4])
-        fold = Fold(place, (w_first, mid_wide, w_last), counts, near_parts[4:])
+        fold = Fold(place, (w_first, mid_wide, w_last), counts, near_parts[4:19])
+        rows_in, back, tiles, tile_boxes, gram_total, y_box, z_box, mate_gram = near_parts[19:27]
+        tile_sems, share_sems, gram_sems = near_parts[27:]
+        block_rows = master.shape[0]
+        side_space = pl.ds(half, width)
+        held_base, held_momentum, held_anchor, fresh = [
+            act_three.at[pl.ds(number * block_rows, block_rows), side_space] for number in range(4)
+        ]
+        rows_in[...] = jnp.zeros_like(rows_in)
+        share = Share(place, counts, (fresh, rows_in, hidden_two, back), share_sems)
+        tile_sum = TileSum(place, tiles, tile_boxes, tile_sems)
         due = spread.steps()
         load.wait()
         spread.fill(held)
-        place.greet(True)
+        place.greet(True, True)
         spread.begin()
     else:
         place.greet(False)
@@ -662,7 +1037,10 @@
     whole_width = pl.ds(0, width)
 
     def first_part(index, carry):
-        act_one[...] += dot_nn(x_all[:, lanes(index, group)], flat_rows(w_first[index]))
+        kernel = flat_rows(w_first[index])
+        for side in range(2):
+            columns = slice(side * width // 2, (side + 1) * width // 2)
+            act_one[:, columns] += dot_nn(x_all[:, lanes(index, group)], kernel[:, columns])
         advance_at(index, (0, 1, 2))
         return carry
 
@@ -729,8 +1107,11 @@
             @pl.when(tap % 3 == over)
             def _():
                 left = row_windows(taps_one, down, low_start[over], reaches[over])
-                kernel = w_middle[pl.ds(pl.multiple_of(tap * width, width), width), :]
-                add_windows(act_two, slice(None), dot_nn(left, kernel), high_start[over], reaches[over])
+                rows = pl.ds(pl.multiple_of(tap * width, width), width)
+                for side in range(2):
+                    columns = slice(side * piece, (side + 1) * piece)
+                    value = dot_nn(left, w_middle[rows, columns])
+                    add_windows(act_two, columns, value, high_start[over], reaches[over])
 
         advance_at(index, (2, 5, 6, 8))
         return carry
@@ -751,14 +1132,16 @@
         value = normal(act_two, 1, index) * gain_two + bias_two
         hidden = (value * sigmoid(value)).astype(low_type)
         hidden_two[tile(index), :] = hidden
-        value = dot_nt(hidden, flat_rows(w_last[...]))
-        act_three[tile(index), :] = value
-        start = jnp.where(index == 0, column_sum(value[0:8]) / 8.0, shift[0:1, :])
-        gap = value - start
-        kept_sums = jnp.where(index == 0, 0.0, shift[8:24, :])
-        shift[0:1, :] = start
-        shift[8:16, :] = kept_sums[0:8] + fold_rows(gap)
-        shift[16:24, :] = kept_sums[8:16] + fold_rows(gap * gap)
+        for which in range(groups):
+            columns = slice(which * group, (which + 1) * group)
+            value = dot_nt(hidden, flat_rows(w_last[which]))
+            act_three[tile(index), columns] = value
+            start = jnp.where(index == 0, column_sum(value[0:8]) / 8.0, shift[0:1, columns])
+            gap = value - start
+            kept_sums = jnp.where(index == 0, 0.0, shift[8:24, columns])
+            shift[0:1, columns] = start
+            shift[8:16, columns] = kept_sums[0:8] + fold_rows(gap)
+            shift[16:24, columns] = kept_sums[8:16] + fold_rows(gap * gap)
         return carry
 
     lax.fori_loop(0, SIDE, third_line, 0)
@@ -941,6 +1324,24 @@
     close_back(4)
     move_back_two = swap(4, width)
     move_back_two.start()
+    if gather:
+        base_loads = [
+            pltpu.make_async_copy(src, dst, sem_local.at[1 + number])
+            for number, (src, dst) in enumerate(
+                ((master, held_base), (momentum, held_momentum), (anchor, held_anchor))
+            )
+        ]
+        for load in base_loads:
+            load.start()
+        tiles[0] = loss_out[...]
+        tile_sum.start()
+
+    def settle_section(slot):
+        if gather:
+            rows = share.section(slot)
+            grad = fold.result(slot) + prox_weight * (held_base[rows, :] - held_anchor[rows, :])
+            fresh[rows, :] = momentum_decay * held_momentum[rows, :] + grad
+            share.send(slot)
 
     if gather:
         spread.drain()
@@ -1003,6 +1404,10 @@
         return carry
 
     lax.fori_loop(0, 3, middle_row, 0)
+    if gather:
+        tile_sum.pair(0)
+        for load in base_loads:
+            load.wait()
 
     def back_one(index, carry):
         down, side = index // 2, index % 2
@@ -1023,6 +1428,7 @@
     lax.fori_loop(0, 6, back_one, 0)
     drop_into(act_one, 0, gain_one, bias_one, space_one)
     fold_step(near_step, 1, 3)
+    settle_section(2)
     close_back(5)
     move_back_one = swap(5, width)
     move_back_one.start()
@@ -1036,6 +1442,8 @@
 
     lax.fori_loop(0, SIDE, grad_one, 0)
     fold_step(far_step, 1, 2)
+    if gather:
+        tile_sum.pair(1)
 
     def reduce_group(which, carry):
         put(w_first, which, dot_tn(x_all[:, lanes(which, group)], hidden_two[...]))
@@ -1072,18 +1480,28 @@
         (far_step, 0, 3),
     ):
         fold_step(*step)
+        if step == (far_step, 0, 0):
+            settle_section(1)
     if gather:
-        start = 0
-        for slot in range(3):
-            rows = fold.counts[slot]
-            act_three[kept + start : kept + start + rows, half : half + width] = fold.result(slot)
-            start += rows
-        leave = pltpu.make_async_copy(
-            act_three.at[pl.ds(kept, start), pl.ds(half, width)], grads_out, sem_local.at[3]
-        )
+        settle_section(0)
+        leave = pltpu.make_async_copy(fresh, fresh_out, sem_local.at[1])
         leave.start()
+        tile_sum.pair(2)
+        part = width // CUTS
+        gram = act_three.at[pl.ds(0, gram_total.shape[0]), pl.ds(half + width, 2 * part)]
+        corner_rows = pl.ds(gram_total.shape[0], width)
+        squares = [act_three.at[corner_rows, pl.ds(spot * width, width)] for spot in (0, 1, 3)]
+        gram_sum = GramSum(place, gram, gram_total, (y_box, z_box), gram_sems)
+        orthogonal(place, ratios, share, share_sems, gram, gram_total, mate_gram, gram_sum, squares, rows_in, hidden_two)
+        share.finish()
+        loss_out[...] = tile_sum.result()
+        ortho_leave = pltpu.make_async_copy(back, ortho_out, sem_local.at[2])
+        ortho_leave.start()
+        gram_sum.drain()
+        tile_sum.drain()
+        fold.drain()
         leave.wait()
-        fold.drain()
+        ortho_leave.wait()
     else:
         outs = [
             pltpu.make_async_copy(ref, out, sem_local.at[slot])
@@ -1098,7 +1516,7 @@
         copy.wait_send()
 
 
-def client_pass(gather, classes, features, labels, flag, params, head, weights):
+def client_pass(gather, ratios, classes, features, labels, flag, params, head, weights):
     pixels, half = features.shape
     images = labels.shape[1]
     count_rows, channels = pixels // 2, 2 * half
@@ -1148,13 +1566,32 @@
         for lead in ((4, 2), (4,), (4,)):
             scratch += [pltpu.VMEM(lead + (rows, width), low_type) for rows in counts]
         scratch += [pltpu.SemaphoreType.DMA((2, 4, size)) for size in (6, 8, 6, 6)]
-        grads_shape = [jax.ShapeDtypeStruct((sum(counts), width), wide)]
-        grads_specs = [any_space]
+        part = width // CUTS
+        gram_rows = CUTS * (CUTS + 1) // 4 * part
+        many = max(4 * counts[0], 2 * counts[1])
+        scratch += [
+            pltpu.VMEM((many, width), wide),
+            pltpu.VMEM((sum(counts), width), low_type),
+            pltpu.VMEM((4, 8, LANES), wide),
+            pltpu.VMEM((6, 8, LANES), wide),
+            pltpu.VMEM((gram_rows, 2 * part), wide),
+            pltpu.VMEM((4, gram_rows // 8, 2 * part), wide),
+            pltpu.VMEM((3, gram_rows // 8, 2 * part), wide),
+            pltpu.VMEM((gram_rows, 2 * part), wide),
+            pltpu.SemaphoreType.DMA((2, 6)),
+            pltpu.SemaphoreType.DMA((2, 8)),
+            pltpu.SemaphoreType.DMA((2, 14)),
+        ]
+        grads_shape = [
+            jax.ShapeDtypeStruct((sum(counts), width), wide),
+            jax.ShapeDtypeStruct((sum(counts), width), low_type),
+        ]
+        grads_specs = [any_space] * 2
     else:
         grads_shape = [jax.ShapeDtypeStruct(weight.shape, low_type) for weight in weights]
         grads_specs = [any_space] * 3
     return pl.pallas_call(
-        functools.partial(client_kernel, gather, images, classes),
+        functools.partial(client_kernel, gather, ratios, images, classes),
         out_shape=grads_shape
         + [
             jax.ShapeDtypeStruct(params.shape, wide),
@@ -1180,411 +1617,6 @@
         first,
         second,
     )
-class GramSum:
-    def __init__(self, place, data, total, boxes, sems):
-        self.place = place
-        self.data = data
-        self.total = total
-        self.y_box, self.z_box = boxes
-        self.sems = sems
-        self.share = data.shape[0] // 8
-        self.down_order = place.others[::-1] + [place.z]
-
-    def rows(self, z, y):
-        return pl.ds(pl.multiple_of((z * 2 + y) * self.share, 8), self.share)
-
-    def copy(self, number, src, dst, to):
-        sems = self.sems
-        return remote(src, dst, sems.at[0, number], sems.at[1, number], to, self.place.core)
-
-    def y_down(self, turn):
-        p = self.place
-        src = self.data.at[self.rows(self.down_order[turn], 1 - p.y), :]
-        return self.copy(turn, src, self.y_box.at[turn], p.along_y())
-
-    def z_down(self, step):
-        p = self.place
-        src = self.data.at[self.rows(p.others[step], p.y), :]
-        return self.copy(4 + step, src, self.z_box.at[step], p.along_z(step))
-
-    def z_up(self, step):
-        p = self.place
-        ref = self.total.at[self.rows(p.z, p.y), :]
-        return self.copy(7 + step, ref, ref, p.along_z(step))
-
-    def y_up(self, turn):
-        p = self.place
-        ref = self.total.at[self.rows(([p.z] + p.others)[turn], p.y), :]
-        return self.copy(10 + turn, ref, ref, p.along_y())
-
-    def run(self, extra):
-        extra = list(extra)
-        p = self.place
-        for turn in range(4):
-            self.y_down(turn).start()
-        for turn in range(4):
-            self.y_down(turn).wait_recv()
-            self.data[self.rows(self.down_order[turn], p.y), :] += self.y_box[turn]
-            if turn < 3:
-                self.z_down(2 - turn).start()
-            if extra:
-                extra.pop(0)()
-        mine = self.rows(p.z, p.y)
-        value = self.data[mine, :]
-        for step in (2, 1, 0):
-            self.z_down(step).wait_recv()
-            value += self.z_box[step]
-        self.total[mine, :] = value
-        for step in range(3):
-            self.z_up(step).start()
-        self.y_up(0).start()
-        for step in range(3):
-            self.z_up(step).wait_recv()
-            self.y_up(1 + step).start()
-        for turn in range(4):
-            self.y_up(turn).wait_recv()
-
-    def drain(self):
-        for turn in range(4):
-            self.y_down(turn).wait_send()
-            self.y_up(turn).wait_send()
-        for step in range(3):
-            self.z_down(step).wait_send()
-            self.z_up(step).wait_send()
-
-
-class TileSum:
-    def __init__(self, place, tiles, boxes, sems):
-        self.place = place
-        self.tiles = tiles
-        self.boxes = boxes
-        self.sems = sems
-
-    def copy(self, stage, box):
-        p = self.place
-        to = (p.client, p.along_x(), p.along_y()) + tuple(p.along_z(step) for step in range(3))
-        core = 1 - p.core if box == 0 else p.core
-        return remote(
-            self.tiles.at[stage], self.boxes.at[box], self.sems.at[0, box], self.sems.at[1, box], to[box], core
-        )
-
-    def steps(self):
-        def start():
-            self.copy(0, 0).start()
-
-        def pair(stage):
-            self.copy(stage, stage).wait_recv()
-            self.tiles[stage + 1] = self.tiles[stage] + self.boxes[stage]
-            if stage < 2:
-                self.copy(stage + 1, stage + 1).start()
-            else:
-                for step in range(3):
-                    self.copy(3, 3 + step).start()
-
-        return [start] + [functools.partial(pair, stage) for stage in range(3)]
-
-    def result(self):
-        for step in range(3):
-            self.copy(3, 3 + step).wait_recv()
-        return (self.tiles[3] + self.boxes[3]) + (self.boxes[4] + self.boxes[5])
-
-    def drain(self):
-        for stage in range(3):
-            self.copy(stage, stage).wait_send()
-        for step in range(3):
-            self.copy(3, 3 + step).wait_send()
-
-
-def dot_high(left, right):
-    return jnp.dot(left, right, precision=lax.Precision.HIGH, preferred_element_type=wide)
-
-
-class Share:
-    def __init__(self, place, sizes, buffers, sems):
-        self.place = place
-        self.sizes = sizes
-        self.fresh, self.rows_in, self.rows_out, self.back = buffers
-        self.sems = sems
-        self.bounds = [0, sizes[0], sizes[0] + sizes[1], sum(sizes)]
-        p = place
-        self.duty = jnp.where(p.x == 1, 1, 2 * p.core)
-        self.mine = p.x * 2 + p.core
-
-    def section(self, slot):
-        return pl.ds(self.bounds[slot], self.sizes[slot])
-
-    def spot(self, slot, x, core):
-        number = x if slot == 1 else x * 2 + core
-        return pl.ds(pl.multiple_of(number * self.sizes[slot], 16), self.sizes[slot])
-
-    def doer(self, slot):
-        return (0, 0) if slot == 0 else (0, 1) if slot == 2 else (1, self.place.core)
-
-    def out_copy(self, slot):
-        p = self.place
-        x, core = self.doer(slot)
-        return remote(
-            self.fresh.at[self.section(slot), :],
-            self.rows_in.at[self.spot(slot, p.x, p.core), :],
-            self.sems.at[0, slot],
-            self.sems.at[1, self.mine],
-            p.at(p.z, p.y, x),
-            core,
-        )
-
-    def in_copy(self, slot, x, core):
-        p = self.place
-        return remote(
-            self.fresh.at[self.section(slot), :],
-            self.rows_in.at[self.spot(slot, x, core), :],
-            self.sems.at[0, slot],
-            self.sems.at[1, x * 2 + core],
-            p.at(p.z, p.y, x),
-            core,
-        )
-
-    def back_copy(self, slot, x, core):
-        p = self.place
-        return remote(
-            self.rows_out.at[self.spot(slot, x, core), :],
-            self.back.at[self.section(slot), :],
-            self.sems.at[0, 3 + x * 2 + core],
-            self.sems.at[1, 4 + slot],
-            p.at(p.z, p.y, x),
-            core,
-        )
-
-    def users(self, slot):
-        p = self.place
-        if slot == 1:
-            return [(0, p.core), (1, p.core)]
-        return [(x, core) for x in (0, 1) for core in (0, 1)]
-
-    def send(self):
-        for slot in range(3):
-
-            @pl.when(self.duty != slot)
-            def _():
-                self.out_copy(slot).start()
-
-            @pl.when(self.duty == slot)
-            def _():
-                self.rows_in[self.spot(slot, self.place.x, self.place.core), :] = self.fresh[self.section(slot), :]
-
-    def gather(self):
-        p = self.place
-        for slot in range(3):
-
-            @pl.when(self.duty == slot)
-            def _():
-                for x, core in self.users(slot):
-
-                    @pl.when((p.x != x) | (p.core != core))
-                    def _():
-                        self.in_copy(slot, x, core).wait_recv()
-
-    def give_back(self):
-        p = self.place
-        for slot in range(3):
-
-            @pl.when(self.duty == slot)
-            def _():
-                for x, core in self.users(slot):
-
-                    @pl.when((p.x != x) | (p.core != core))
-                    def _():
-                        self.back_copy(slot, x, core).start()
-
-                self.back[self.section(slot), :] = self.rows_out[self.spot(slot, p.x, p.core), :]
-
-    def finish(self):
-        p = self.place
-        for slot in range(3):
-
-            @pl.when(self.duty != slot)
-            def _():
-                self.back_copy(slot, p.x, p.core).wait_recv()
-                self.out_copy(slot).wait_send()
-
-            @pl.when(self.duty == slot)
-            def _():
-                for x, core in self.users(slot):
-
-                    @pl.when((p.x != x) | (p.core != core))
-                    def _():
-                        self.back_copy(slot, x, core).wait_send()
-
-
-def corner_spot(number, part):
-    row, column = number // 2, number % 2
-    return slice(row * part, (row + 1) * part), slice(column * part, (column + 1) * part)
-
-
-def base_kernel(
-    ratios,
-    sizes,
-    master,
-    momentum,
-    anchor,
-    loss_in,
-    grads,
-    *rest,
-):
-    place = Place()
-    rest = list(rest)
-
-    def take(count):
-        taken = rest[:count]
-        del rest[:count]
-        return taken
-
-    ortho_out, loss_out = take(2)
-    gram, gram_total = take(2)
-    gram_boxes = take(2)
-    (mate_gram,) = take(1)
-    grams, fresh, rows_in, rows_out, back, tiles, tile_boxes = take(7)
-    gram_sems, tile_sems, share_sems = take(3)
-
-    rows_in[...] = jnp.zeros_like(rows_in)
-    place.greet(True, True)
-    fresh[...] = momentum_decay * momentum[...] + (grads[...] + prox_weight * (master[...] - anchor[...]))
-    share = Share(place, sizes, (fresh, rows_in, rows_out, back), share_sems)
-    share.send()
-    tiles[0] = loss_in[...]
-    tile_sum = TileSum(place, tiles, tile_boxes, tile_sems)
-    extra = tile_sum.steps()
-    extra.pop(0)()
-
-    width = master.shape[1]
-    part = width // CUTS
-    corners = [(row, column) for row in range(CUTS) for column in range(row, CUTS)]
-    share.gather()
-    held = rows_in[...]
-    partial = lax.dot_general(
-        held, held, (((0,), (0,)), ((), ())), precision=precise, preferred_element_type=wide
-    )
-    for number, (row, column) in enumerate(corners):
-        gram[corner_spot(number, part)] = partial[
-            row * part : (row + 1) * part, column * part : (column + 1) * part
-        ]
-
-    @pl.when(place.x == 1)
-    def _():
-        swap = remote(gram, mate_gram, share_sems.at[0, 7], share_sems.at[1, 7], place.client, 1 - place.core)
-        swap.start()
-        swap.wait()
-        gram[...] += mate_gram[...]
-
-    gram_sum = GramSum(place, gram, gram_total, gram_boxes, gram_sems)
-    gram_sum.run(extra)
-    loss_out[...] = tile_sum.result()
-
-    spots = lax.broadcasted_iota(jnp.int32, (part, part), 0)
-    diagonal = spots == lax.broadcasted_iota(jnp.int32, (part, part), 1)
-    blocks = [gram_total[corner_spot(number, part)] for number in range(len(corners))]
-    trace = sum(
-        jnp.sum(jnp.where(diagonal, block, 0.0)) for block, (row, column) in zip(blocks, corners) if row == column
-    )
-    factor = 1.0 / (jnp.sqrt(trace) + 1e-07)
-    square = factor * factor
-    for block, (row, column) in zip(blocks, corners):
-        rows, columns = slice(row * part, (row + 1) * part), slice(column * part, (column + 1) * part)
-        grams[rows, columns] = block * square
-        if row < column:
-            grams[columns, rows] = block.T * square
-    rows_in[...] = rows_in[...] * factor
-
-    def turn(count, carry):
-        current = grams[...]
-        mixed = schulz_second * current + schulz_third * dot_high(current, current)
-        held = rows_in[...]
-        rows_in[...] = schulz_first * held + dot_high(held, mixed)
-
-        @pl.when(count < NS_STEPS - 1)
-        def _():
-            once = schulz_first * current + dot_high(current, mixed)
-            grams[...] = schulz_first * once + dot_high(once, mixed)
-
-        return carry
-
-    lax.fori_loop(0, NS_STEPS, turn, 0)
-    ratio = jnp.where(share.duty == 1, ratios[1], ratios[0])
-    rows_out[...] = (rows_in[...] * ratio).astype(low_type)
-    share.give_back()
-    share.finish()
-    ortho_out[...] = back[...].astype(wide)
-    gram_sum.drain()
-    tile_sum.drain()
-
-
-def base_pass(ratios, sizes, master, momentum, anchor, loss_tile, grads):
-    rows, width = master.shape
-    part = width // CUTS
-    gram_rows = CUTS * (CUTS + 1) // 4 * part
-    vmem = pl.BlockSpec(memory_space=pltpu.VMEM)
-    scratch = [pltpu.VMEM((gram_rows, 2 * part), wide)] * 2
-    scratch += [pltpu.VMEM((count, gram_rows // 8, 2 * part), wide) for count in (4, 3)]
-    scratch += [pltpu.VMEM((gram_rows, 2 * part), wide)]
-    scratch += [
-        pltpu.VMEM((width, width), wide),
-        pltpu.VMEM((rows, width), wide),
-        pltpu.VMEM((max(4 * sizes[0], 2 * sizes[1]), width), wide),
-        pltpu.VMEM((max(4 * sizes[0], 2 * sizes[1]), width), low_type),
-        pltpu.VMEM((rows, width), low_type),
-        pltpu.VMEM((4, 8, LANES), wide),
-        pltpu.VMEM((6, 8, LANES), wide),
-        pltpu.SemaphoreType.DMA((2, 14)),
-        pltpu.SemaphoreType.DMA((2, 6)),
-        pltpu.SemaphoreType.DMA((2, 8)),
-    ]
-    block = jax.ShapeDtypeStruct((rows, width), wide)
-    outs = [block, jax.ShapeDtypeStruct((8, LANES), wide)]
-    operands = [master, momentum, anchor, loss_tile, grads]
-    return pl.pallas_call(
-        functools.partial(base_kernel, ratios, sizes),
-        out_shape=outs,
-        in_specs=[vmem] * len(operands),
-        out_specs=[vmem] * len(outs),
-        scratch_shapes=scratch,
-        compiler_params=pltpu.CompilerParams(
-            collective_id=1, has_side_effects=True, vmem_limit_bytes=VMEM_BYTES
-        ),
-    )(*operands)
-
-
-def update_kernel(loss_tile, master, momentum, anchor, grads, ortho, *rest):
-    norms, grad_norm, heads, grad_head, outs = rest[0:3], rest[3], rest[4:7], rest[7], rest[8:]
-    loss_out, *outs = outs
-    loss_out[0] = loss_tile[0, 0]
-    loss_out[1] = loss_tile[0, 1]
-    momentum_out, base_out, low_out = outs[0:3]
-    held = master[...]
-    momentum_out[...] = momentum_decay * momentum[...] + (grads[...] + prox_weight * (held - anchor[...]))
-    fresh = held - muon_rate * (ortho[...] + muon_decay * held)
-    base_out[...] = fresh
-    low_out[...] = fresh.astype(low_type)
-    for targets, values, grad, rate, decay in (
-        (outs[3:6], norms, grad_norm, norm_rate, 0.0),
-        (outs[6:9], heads, grad_head, head_rate, head_decay),
-    ):
-        updates = adam_update(values[0][...], grad[...], values[1][...], values[2][...], rate, decay)
-        for target, value in zip(targets, updates):
-            target[...] = value
-
-
-def update_pass(loss_tile, master, momentum, anchor, grads, ortho, norms, grad_norm, heads, grad_head):
-    vmem = pl.BlockSpec(memory_space=pltpu.VMEM)
-    smem = pl.BlockSpec(memory_space=pltpu.SMEM)
-    operands = [loss_tile, master, momentum, anchor, grads, ortho, *norms, grad_norm, *heads, grad_head]
-    outs = [(2,), master.shape, master.shape, master.shape] + [grad_norm.shape] * 3 + [grad_head.shape] * 3
-    types = [wide, wide, wide, low_type] + [wide] * 6
-    return pl.pallas_call(
-        update_kernel,
-        out_shape=[jax.ShapeDtypeStruct(shape, kind) for shape, kind in zip(outs, types)],
-        in_specs=[smem] + [vmem] * (len(operands) - 1),
-        out_specs=[smem] + [vmem] * (len(outs) - 1),
-        compiler_params=pltpu.CompilerParams(vmem_limit_bytes=VMEM_BYTES),
-    )(*operands)
 
 
 def gram_of(section):
@@ -1623,7 +1655,7 @@
     momentum_new = momentum_decay * momentum + (grad_base + prox_weight * (master - anchor))
     current = schulz([momentum_new[bounds[slot] : bounds[slot + 1]] for slot in range(3)])
     ortho = jnp.concatenate([current[slot] * ratios[slot] for slot in range(3)], axis=0)
-    return grad_base, ortho, lax.psum(loss_tile, ("client", "chan"))
+    return momentum_new, ortho, lax.psum(loss_tile, ("client", "chan"))
 
 
 def as_stored(rows, shape):
@@ -1652,7 +1684,6 @@
     classes = head.shape[2]
     rows_first = channels // blocks
     rows_mid = 9 * width // blocks
-    sizes = (rows_first, rows_mid, rows_first)
     bounds = (0, rows_first, rows_first + rows_mid, base_master.shape[1])
     ratio = (channels / width) ** 0.5
     ratios = (ratio, 3.0, ratio)
@@ -1661,7 +1692,7 @@
     heads = [jnp.transpose(value, (2, 0, 1)).reshape(-1, LANES) for value in (head, head_first, head_second)]
     near = lax.axis_size("client") == SPOTS[0] * SPOTS[1] * SPOTS[2]
     if near:
-        weights = [master]
+        weights = [master, momentum, anchor]
     else:
         low_master = master.astype(low_type)
         weights = [
@@ -1671,15 +1702,14 @@
         split = SPOTS + (2, channels // 32, width)
         weights = [weights[0].reshape(split), weights[1], weights[2].reshape(split)]
     *grads, grad_norm, grad_head, loss_tile = client_pass(
-        near, classes, features[0], labels, mask, norms[0], heads[0], weights
+        near, ratios, classes, features[0], labels, mask, norms[0], heads[0], weights
     )
     if near:
-        (grad_base,) = grads
-        ortho, loss_tile = base_pass(ratios, sizes, master, momentum, anchor, loss_tile, grad_base)
+        fresh_momentum, ortho = grads
     else:
-        grad_base, ortho, loss_tile = base_far(ratios, bounds, master, momentum, anchor, loss_tile, grads)
+        fresh_momentum, ortho, loss_tile = base_far(ratios, bounds, master, momentum, anchor, loss_tile, grads)
     loss, momentum_new, base_new, base_low, *fresh = update_pass(
-        loss_tile, master, momentum, anchor, grad_base, ortho, norms, grad_norm, heads, grad_head
+        loss_tile, master, fresh_momentum, ortho, norms, grad_norm, heads, grad_head
     )
     fresh_norms = [as_stored(value, norm_params.shape) for value in fresh[:3]]
     fresh_heads = [jnp.transpose(as_stored(value, (classes, 1, half)), (1, 2, 0)) for value in fresh[3:]]

time: 217 us -> 215 us (level)
  Pallas kernels: 216 us -> 213 us
    pallas_call x2 -> x1, Pallas kernels: 212 us -> 210 us  [client_pass(): pl.pallas_call(functools.partial(client_kernel, gather, ratios, images, c...]
where the time goes in v6:
time: 215 us
  Pallas kernels  213 us (99%)
    pallas_call x1, Pallas kernels, client_pass(): pl.pallas_call(functools.partial(client_kernel, gather, ratios, images, c...  210 us

profile of v6, /device:TPU:0, one launch (start us, length us, event | category | flops | bytes accessed | tf_op | source)
XLA Modules:
  0.0 214.9 jit_solution(8999066992712665495)
XLA Ops:
  1.3 209.9 %shard_map.195 = (f32[272,512]{1,0:T(8,128)}, bf16[272,512]{1,0:T(8,128)(2,1)}, f32[24,128]{1,0:T(8,128)}, f32[800,128]{1,0:T(8,128)}, f32[8,128]{1,0:T(8,128)}) custom-call(bf16[3136,1024]{1,0:T(8,128)(2,1)} %bitcast.31, s32[1,64]{1,0:T(1,128)} %labels.1, s32[1]{0:T(128)S(6)} %copy.22.flag, f32[24,128]{1,0:T(8,128)} %bitcast.40, f32[800,128]{1,0:T(8,128)} %bitcast.34, ...), custom_call_target="tpu_custom_call" | custom-call | tf_op jit(solution)/shard_map/pallas_call | solution.py:1593
  211.2 3.5 %shard_map.196 = (f32[2]{0:T(128)}, f32[272,512]{1,0:T(8,128)}, f32[272,512]{1,0:T(8,128)}, bf16[272,512]{1,0:T(8,128)(2,1)}, f32[24,128]{1,0:T(8,128)}, /*index...) custom-call(f32[8,128]{1,0:T(8,128)} %get-tuple-element.25.loss_tile, ...), custom_call_target="tpu_custom_call" | custom-call | tf_op jit(solution)/shard_map/pallas_call | solution.py:750

commit v7 on v6

--- a/solution.py
+++ b/solution.py
@@ -244,15 +244,13 @@
             for copy in self.core_copies(turn, slot):
                 copy.wait_recv()
 
-    def drain(self):
-        for slot in range(3):
-            for step in range(3):
-                self.z_copy(step, slot).wait_send()
-            for turn in range(4):
-                for copy in self.core_copies(turn, slot):
-                    copy.wait_send()
-        for number in range(6):
-            for turn in range(4):
+    def drain(self, slot):
+        for step in range(3):
+            self.z_copy(step, slot).wait_send()
+        for turn in range(4):
+            for copy in self.core_copies(turn, slot):
+                copy.wait_send()
+            for number in (2 * slot, 2 * slot + 1):
                 self.near_copy(turn, number).wait_send()
                 for copy in self.far_copies(turn, number):
                     copy.wait_send()
@@ -641,13 +639,6 @@
         right = jnp.concatenate([right_high[...], right_low[...], right_high[...]], axis=0)
         return dot_nn(left, right)
 
-    def by_rows(rows, step, call):
-        def body(index, carry):
-            call(pl.ds(pl.multiple_of(index * step, step), step))
-            return carry
-
-        lax.fori_loop(0, rows // step, body, 0)
-
     share.gather()
     high, low = halves_of(rows_in[...])
     left = jnp.concatenate([high, high, low], axis=0)
@@ -682,36 +673,22 @@
         if row < column:
             grams[columns, rows] = block.T
     rows_in[...] = rows_in[...] * factor
-    step = width // 2
 
     def turn(number, carry):
         set_right(grams)
-
-        def mix(rows):
-            current = grams[rows, :]
-            mixed[rows, :] = schulz_second * current + schulz_third * times_right(current)
-
-        by_rows(width, step, mix)
+        mixed[...] = schulz_second * grams[...] + schulz_third * times_right(grams[...])
         set_right(mixed)
-
-        def move(rows):
-            held = rows_in[rows, :]
-            rows_in[rows, :] = schulz_first * held + times_right(held)
-
-        by_rows(count, count // 2, move)
 
         @pl.when(number < NS_STEPS - 1)
         def _():
-            def first(rows):
-                current = grams[rows, :]
-                once[rows, :] = schulz_first * current + times_right(current)
-
-            def second(rows):
-                current = once[rows, :]
-                grams[rows, :] = schulz_first * current + times_right(current)
-
-            by_rows(width, step, first)
-            by_rows(width, step, second)
+            both = times_right(jnp.concatenate([grams[...], rows_in[...]], axis=0))
+            once[...] = schulz_first * grams[...] + both[:width]
+            rows_in[...] = schulz_first * rows_in[...] + both[width:]
+            grams[...] = schulz_first * once[...] + times_right(once[...])
+
+        @pl.when(number == NS_STEPS - 1)
+        def _():
+            rows_in[...] = schulz_first * rows_in[...] + times_right(rows_in[...])
 
         return carry
 
@@ -1037,10 +1014,7 @@
     whole_width = pl.ds(0, width)
 
     def first_part(index, carry):
-        kernel = flat_rows(w_first[index])
-        for side in range(2):
-            columns = slice(side * width // 2, (side + 1) * width // 2)
-            act_one[:, columns] += dot_nn(x_all[:, lanes(index, group)], kernel[:, columns])
+        act_one[...] += dot_nn(x_all[:, lanes(index, group)], flat_rows(w_first[index]))
         advance_at(index, (0, 1, 2))
         return carry
 
@@ -1107,11 +1081,8 @@
             @pl.when(tap % 3 == over)
             def _():
                 left = row_windows(taps_one, down, low_start[over], reaches[over])
-                rows = pl.ds(pl.multiple_of(tap * width, width), width)
-                for side in range(2):
-                    columns = slice(side * piece, (side + 1) * piece)
-                    value = dot_nn(left, w_middle[rows, columns])
-                    add_windows(act_two, columns, value, high_start[over], reaches[over])
+                kernel = w_middle[pl.ds(pl.multiple_of(tap * width, width), width), :]
+                add_windows(act_two, slice(None), dot_nn(left, kernel), high_start[over], reaches[over])
 
         advance_at(index, (2, 5, 6, 8))
         return carry
@@ -1123,10 +1094,17 @@
     close_stats(1, whole_width, width)
     move_two = swap(1, width)
     move_two.start()
+    arrive(2, 0)
+    if gather:
+        spread.drain(0)
+
+    def turn_weights(which, carry):
+        w_first[which] = jnp.transpose(flat_rows(w_last[which])).reshape(w_first.shape[1:])
+        return carry
+
+    lax.fori_loop(0, groups, turn_weights, 0)
     move_two.wait()
     settle(1, width)
-
-    arrive(2, 0)
 
     def third_line(index, carry):
         value = normal(act_two, 1, index) * gain_two + bias_two
@@ -1134,7 +1112,7 @@
         hidden_two[tile(index), :] = hidden
         for which in range(groups):
             columns = slice(which * group, (which + 1) * group)
-            value = dot_nt(hidden, flat_rows(w_last[which]))
+            value = dot_nn(hidden, flat_rows(w_first[which]))
             act_three[tile(index), columns] = value
             start = jnp.where(index == 0, column_sum(value[0:8]) / 8.0, shift[0:1, columns])
             gap = value - start
@@ -1264,16 +1242,6 @@
             mid_wide[mid_line(which, index), :] = value.astype(low_type)
 
     pull(0)
-    for copy in head_moves:
-        copy.wait_recv()
-    head_grad = dot_nn(logit_grads[0], pool_all[0]) + dot_nn(logit_grads[1], pool_all[1])
-    for spot in range(half // LANES):
-        stage[pl.ds(spot, classes, stride=half // LANES), :] = head_grad[
-            0:classes, spot * LANES : (spot + 1) * LANES
-        ]
-    head_space = stage.at[pl.ds(0, grad_head_out.shape[0]), :]
-    head_leave = pltpu.make_async_copy(head_space, grad_head_out, sem_local.at[0])
-    head_leave.start()
 
     def drop_into(act, slot, gain, bias, columns):
         size = pl.ds(0, width)
@@ -1344,7 +1312,8 @@
             share.send(slot)
 
     if gather:
-        spread.drain()
+        spread.drain(1)
+        spread.drain(2)
 
     def put(ref, which, value):
         ref[which] = value.astype(low_type).reshape(ref.shape[1:])
@@ -1404,6 +1373,16 @@
         return carry
 
     lax.fori_loop(0, 3, middle_row, 0)
+    for copy in head_moves:
+        copy.wait_recv()
+    head_grad = dot_nn(logit_grads[0], pool_all[0]) + dot_nn(logit_grads[1], pool_all[1])
+    for spot in range(half // LANES):
+        stage[pl.ds(spot, classes, stride=half // LANES), :] = head_grad[
+            0:classes, spot * LANES : (spot + 1) * LANES
+        ]
+    head_space = stage.at[pl.ds(0, grad_head_out.shape[0]), :]
+    head_leave = pltpu.make_async_copy(head_space, grad_head_out, sem_local.at[0])
+    head_leave.start()
     if gather:
         tile_sum.pair(0)
         for load in base_loads:

time: 215 us -> 210 us (0.977)
  Pallas kernels: 213 us -> 209 us
    pallas_call x1, Pallas kernels: 210 us -> 205 us  [client_pass(): pl.pallas_call(functools.partial(client_kernel, gather, ratios, images, c...]
where the time goes in v7:
time: 210 us
  Pallas kernels  209 us (100%)
    pallas_call x1, Pallas kernels, client_pass(): pl.pallas_call(functools.partial(client_kernel, gather, ratios, images, c...  205 us

profile of v7, /device:TPU:0, one launch (start us, length us, event | category | flops | bytes accessed | tf_op | source)
XLA Modules:
  0.0 210.2 jit_solution(12857942517852288887)
XLA Ops:
  1.3 205.2 %shard_map.195 = (f32[272,512]{1,0:T(8,128)}, bf16[272,512]{1,0:T(8,128)(2,1)}, f32[24,128]{1,0:T(8,128)}, f32[800,128]{1,0:T(8,128)}, f32[8,128]{1,0:T(8,128)}) custom-call(bf16[3136,1024]{1,0:T(8,128)(2,1)} %bitcast.31, s32[1,64]{1,0:T(1,128)} %labels.1, s32[1]{0:T(128)S(6)} %copy.22.flag, f32[24,128]{1,0:T(8,128)} %bitcast.40, f32[800,128]{1,0:T(8,128)} %bitcast.34, ...), custom_call_target="tpu_custom_call" | custom-call | tf_op jit(solution)/shard_map/pallas_call | solution.py:1572
  206.5 3.5 %shard_map.196 = (f32[2]{0:T(128)}, f32[272,512]{1,0:T(8,128)}, f32[272,512]{1,0:T(8,128)}, bf16[272,512]{1,0:T(8,128)(2,1)}, f32[24,128]{1,0:T(8,128)}, /*index...) custom-call(f32[8,128]{1,0:T(8,128)} %get-tuple-element.25.loss_tile, ...), custom_call_target="tpu_custom_call" | custom-call | tf_op jit(solution)/shard_map/pallas_call | solution.py:727

commit v8 on v7

--- a/solution.py
+++ b/solution.py
@@ -425,15 +425,19 @@
         ref = self.total.at[self.rows(([p.z] + p.others)[turn], p.y), :]
         return self.copy(10 + turn, ref, ref, p.along_y())
 
-    def run(self):
-        p = self.place
+    def start(self):
         for turn in range(4):
             self.y_down(turn).start()
+
+    def pass_down(self):
         for turn in range(4):
             self.y_down(turn).wait_recv()
-            self.data[self.rows(self.down_order[turn], p.y), :] += self.y_box[turn]
+            self.data[self.rows(self.down_order[turn], self.place.y), :] += self.y_box[turn]
             if turn < 3:
                 self.z_down(2 - turn).start()
+
+    def turn_up(self):
+        p = self.place
         mine = self.rows(p.z, p.y)
         value = self.data[mine, :]
         for step in (2, 1, 0):
@@ -443,9 +447,13 @@
         for step in range(3):
             self.z_up(step).start()
         self.y_up(0).start()
+
+    def pass_up(self):
         for step in range(3):
             self.z_up(step).wait_recv()
             self.y_up(1 + step).start()
+
+    def close(self):
         for turn in range(4):
             self.y_up(turn).wait_recv()
 
@@ -572,17 +580,13 @@
         def _():
             self.rows_in[self.spot(slot, self.place.x, self.place.core), :] = self.fresh[self.section(slot), :]
 
-    def gather(self):
-        p = self.place
-        for slot in range(3):
-
-            @pl.when(self.duty == slot)
+    def gather(self, slot):
+        p = self.place
+        for x, core in self.users(slot):
+
+            @pl.when((p.x != x) | (p.core != core))
             def _():
-                for x, core in self.users(slot):
-
-                    @pl.when((p.x != x) | (p.core != core))
-                    def _():
-                        self.in_copy(slot, x, core).wait_recv()
+                self.in_copy(slot, x, core).wait_recv()
 
     def give_back(self):
         p = self.place
@@ -621,25 +625,14 @@
     return slice(row * part, (row + 1) * part), slice(column * part, (column + 1) * part)
 
 
-def orthogonal(place, ratios, share, share_sems, gram, gram_total, mate_gram, gram_sum, squares, rows_in, low_rows):
-    grams, mixed, once = squares
-    count, width = rows_in.shape
+def triangle(width):
     part = width // CUTS
-    corners = [(row, column) for row in range(CUTS) for column in range(row, CUTS)]
-    right_high, right_low = [low_rows.at[pl.ds(count + spot * width, width), :] for spot in range(2)]
-
-    def set_right(value_ref):
-        for start in range(0, width, part):
-            rows = slice(start, start + part)
-            right_high[rows, :], right_low[rows, :] = halves_of(value_ref[rows, :])
-
-    def times_right(value):
-        high, low = halves_of(value)
-        left = jnp.concatenate([high, high, low], axis=1)
-        right = jnp.concatenate([right_high[...], right_low[...], right_high[...]], axis=0)
-        return dot_nn(left, right)
-
-    share.gather()
+    return part, [(row, column) for row in range(CUTS) for column in range(row, CUTS)]
+
+
+def form_gram(place, slot, share, share_sems, gram, mate_gram, rows_in):
+    part, corners = triangle(rows_in.shape[1])
+    share.gather(slot)
     high, low = halves_of(rows_in[...])
     left = jnp.concatenate([high, high, low], axis=0)
     right = jnp.concatenate([high, low, high], axis=0)
@@ -650,14 +643,30 @@
                 :, (column - row) * part : (column - row + 1) * part
             ]
 
-    @pl.when(place.x == 1)
-    def _():
+    if slot == 1:
         swap = remote(gram, mate_gram, share_sems.at[0, 7], share_sems.at[1, 7], place.client, 1 - place.core)
         swap.start()
         swap.wait()
         gram[...] += mate_gram[...]
 
-    gram_sum.run()
+
+def orthogonal(ratios, share, gram_total, squares, rows_in, low_rows):
+    grams, mixed, once = squares
+    count, width = rows_in.shape
+    part, corners = triangle(width)
+    right_high, right_low = [low_rows.at[pl.ds(count + spot * width, width), :] for spot in range(2)]
+
+    def set_right(value_ref):
+        for start in range(0, width, part):
+            rows = slice(start, start + part)
+            right_high[rows, :], right_low[rows, :] = halves_of(value_ref[rows, :])
+
+    def times_right(value):
+        high, low = halves_of(value)
+        left = jnp.concatenate([high, high, low], axis=1)
+        right = jnp.concatenate([right_high[...], right_low[...], right_high[...]], axis=0)
+        return dot_nn(left, right)
+
     spots = lax.broadcasted_iota(jnp.int32, (part, part), 0)
     diagonal = spots == lax.broadcasted_iota(jnp.int32, (part, part), 1)
     trace = 0.0
@@ -1447,31 +1456,50 @@
             grad_norm_out[kind * per_kind + spot : kind * per_kind + spot + 1, :] = whole[
                 :, spot * LANES : (spot + 1) * LANES
             ]
-    for step in (
-        (core_step, 0, 2),
-        (core_step, 0, 3),
-        (far_step, 0, 0),
-        (near_step, 0, 1),
-        (near_step, 0, 2),
-        (far_step, 0, 1),
-        (near_step, 0, 3),
-        (far_step, 0, 2),
-        (far_step, 0, 3),
-    ):
-        fold_step(*step)
-        if step == (far_step, 0, 0):
-            settle_section(1)
+    if gather:
+        part = width // CUTS
+        gram = act_three.at[pl.ds(0, gram_total.shape[0]), pl.ds(half + width, 2 * part)]
+        corner_rows = pl.ds(gram_total.shape[0], width)
+        squares = [act_three.at[corner_rows, pl.ds(spot * width, width)] for spot in (0, 1, 3)]
+        gram_sum = GramSum(place, gram, gram_total, (y_box, z_box), gram_sems)
+
+        def form(slot):
+            form_gram(place, slot, share, share_sems, gram, mate_gram, rows_in)
+            gram_sum.start()
+
+    def for_duty(slot, *calls):
+        if gather:
+
+            @pl.when(share.duty == slot)
+            def _():
+                for call in calls:
+                    call()
+
+    for_duty(2, lambda: form(2))
+    fold_step(core_step, 0, 2)
+    fold_step(core_step, 0, 3)
+    fold_step(far_step, 0, 0)
+    settle_section(1)
+    fold_step(near_step, 0, 1)
+    for_duty(2, lambda: gram_sum.pass_down())
+    fold_step(near_step, 0, 2)
+    fold_step(far_step, 0, 1)
+    fold_step(near_step, 0, 3)
+    for_duty(2, lambda: gram_sum.turn_up())
+    for_duty(1, lambda: form(1))
+    fold_step(far_step, 0, 2)
+    fold_step(far_step, 0, 3)
+    for_duty(2, lambda: gram_sum.pass_up())
+    for_duty(1, lambda: gram_sum.pass_down())
     if gather:
         settle_section(0)
         leave = pltpu.make_async_copy(fresh, fresh_out, sem_local.at[1])
         leave.start()
         tile_sum.pair(2)
-        part = width // CUTS
-        gram = act_three.at[pl.ds(0, gram_total.shape[0]), pl.ds(half + width, 2 * part)]
-        corner_rows = pl.ds(gram_total.shape[0], width)
-        squares = [act_three.at[corner_rows, pl.ds(spot * width, width)] for spot in (0, 1, 3)]
-        gram_sum = GramSum(place, gram, gram_total, (y_box, z_box), gram_sems)
-        orthogonal(place, ratios, share, share_sems, gram, gram_total, mate_gram, gram_sum, squares, rows_in, hidden_two)
+        for_duty(0, lambda: form(0), gram_sum.pass_down, gram_sum.turn_up, gram_sum.pass_up, gram_sum.close)
+        for_duty(1, gram_sum.turn_up, gram_sum.pass_up, gram_sum.close)
+        for_duty(2, gram_sum.close)
+        orthogonal(ratios, share, gram_total, squares, rows_in, hidden_two)
         share.finish()
         loss_out[...] = tile_sum.result()
         ortho_leave = pltpu.make_async_copy(back, ortho_out, sem_local.at[2])

time: 210 us -> 215 us (1.024)
  Pallas kernels: 209 us -> 213 us
    pallas_call x1, Pallas kernels: 205 us -> 209 us  [client_pass(): pl.pallas_call(functools.partial(client_kernel, gather, ratios, images, c...]
where the time goes in v8:
time: 215 us; the launch traced here: 214 us
  Pallas kernels  213 us (99%)
    pallas_call x1, Pallas kernels, client_pass(): pl.pallas_call(functools.partial(client_kernel, gather, ratios, images, c...  209 us

profile of v8, /device:TPU:0, one launch (start us, length us, event | category | flops | bytes accessed | tf_op | source)
XLA Modules:
  0.0 214.4 jit_solution(6114357618203243613)
XLA Ops:
  1.3 209.4 %shard_map.195 = (f32[272,512]{1,0:T(8,128)}, bf16[272,512]{1,0:T(8,128)(2,1)}, f32[24,128]{1,0:T(8,128)}, f32[800,128]{1,0:T(8,128)}, f32[8,128]{1,0:T(8,128)}) custom-call(bf16[3136,1024]{1,0:T(8,128)(2,1)} %bitcast.31, s32[1,64]{1,0:T(1,128)} %labels.1, s32[1]{0:T(128)S(6)} %copy.22.flag, f32[24,128]{1,0:T(8,128)} %bitcast.40, f32[800,128]{1,0:T(8,128)} %bitcast.34, ...), custom_call_target="tpu_custom_call" | custom-call | tf_op jit(solution)/shard_map/pallas_call | solution.py:1600
  210.7 3.5 %shard_map.196 = (f32[2]{0:T(128)}, f32[272,512]{1,0:T(8,128)}, f32[272,512]{1,0:T(8,128)}, bf16[272,512]{1,0:T(8,128)(2,1)}, f32[24,128]{1,0:T(8,128)}, /*index...) custom-call(f32[8,128]{1,0:T(8,128)} %get-tuple-element.25.loss_tile, ...), custom_call_target="tpu_custom_call" | custom-call | tf_op jit(solution)/shard_map/pallas_call | solution.py:736

commit v9 on v7

--- a/solution.py
+++ b/solution.py
@@ -639,6 +639,21 @@
         right = jnp.concatenate([right_high[...], right_low[...], right_high[...]], axis=0)
         return dot_nn(left, right)
 
+    middle = width // 2
+
+    def times_right_even(value, more=()):
+        high, low = halves_of(value)
+        left = jnp.concatenate([high, high, low], axis=1)
+        right = jnp.concatenate([right_high[...], right_low[...], right_high[...]], axis=0)
+        upper = left[:middle]
+        for rows in more:
+            high, low = halves_of(rows)
+            upper = jnp.concatenate([upper, jnp.concatenate([high, high, low], axis=1)], axis=0)
+        upper = dot_nn(upper, right)
+        corner = dot_nn(left[middle:], right[:, middle:])
+        lower = jnp.concatenate([upper[:middle, middle:].T, corner], axis=1)
+        return jnp.concatenate([upper[:middle], lower], axis=0), upper[middle:]
+
     share.gather()
     high, low = halves_of(rows_in[...])
     left = jnp.concatenate([high, high, low], axis=0)
@@ -676,15 +691,15 @@
 
     def turn(number, carry):
         set_right(grams)
-        mixed[...] = schulz_second * grams[...] + schulz_third * times_right(grams[...])
+        mixed[...] = schulz_second * grams[...] + schulz_third * times_right_even(grams[...])[0]
         set_right(mixed)
 
         @pl.when(number < NS_STEPS - 1)
         def _():
-            both = times_right(jnp.concatenate([grams[...], rows_in[...]], axis=0))
-            once[...] = schulz_first * grams[...] + both[:width]
-            rows_in[...] = schulz_first * rows_in[...] + both[width:]
-            grams[...] = schulz_first * once[...] + times_right(once[...])
+            product, moved = times_right_even(grams[...], (rows_in[...],))
+            once[...] = schulz_first * grams[...] + product
+            rows_in[...] = schulz_first * rows_in[...] + moved
+            grams[...] = schulz_first * once[...] + times_right_even(once[...])[0]
 
         @pl.when(number == NS_STEPS - 1)
         def _():
@@ -1106,14 +1121,19 @@
     move_two.wait()
     settle(1, width)
 
-    def third_line(index, carry):
-        value = normal(act_two, 1, index) * gain_two + bias_two
+    tall = count_rows // 2
+
+    def third_tile(index, carry):
+        rows = pl.ds(pl.multiple_of(index * tall, 16), tall)
+        act = act_two[rows, :]
+        normed = (act - fwd_stats[1, 0:1, whole_width]) * fwd_stats[1, 1:2, whole_width]
+        value = normed * gain_two + bias_two
         hidden = (value * sigmoid(value)).astype(low_type)
-        hidden_two[tile(index), :] = hidden
+        hidden_two[rows, :] = hidden
         for which in range(groups):
             columns = slice(which * group, (which + 1) * group)
             value = dot_nn(hidden, flat_rows(w_first[which]))
-            act_three[tile(index), columns] = value
+            act_three[rows, columns] = value
             start = jnp.where(index == 0, column_sum(value[0:8]) / 8.0, shift[0:1, columns])
             gap = value - start
             kept_sums = jnp.where(index == 0, 0.0, shift[8:24, columns])
@@ -1122,7 +1142,7 @@
             shift[16:24, columns] = kept_sums[8:16] + fold_rows(gap * gap)
         return carry
 
-    lax.fori_loop(0, SIDE, third_line, 0)
+    lax.fori_loop(0, 2, third_tile, 0)
     close_stats(2, pl.ds(0, channels), channels)
     move_three = swap(2, channels)
     move_three.start()

time: 210 us -> 208 us (level)
  Pallas kernels: 209 us -> 206 us
    pallas_call x1, Pallas kernels: 205 us -> 202 us  [client_pass(): pl.pallas_call(functools.partial(client_kernel, gather, ratios, images, c...]
where the time goes in v9:
time: 208 us; the launch traced here: 207 us
  Pallas kernels  206 us (99%)
    pallas_call x1, Pallas kernels, client_pass(): pl.pallas_call(functools.partial(client_kernel, gather, ratios, images, c...  202 us

profile of v9, /device:TPU:0, one launch (start us, length us, event | category | flops | bytes accessed | tf_op | source)
XLA Modules:
  0.0 207.3 jit_solution(2318081150210212877)
XLA Ops:
  1.3 202.3 %shard_map.195 = (f32[272,512]{1,0:T(8,128)}, bf16[272,512]{1,0:T(8,128)(2,1)}, f32[24,128]{1,0:T(8,128)}, f32[800,128]{1,0:T(8,128)}, f32[8,128]{1,0:T(8,128)}) custom-call(bf16[3136,1024]{1,0:T(8,128)(2,1)} %bitcast.31, s32[1,64]{1,0:T(1,128)} %labels.1, s32[1]{0:T(128)S(6)} %copy.22.flag, f32[24,128]{1,0:T(8,128)} %bitcast.40, f32[800,128]{1,0:T(8,128)} %bitcast.34, ...), custom_call_target="tpu_custom_call" | custom-call | tf_op jit(solution)/shard_map/pallas_call | solution.py:1592
  203.6 3.5 %shard_map.196 = (f32[2]{0:T(128)}, f32[272,512]{1,0:T(8,128)}, f32[272,512]{1,0:T(8,128)}, bf16[272,512]{1,0:T(8,128)(2,1)}, f32[24,128]{1,0:T(8,128)}, /*index...) custom-call(f32[8,128]{1,0:T(8,128)} %get-tuple-element.25.loss_tile, ...), custom_call_target="tpu_custom_call" | custom-call | tf_op jit(solution)/shard_map/pallas_call | solution.py:742

commit v10 on v9

--- a/solution.py
+++ b/solution.py
@@ -866,6 +866,19 @@
         )
         for side, buffer in enumerate((hidden_two, mid_wide.at[top_rows, :]))
     ]
+    feature_copies = []
+    for side, buffer in enumerate((taps_one, taps_two)):
+        feature_copies.append(
+            remote(
+                features.at[mate_rows, pl.ds(side * quarter, quarter)],
+                buffer.at[top_rows, :],
+                sem_misc.at[0, 5 + side],
+                sem_misc.at[1, 5 + side],
+                *mate,
+            )
+        )
+    for copy in feature_copies + own_copies:
+        copy.start()
     per_kind = params.shape[0] // 2
     for kind in range(2):
         rows = [params[kind * per_kind + spot : kind * per_kind + spot + 1, :] for spot in range(per_kind)]
@@ -879,18 +892,9 @@
         remote(params_all.at[core], params_all.at[core], sem_misc.at[0, 0], sem_misc.at[1, 0], *mate),
         remote(head_all.at[core], head_all.at[core], sem_misc.at[0, 1], sem_misc.at[1, 1], *mate),
     ]
-    for side, buffer in enumerate((taps_one, taps_two)):
-        to_mate.append(
-            remote(
-                features.at[mate_rows, pl.ds(side * quarter, quarter)],
-                buffer.at[top_rows, :],
-                sem_misc.at[0, 5 + side],
-                sem_misc.at[1, 5 + side],
-                *mate,
-            )
-        )
-    for copy in to_mate + own_copies:
+    for copy in to_mate:
         copy.start()
+    to_mate += feature_copies
 
     def advance(count):
         for group in due[:count]:
@@ -1289,26 +1293,35 @@
     def mid_group(which):
         return mid_wide[pl.ds(pl.multiple_of(which * count_rows, count_rows), count_rows), :]
 
-    def back_two(index):
-        left = jnp.concatenate([mid_wide[mid_line(which, index), :] for which in range(groups)], axis=1)
+    def back_two(first, lines):
+        def rows_from(base):
+            return pl.ds(pl.multiple_of(base + first * line, line), lines * line)
+
+        left = jnp.concatenate([mid_wide[rows_from(which * count_rows), :] for which in range(groups)], axis=1)
         value = dot_nn(left, flat_rows(w_last[...]))
-        normed = normal(act_two, 1, index)
+        normed = (act_two[rows_from(0), :] - fwd_stats[1, 0:1, whole_width]) * fwd_stats[1, 1:2, whole_width]
         norm = normed * gain_two + bias_two
         sig = sigmoid(norm)
         grad = value * (sig + norm * sig * (1.0 - sig))
-        act_three[tile(index), space_two] = grad
+        act_three[rows_from(0), space_two] = grad
         size = pl.ds(0, width)
         shift[8:16, size] += fold_rows(grad)
         shift[16:24, size] += fold_rows(grad * normed)
 
-    def back_two_line(index, carry):
-        pull(index + 1)
-        back_two(index)
+    pairs = (SIDE - 1) // 2
+
+    def back_two_loop(index, carry):
+        pull(2 * index + 2)
+        pull(2 * index + 3)
+        back_two(2 * index, 2)
         return carry
 
     shift[8:24, :] = jnp.zeros((16, channels), wide)
-    lax.fori_loop(0, SIDE - 1, back_two_line, 0)
-    back_two(SIDE - 1)
+    pull(1)
+    lax.fori_loop(0, pairs - 1, back_two_loop, 0)
+    pull(SIDE - 1)
+    back_two(SIDE - 3, 2)
+    back_two(SIDE - 1, 1)
     close_back(4)
     move_back_two = swap(4, width)
     move_back_two.start()

time: 208 us -> 205 us (0.986)
    pallas_call x1, Pallas kernels: 202 us -> 200 us  [client_pass(): pl.pallas_call(functools.partial(client_kernel, gather, ratios, images, c...]
where the time goes in v10:
time: 205 us
  Pallas kernels  204 us (100%)
    pallas_call x1, Pallas kernels, client_pass(): pl.pallas_call(functools.partial(client_kernel, gather, ratios, images, c...  200 us

profile of v10, /device:TPU:0, one launch (start us, length us, event | category | flops | bytes accessed | tf_op | source)
XLA Modules:
  0.0 205.2 jit_solution(16383489452367731348)
XLA Ops:
  1.3 200.2 %shard_map.195 = (f32[272,512]{1,0:T(8,128)}, bf16[272,512]{1,0:T(8,128)(2,1)}, f32[24,128]{1,0:T(8,128)}, f32[800,128]{1,0:T(8,128)}, f32[8,128]{1,0:T(8,128)}) custom-call(bf16[3136,1024]{1,0:T(8,128)(2,1)} %bitcast.31, s32[1,64]{1,0:T(1,128)} %labels.1, s32[1]{0:T(128)S(6)} %copy.22.flag, f32[24,128]{1,0:T(8,128)} %bitcast.40, f32[800,128]{1,0:T(8,128)} %bitcast.34, ...), custom_call_target="tpu_custom_call" | custom-call | tf_op jit(solution)/shard_map/pallas_call | solution.py:1605
  201.5 3.5 %shard_map.196 = (f32[2]{0:T(128)}, f32[272,512]{1,0:T(8,128)}, f32[272,512]{1,0:T(8,128)}, bf16[272,512]{1,0:T(8,128)(2,1)}, f32[24,128]{1,0:T(8,128)}, /*index...) custom-call(f32[8,128]{1,0:T(8,128)} %get-tuple-element.25.loss_tile, ...), custom_call_target="tpu_custom_call" | custom-call | tf_op jit(solution)/shard_map/pallas_call | solution.py:742

commit v11 on v10

--- a/solution.py
+++ b/solution.py
@@ -884,8 +884,9 @@
         rows = [params[kind * per_kind + spot : kind * per_kind + spot + 1, :] for spot in range(per_kind)]
         params_all[core, kind : kind + 1, :] = jnp.concatenate(rows, axis=1)
     head_all[core] = jnp.zeros(head_all.shape[1:], low_type)
+    stage[0 : head.shape[0], :] = head[...]
     for spot in range(half // LANES):
-        head_all[core, 0:classes, spot * LANES : (spot + 1) * LANES] = head[
+        head_all[core, 0:classes, spot * LANES : (spot + 1) * LANES] = stage[
             pl.ds(spot, classes, stride=half // LANES), :
         ].astype(low_type)
     to_mate = [
@@ -948,7 +949,7 @@
 
     def turn_from(source, base):
         def turn(index, carry):
-            stage[...] = source(lanes(index, LANES)).astype(wide)
+            stage[0:count_rows, :] = source(lanes(index, LANES)).astype(wide)
 
             def pixel(spot, inner):
                 x_all[
@@ -1554,7 +1555,7 @@
         pltpu.VMEM((count_rows + 2 * line, width), low_type),
         pltpu.VMEM((count_rows + 2 * line, width), low_type),
         pltpu.VMEM((count_rows, width), low_type),
-        pltpu.VMEM((count_rows, LANES), wide),
+        pltpu.VMEM((count_rows + 64, LANES), wide),
         pltpu.VMEM((2, 2, half + width), wide),
         pltpu.VMEM((2, head_rows, half), low_type),
         pltpu.VMEM((mine_images, channels), wide),

time: 205 us -> 205 us (level)
  no operation moved by 1% of the time
where the time goes in v11:
time: 205 us
  Pallas kernels  204 us (100%)
    pallas_call x1, Pallas kernels, client_pass(): pl.pallas_call(functools.partial(client_kernel, gather, ratios, images, c...  200 us

profile of v11, /device:TPU:0, one launch (start us, length us, event | category | flops | bytes accessed | tf_op | source)
XLA Modules:
  0.0 205.2 jit_solution(15995912271463692686)
XLA Ops:
  1.3 200.2 %shard_map.195 = (f32[272,512]{1,0:T(8,128)}, bf16[272,512]{1,0:T(8,128)(2,1)}, f32[24,128]{1,0:T(8,128)}, f32[800,128]{1,0:T(8,128)}, f32[8,128]{1,0:T(8,128)}) custom-call(bf16[3136,1024]{1,0:T(8,128)(2,1)} %bitcast.31, s32[1,64]{1,0:T(1,128)} %labels.1, s32[1]{0:T(128)S(6)} %copy.22.flag, f32[24,128]{1,0:T(8,128)} %bitcast.40, f32[800,128]{1,0:T(8,128)} %bitcast.34, ...), custom_call_target="tpu_custom_call" | custom-call | tf_op jit(solution)/shard_map/pallas_call | solution.py:1606
  201.5 3.5 %shard_map.196 = (f32[2]{0:T(128)}, f32[272,512]{1,0:T(8,128)}, f32[272,512]{1,0:T(8,128)}, bf16[272,512]{1,0:T(8,128)(2,1)}, f32[24,128]{1,0:T(8,128)}, /*index...) custom-call(f32[8,128]{1,0:T(8,128)} %get-tuple-element.25.loss_tile, ...), custom_call_target="tpu_custom_call" | custom-call | tf_op jit(solution)/shard_map/pallas_call | solution.py:742
